TPU v7x, 32 devices: a whole 2x2x4 slice. The times are simulated.
32 devices in a mesh: rx: 4 (over y, x), ry: 8 (over z, core).
Axes of the slice: x: 2, y: 2, z: 4, core: 2. Of those that a mesh axis runs over, the one named last changes fastest.
Arguments:
- block_input: bfloat16 [4, 8, 4, 197, 768], P('rx', 'ry'), may hold values from -6 to 6
- out_cotangent: bfloat16 [4, 8, 4, 197, 768], P('rx', 'ry'), may hold values from -6 to 6
- w_qkv: bfloat16 [4, 8, 768, 2304], P('rx', 'ry'), may hold values from -6 to 6
- w_proj: bfloat16 [4, 8, 768, 768], P('rx', 'ry'), may hold values from -6 to 6
Outputs:
- new_qkv: bfloat16 [4, 8, 768, 2304], P('rx', 'ry')
- new_proj: bfloat16 [4, 8, 768, 768], P('rx', 'ry')
All inputs are finite; a program needn't handle non-finite values.
Results may differ from a plain program's by a relative error of at most 0.0059.
Values may be sent and summed in bfloat16 or wider, within the bound.
No kernel may reach another device: no remote copies, remote signals or barrier semaphores. Data moves between devices by JAX's collectives and lax.ppermute only.
A program may use at most 192 MiB of HBM per device.

v0:
```python
import jax
import jax.numpy as jnp
from jax import lax
from jax.sharding import PartitionSpec as P

HEADS = 12
LR = 1


def from_behind(block, axis, distance):
    devices = range(lax.axis_size(axis))
    route = [((i - distance) % len(devices), i) for i in devices]
    return lax.ppermute(block, axis, route)


def neighbour_total(stacked):
    wide = jnp.float32
    total = from_behind(stacked, "rx", 1).astype(wide)
    total = total + from_behind(stacked, "rx", -1).astype(wide)
    total = total + from_behind(stacked, "ry", 1).astype(wide)
    total = total + from_behind(stacked, "ry", -1).astype(wide)
    return total + stacked.astype(wide)


def local_grads(tokens, cotangent, w_qkv, w_proj):
    f32 = jnp.float32
    bf16 = jnp.bfloat16
    width = w_proj.shape[0]
    images, length = (tokens.shape[0], tokens.shape[1])
    head_size = width // HEADS
    scale = width ** (-0.5)
    hscale = head_size ** (-0.5)
    xf = tokens.astype(f32)
    mean = jnp.mean(xf, axis=-1, keepdims=True)
    var = jnp.mean((xf - mean) ** 2, axis=-1, keepdims=True)
    normed = ((xf - mean) * lax.rsqrt(var + 1e-06)).astype(bf16)
    qkv = (jnp.einsum("btd,de->bte", normed, w_qkv, preferred_element_type=f32) * scale).astype(
        bf16
    )
    query = qkv[:, :, :width].reshape(images, length, HEADS, head_size)
    keys = qkv[:, :, width : 2 * width].reshape(images, length, HEADS, head_size)
    values = qkv[:, :, 2 * width :].reshape(images, length, HEADS, head_size)
    scores = jnp.einsum("bqhe,bkhe->bhqk", query, keys, preferred_element_type=f32) * hscale
    probs = jax.nn.softmax(scores, axis=-1)
    probs_b = probs.astype(bf16)
    attended = jnp.einsum("bhqk,bkhe->bqhe", probs_b, values, preferred_element_type=f32).astype(
        bf16
    )
    attended = attended.reshape(images, length, width)
    grad_proj = jnp.einsum("btd,bte->de", attended, cotangent, preferred_element_type=f32) * scale
    d_att = (
        jnp.einsum("bte,de->btd", cotangent, w_proj, preferred_element_type=f32) * scale
    ).astype(bf16)
    d_att = d_att.reshape(images, length, HEADS, head_size)
    d_probs = jnp.einsum("bqhe,bkhe->bhqk", d_att, values, preferred_element_type=f32)
    d_scores = (
        probs * (d_probs - jnp.sum(d_probs * probs, axis=-1, keepdims=True)) * hscale
    ).astype(bf16)
    d_query = jnp.einsum("bhqk,bkhe->bqhe", d_scores, keys, preferred_element_type=f32)
    d_keys = jnp.einsum("bhqk,bqhe->bkhe", d_scores, query, preferred_element_type=f32)
    d_values = jnp.einsum("bhqk,bqhe->bkhe", probs_b, d_att, preferred_element_type=f32)
    d_qkv = jnp.concatenate(
        [
            d_query.reshape(images, length, width),
            d_keys.reshape(images, length, width),
            d_values.reshape(images, length, width),
        ],
        axis=-1,
    ).astype(bf16)
    grad_qkv = jnp.einsum("btd,bte->de", normed, d_qkv, preferred_element_type=f32) * scale
    return (grad_qkv, grad_proj)


def local(block_input, out_cotangent, w_qkv, w_proj):
    width = w_proj.shape[2]
    stacked = jnp.concatenate([w_qkv, w_proj], axis=3)
    summed = None
    grad_qkv, grad_proj = local_grads(
        block_input[0, 0], out_cotangent[0, 0], w_qkv[0, 0], w_proj[0, 0]
    )
    summed = neighbour_total(stacked)
    new_qkv = (summed[:, :, :, : 3 * width] / 5.0 - LR * grad_qkv[None, None]).astype(jnp.bfloat16)
    new_proj = (summed[:, :, :, 3 * width :] / 5.0 - LR * grad_proj[None, None]).astype(
        jnp.bfloat16
    )
    return (new_qkv, new_proj)


def solution(mesh):
    return jax.shard_map(
        local,
        mesh=mesh,
        in_specs=(
            P("rx", "ry", None, None, None),
            P("rx", "ry", None, None, None),
            P("rx", "ry", None, None),
            P("rx", "ry", None, None),
        ),
        out_specs=(P("rx", "ry", None, None), P("rx", "ry", None, None)),
        check_vma=False,
    )
```

profile of v0, /device:TPU:0, one launch (start us, length us, event | category | flops | bytes accessed | tf_op | source)
XLA Modules:
  0.0 233.8 jit_solution(17636659735912427352)
XLA Ops:
  0.6 4.2 %constant_dynamic-update-slice_fusion.1 = bf16[1,1,768,3072]{3,2,1,0:T(8,128)(2,1)} fusion(bf16[1,1,768,2304]{3,2,1,0:T(8,128)(2,1)} %param.6), kind=kLoop, calls=%fused_computation.59 | loop fusion | bytes 7077888
  4.8 1.1 constant_dynamic-update-slice_fusion
  6.0 4.5 %collective-permute-start.3 = (bf16[1,1,768,3072]{3,2,1,0:T(8,128)(2,1)}, bf16[1,1,768,3072]{3,2,1,0:T(8,128)(2,1)}, u32[]{:S(2)}, u32[]{:S(2)}) collective-permute-start(bf16[1,1,768,3072]{3,2,1,0:T(8,128)(2,1)} %constant_dynamic-update-slice_fusion), channel_id=1, source_target_pairs={{1,0},{2,1},{3,2},{4,3},{5,4},{6,5},{7,6},{0,7},{9,8},{10,9},{11,1... | collective-permute-start | bytes 14155784 | tf_op jit(solution)/shard_map/ppermute | solution.py:13
  10.5 2.4 %collective-permute-start.1 = (bf16[1,1,768,3072]{3,2,1,0:T(8,128)(2,1)}, bf16[1,1,768,3072]{3,2,1,0:T(8,128)(2,1)}, u32[]{:S(2)}, u32[]{:S(2)}) collective-permute-start(bf16[1,1,768,3072]{3,2,1,0:T(8,128)(2,1)} %constant_dynamic-update-slice_fusion), channel_id=1, source_target_pairs={{8,0},{16,8},{24,16},{0,24},{9,1},{17,9},{25,17},{1,25},{10,2},{18... | collective-permute-start | bytes 14155784 | tf_op jit(solution)/shard_map/ppermute | solution.py:13
  12.9 0.5 convert_reduce_fusion
  13.5 1.2 fusion.32
  14.7 0.7 fusion.52
  15.4 3.2 %multiply_convert_fusion.1 = bf16[4,197,2304]{2,1,0:T(8,128)(2,1)S(1)} fusion(bf16[1,1,768,2304]{3,2,1,0:T(8,128)(2,1)S(1)} %copy-done.2, bf16[4,197,768]{2,0,1:T(4,128)(2,1)S(1)} %fusion.52), kind=kOutput, calls=%fused_computation.9 | convolution fusion | flops 2792318976 | bytes 8380416 | tf_op jit(solution)/shard_map/btd,de->bte/dot_general | solution.py:37
  18.6 0.0 copy-start.7
  18.6 2.0 fusion.64
  20.6 2.2 multiply_convert_fusion.2
  22.8 1.6 copy.30
  24.5 3.0 %copy.28 = bf16[4,197,768]{1,2,0:T(8,128)(2,1)} copy(bf16[4,197,768]{2,1,0:T(8,128)(2,1)} %get-tuple-element.3) | data formatting | bytes 2420736 | tf_op jit(solution)/shard_map/slice | solution.py:40
  27.5 2.5 %copy.27 = bf16[4,197,768]{1,2,0:T(8,128)(2,1)} copy(bf16[4,197,768]{2,1,0:T(8,128)(2,1)} %get-tuple-element.4) | data formatting | bytes 2420736 | tf_op jit(solution)/shard_map/slice | solution.py:41
  30.0 9.3 %fusion.65 = (f32[4,12,197]{2,1,0:T(8,128)S(1)}, f32[4,12,197,197]{2,3,1,0:T(8,128)}) fusion(bf16[4,197,12,64]{1,3,2,0:T(8,128)(2,1)} %bitcast.70, bf16[4,197,12,64]{1,3,2,0:T(8,128)(2,1)} %bitcast.68), kind=kOutput, calls=%fused_computation.67 | convolution fusion | flops 244031184 | bytes 9909888 | tf_op jit(solution)/shard_map/sub | solution.py:44
  39.3 6.6 %fusion.38 = bf16[4,12,64,197]{3,2,1,0:T(8,128)(2,1)} fusion(bf16[4,197,12,64]{1,3,2,0:T(8,128)(2,1)S(1)} %bitcast.66, f32[4,12,197,197]{2,3,1,0:T(8,128)} %get-tuple-element.6, f32[4,12,197]{2,1,0:T(8,128)S(1)} %get-tuple-element.5), kind=kOutput, calls=%fused_computation.45 | convolution fusion | flops 242773344 | bytes 9909888 | tf_op jit(solution)/shard_map/bhqk,bqhe->bkhe/dot_general | solution.py:61
  45.9 2.5 %copy.37 = bf16[4,197,768]{2,1,0:T(8,128)(2,1)} copy(bf16[4,197,768]{1,2,0:T(8,128)(2,1)} %bitcast.74) | data formatting | bytes 2420736 | tf_op jit(solution)/shard_map/reshape | solution.py:66
  48.5 1.8 copy.31
  50.3 6.7 %fusion.66 = f32[4,12,197,197]{2,3,1,0:T(8,128)} fusion(bf16[4,197,12,64]{1,3,2,0:T(8,128)(2,1)} %bitcast.67, bf16[4,197,12,64]{1,3,2,0:T(8,128)(2,1)S(1)} %bitcast.64), kind=kOutput, calls=%fused_computation.68 | convolution fusion | flops 238442496 | bytes 9872064 | tf_op jit(solution)/shard_map/bqhe,bkhe->bhqk/dot_general | solution.py:55
  57.0 17.1 %fusion.47 = bf16[4,12,64,197]{3,2,1,0:T(8,128)(2,1)} fusion(bf16[4,197,12,64]{1,3,2,0:T(8,128)(2,1)} %bitcast.71, f32[4,12,197,197]{2,3,1,0:T(8,128)} %fusion.66, f32[4,12,197,197]{2,3,1,0:T(8,128)} %get-tuple-element.6, f32[4,12,197]{2,1,0:T(8,128)S(1)} %get-tuple-element.5), kind=kOutput, calls=%fused_computation.48 | convolution fusion | flops 252097152 | bytes 17361216 | tf_op jit(solution)/shard_map/bhqk,bqhe->bkhe/dot_general | solution.py:60
  74.0 2.5 %copy.36 = bf16[4,197,768]{2,1,0:T(8,128)(2,1)} copy(bf16[4,197,768]{1,2,0:T(8,128)(2,1)} %bitcast.73) | data formatting | bytes 2420736 | tf_op jit(solution)/shard_map/reshape | solution.py:65
  76.5 17.1 %fusion.44 = bf16[4,12,64,197]{3,2,1,0:T(8,128)(2,1)} fusion(bf16[4,197,12,64]{1,3,2,0:T(8,128)(2,1)} %bitcast.69, f32[4,12,197,197]{2,3,1,0:T(8,128)} %fusion.66, f32[4,12,197,197]{2,3,1,0:T(8,128)} %get-tuple-element.6, f32[4,12,197]{2,1,0:T(8,128)S(1)} %get-tuple-element.5), kind=kOutput, calls=%fused_computation.47 | convolution fusion | flops 252097152 | bytes 17361216 | tf_op jit(solution)/shard_map/bhqk,bkhe->bqhe/dot_general | solution.py:59
  93.6 2.5 %copy.35 = bf16[4,197,768]{2,1,0:T(8,128)(2,1)} copy(bf16[4,197,768]{1,2,0:T(8,128)(2,1)} %bitcast.72) | data formatting | bytes 2420736 | tf_op jit(solution)/shard_map/reshape | solution.py:64
  96.1 0.7 fusion.33
  96.8 4.9 %fusion.41 = bf16[4,12,64,197]{3,2,1,0:T(8,128)(2,1)S(1)} fusion(bf16[4,197,12,64]{1,3,2,0:T(8,128)(2,1)S(1)} %bitcast.65, f32[4,12,197,197]{2,3,1,0:T(8,128)} %get-tuple-element.6, f32[4,12,197]{2,1,0:T(8,128)S(1)} %get-tuple-element.5), kind=kOutput, calls=%fused_computation.46 | convolution fusion | flops 242773344 | bytes 9909888 | tf_op jit(solution)/shard_map/bhqk,bkhe->bqhe/dot_general | solution.py:46
  101.7 9.3 %collective-permute-done.3 = bf16[1,1,768,3072]{3,2,1,0:T(8,128)(2,1)} collective-permute-done((bf16[1,1,768,3072]{3,2,1,0:T(8,128)(2,1)}, bf16[1,1,768,3072]{3,2,1,0:T(8,128)(2,1)}, u32[]{:S(2)}, u32[]{:S(2)}) %collective-permute-start.3) | collective-permute-done | bytes 4718624 | tf_op jit(solution)/shard_map/ppermute | solution.py:13
  111.0 3.0 %collective-permute-done.2 = bf16[1,1,768,3072]{3,2,1,0:T(8,128)(2,1)} collective-permute-done((bf16[1,1,768,3072]{3,2,1,0:T(8,128)(2,1)}, bf16[1,1,768,3072]{3,2,1,0:T(8,128)(2,1)}, u32[]{:S(2)}, u32[]{:S(2)}) %collective-permute-start.2) | collective-permute-done | bytes 4718624 | tf_op jit(solution)/shard_map/ppermute | solution.py:13
  114.0 1.5 collective-permute-done.1
  115.5 99.7 %collective-permute-done = bf16[1,1,768,3072]{3,2,1,0:T(8,128)(2,1)} collective-permute-done((bf16[1,1,768,3072]{3,2,1,0:T(8,128)(2,1)}, bf16[1,1,768,3072]{3,2,1,0:T(8,128)(2,1)}, u32[]{:S(2)}, u32[]{:S(2)}) %collective-permute-start) | collective-permute-done | bytes 4718624 | tf_op jit(solution)/shard_map/ppermute | solution.py:13
  215.2 9.5 %convert_add_fusion = f32[1,1,768,3072]{3,2,1,0:T(8,128)S(1)} fusion(bf16[1,1,768,3072]{3,2,1,0:T(8,128)(2,1)} %constant_dynamic-update-slice_fusion, bf16[1,1,768,3072]{3,2,1,0:T(8,128)(2,1)} %collective-permute-done.3, bf16[1,1,768,3072]{3,2,1,0:T(8,128)(2,1)} %collective-permute-done.2, bf16[1,1,768,3072]{3,2,1,0:T(8,128)(2,1)} %collective-permute-done.1, ...), kind=kLoop, calls=%fused_computation.6 | loop fusion | flops 21233664 | bytes 33030144 | tf_op jit(solution)/shard_map/add | solution.py:22
  224.7 2.5 %fusion.37 = bf16[1,1,768,768]{3,2,1,0:T(8,128)(2,1)} fusion(f32[1,1,768,3072]{3,2,1,0:T(8,128)S(1)} %convert_add_fusion, bf16[4,197,768]{1,2,0:T(8,128)(2,1)S(1)} %bitcast.77, bf16[4,197,768]{2,0,1:T(4,128)(2,1)S(1)} %bitcast.76), kind=kOutput, calls=%fused_computation.43 | convolution fusion | flops 931921920 | bytes 5959680 | tf_op jit(solution)/shard_map/btd,bte->de/dot_general | solution.py:50
  227.2 6.6 %fusion.5 = bf16[1,1,768,2304]{3,2,1,0:T(8,128)(2,1)} fusion(f32[1,1,768,3072]{3,2,1,0:T(8,128)S(1)} %convert_add_fusion, bf16[4,197,768]{2,1,0:T(8,128)(2,1)S(1)} %copy-done.3, bf16[4,197,768]{2,1,0:T(8,128)(2,1)S(1)} %copy-done.4, bf16[4,197,768]{2,1,0:T(8,128)(2,1)S(1)} %copy-done.5, bf16[4,197,768]{2,0,1:T(4,128)(2,1)S(1)} %fusion.33), kind=kOutput, calls=%fused_computation.12 | convolution fusion | flops 2806659072 | bytes 15458304 | tf_op jit(solution)/shard_map/btd,bte->de/dot_general | solution.py:70
  (21 shorter events, 0.1 us)
Async XLA Ops:
  0.6 4.2 %copy-start.6 = (bf16[1,1,768,768]{3,2,1,0:T(8,128)(2,1)S(1)}, bf16[1,1,768,768]{3,2,1,0:T(8,128)(2,1)}, u32[]{:S(2)}) copy-start(bf16[1,1,768,768]{3,2,1,0:T(8,128)(2,1)} %param.7) | copy-start | bytes 3538948
  0.6 12.3 %copy-start = (bf16[1,1,4,197,768]{4,2,3,1,0:T(4,128)(2,1)S(1)}, bf16[1,1,4,197,768]{4,2,3,1,0:T(4,128)(2,1)}, u32[]{:S(2)}) copy-start(bf16[1,1,4,197,768]{4,2,3,1,0:T(4,128)(2,1)} %param.4) | copy-start | bytes 3631108
  6.0 9.4 %copy-start.2 = (bf16[1,1,768,2304]{3,2,1,0:T(8,128)(2,1)S(1)}, bf16[1,1,768,2304]{3,2,1,0:T(8,128)(2,1)}, u32[]{:S(2)}) copy-start(bf16[1,1,768,2304]{3,2,1,0:T(8,128)(2,1)} %param.6) | copy-start | bytes 10616836
  6.0 105.0 %collective-permute-start.3 = (bf16[1,1,768,3072]{3,2,1,0:T(8,128)(2,1)}, bf16[1,1,768,3072]{3,2,1,0:T(8,128)(2,1)}, u32[]{:S(2)}, u32[]{:S(2)}) collective-permute-start(bf16[1,1,768,3072]{3,2,1,0:T(8,128)(2,1)} %constant_dynamic-update-slice_fusion), channel_id=1, source_target_pairs={{1,0},{2,1},{3,2},{4,3},{5,4},{6,5},{7,6},{0,7},{9,8},{10,9},{11,1... | collective-permute-start | bytes 14155784 | tf_op jit(solution)/shard_map/ppermute | solution.py:13
  10.5 103.5 %collective-permute-start.2 = (bf16[1,1,768,3072]{3,2,1,0:T(8,128)(2,1)}, bf16[1,1,768,3072]{3,2,1,0:T(8,128)(2,1)}, u32[]{:S(2)}, u32[]{:S(2)}) collective-permute-start(bf16[1,1,768,3072]{3,2,1,0:T(8,128)(2,1)} %constant_dynamic-update-slice_fusion), channel_id=1, source_target_pairs={{7,0},{0,1},{1,2},{2,3},{3,4},{4,5},{5,6},{6,7},{15,8},{8,9},{9,10... | collective-permute-start | bytes 14155784 | tf_op jit(solution)/shard_map/ppermute | solution.py:13
  10.5 105.1 %collective-permute-start.1 = (bf16[1,1,768,3072]{3,2,1,0:T(8,128)(2,1)}, bf16[1,1,768,3072]{3,2,1,0:T(8,128)(2,1)}, u32[]{:S(2)}, u32[]{:S(2)}) collective-permute-start(bf16[1,1,768,3072]{3,2,1,0:T(8,128)(2,1)} %constant_dynamic-update-slice_fusion), channel_id=1, source_target_pairs={{8,0},{16,8},{24,16},{0,24},{9,1},{17,9},{25,17},{1,25},{10,2},{18... | collective-permute-start | bytes 14155784 | tf_op jit(solution)/shard_map/ppermute | solution.py:13
  12.9 202.3 %collective-permute-start = (bf16[1,1,768,3072]{3,2,1,0:T(8,128)(2,1)}, bf16[1,1,768,3072]{3,2,1,0:T(8,128)(2,1)}, u32[]{:S(2)}, u32[]{:S(2)}) collective-permute-start(bf16[1,1,768,3072]{3,2,1,0:T(8,128)(2,1)} %constant_dynamic-update-slice_fusion), channel_id=1, source_target_pairs={{24,0},{0,8},{8,16},{16,24},{25,1},{1,9},{9,17},{17,25},{26,2},{2,... | collective-permute-start | bytes 14155784 | tf_op jit(solution)/shard_map/ppermute | solution.py:13
  18.6 2.0 copy-start.7
  24.5 14.8 %copy-start.1 = (bf16[4,197,768]{1,2,0:T(8,128)(2,1)}, bf16[4,197,768]{1,2,0:T(8,128)(2,1)S(1)}, u32[]{:S(2)}) copy-start(bf16[4,197,768]{1,2,0:T(8,128)(2,1)S(1)} %copy.30) | copy-start | bytes 3631108
  101.7 123.0 %copy-start.8 = (bf16[1,1,4,197,768]{4,2,3,1,0:T(4,128)(2,1)S(1)}, bf16[1,1,4,197,768]{4,2,3,1,0:T(4,128)(2,1)}, u32[]{:S(2)}) copy-start(bf16[1,1,4,197,768]{4,2,3,1,0:T(4,128)(2,1)} %param.5) | copy-start | bytes 3631108
  224.7 2.5 %copy-start.3 = (bf16[4,197,768]{2,1,0:T(8,128)(2,1)S(1)}, bf16[4,197,768]{2,1,0:T(8,128)(2,1)}, u32[]{:S(2)}) copy-start(bf16[4,197,768]{2,1,0:T(8,128)(2,1)} %copy.37) | copy-start | bytes 3631108
  224.7 2.5 %copy-start.4 = (bf16[4,197,768]{2,1,0:T(8,128)(2,1)S(1)}, bf16[4,197,768]{2,1,0:T(8,128)(2,1)}, u32[]{:S(2)}) copy-start(bf16[4,197,768]{2,1,0:T(8,128)(2,1)} %copy.36) | copy-start | bytes 3631108
  224.7 2.5 %copy-start.5 = (bf16[4,197,768]{2,1,0:T(8,128)(2,1)S(1)}, bf16[4,197,768]{2,1,0:T(8,128)(2,1)}, u32[]{:S(2)}) copy-start(bf16[4,197,768]{2,1,0:T(8,128)(2,1)} %copy.35) | copy-start | bytes 3631108
where the time goes:
time: 234 us
  waiting for transfers between devices  114 us (49%)
  matrix products  76.1 us (33%)
  local copies, waits for them, and re-layouts  23.8 us (10%)
  other arithmetic  12.6 us (5%)
  starting transfers between devices  6.94 us (3%)
    ppermute x4, waiting for transfers between devices, from_behind(): return lax.ppermute(block, axis, route)  114 us
    dot_general x1, matrix products, local_grads(): jnp.einsum('bhqk,bkhe->bqhe', d_scores, keys, preferred_element_type=f32)  17.1 us
    dot_general x1, matrix products, local_grads(): jnp.einsum('bhqk,bqhe->bkhe', d_scores, query, preferred_element_type=f32)  17.1 us
    add x1, other arithmetic, neighbour_total(): return total + stacked.astype(wide)  9.46 us
    sub x1, matrix products, local_grads(): probs = jax.nn.softmax(scores, axis=-1)  9.3 us
    ppermute x4, starting transfers between devices, from_behind(): return lax.ppermute(block, axis, route)  6.94 us
    dot_general x1, matrix products, local_grads(): jnp.einsum('bqhe,bkhe->bhqk', d_att, values, preferred_element_type=f32)  6.68 us
    dot_general x1, matrix products, local_grads(): jnp.einsum('bhqk,bqhe->bkhe', probs_b, d_att, preferred_element_type=f32)  6.64 us
  transfers between devices with their start and end apart: 4, of which 4 were waited for; matrix products, arithmetic and copies ran while one was open for 38% of the time, Pallas kernels for 0%

commit v1 on v0

v1 whole, which is shorter than its diff:
```python
import functools

import jax
import jax.numpy as jnp
from jax import lax
from jax.experimental import pallas as pl
from jax.experimental.pallas import tpu as pltpu
from jax.sharding import PartitionSpec as P

HEADS = 12
LR = 1
F32 = jnp.float32
BF16 = jnp.bfloat16
VMEM_LIMIT = 56 * 2**20


def mm(a,b,ca,cb):
    return lax.dot_general(a,b,(((ca,),(cb,)),((),())),preferred_element_type=F32)

def grads_body(length, heads, tok, cot, wq, wp, gq, gp, normed, qkv, datt, att, dqkv):
    T, D = normed.shape
    hd = D // heads
    scale = D ** -0.5
    hscale = hd ** -0.5
    x = tok[0].astype(F32)
    mean = jnp.mean(x, axis=-1, keepdims=True)
    xc = x - mean
    var = jnp.mean(xc * xc, axis=-1, keepdims=True)
    normed[...] = (xc * lax.rsqrt(var + 1e-06)).astype(BF16)
    for c in range(3):
        cols = slice(c * D, (c + 1) * D)
        qkv[:, cols] = (mm(normed[...], wq[:, cols], 1, 0) * scale).astype(BF16)
    datt[...] = (mm(cot[0], wp[...], 1, 1) * scale).astype(BF16)
    keep = lax.broadcasted_iota(jnp.int32, (T, T), 1) < length
    pack = 128 // hd
    def group(g, _):
        at = [pl.ds(pl.multiple_of(c * D + g * 128, 128), 128) for c in range(3)]
        qg, kg, vg = (qkv[:, a] for a in at)
        dg = datt[:, at[0]]
        outs = [[], [], [], []]
        for j in range(pack):
            s_ = slice(j * hd, (j + 1) * hd)
            q, k, v, da = qg[:, s_], kg[:, s_], vg[:, s_], dg[:, s_]
            s = jnp.where(keep, mm(q, k, 1, 1) * hscale, -1e30)
            e = jnp.exp(s - jnp.max(s, axis=-1, keepdims=True))
            p = e * (1.0 / jnp.sum(e, axis=-1, keepdims=True))
            pb = p.astype(BF16)
            dp = mm(da, v, 1, 1)
            ds = (p * (dp - jnp.sum(dp * p, axis=-1, keepdims=True)) * hscale).astype(BF16)
            outs[0].append(mm(pb, v, 1, 0).astype(BF16))
            outs[1].append(mm(ds, k, 1, 0).astype(BF16))
            outs[2].append(mm(ds, q, 0, 0).astype(BF16))
            outs[3].append(mm(pb, da, 0, 0).astype(BF16))
        o = [jnp.concatenate(z, axis=1) for z in outs]
        att[:, at[0]] = o[0]
        for c in range(3):
            dqkv[:, at[c]] = o[1 + c]
        return 0
    lax.fori_loop(0, heads // pack, group, 0)
    first = pl.program_id(0) == 0
    @pl.when(first)
    def _():
        gq[...] = jnp.zeros_like(gq)
        gp[...] = jnp.zeros_like(gp)
    nt = normed[...].T
    for c in range(3):
        cols = slice(c * D, (c + 1) * D)
        gq[:, cols] += mm(nt, dqkv[:, cols], 1, 0) * scale
    gp[...] += mm(att[...].T, cot[0], 1, 0) * scale

def grads(tokens, cot, wq, wp, heads):
    images, length, D = tokens.shape
    T = -(-length // 16) * 16
    pad = ((0, 0), (0, T - length), (0, 0))
    tokens, cot = jnp.pad(tokens, pad), jnp.pad(cot, pad)
    row = pl.BlockSpec((1, T, D), lambda b: (b, 0, 0))
    full = lambda r, c: pl.BlockSpec((r, c), lambda b: (0, 0))
    return pl.pallas_call(
        functools.partial(grads_body, length, heads),
        grid=(images,),
        in_specs=[row, row, full(D, 3 * D), full(D, D)],
        out_specs=[full(D, 3 * D), full(D, D)],
        out_shape=[jax.ShapeDtypeStruct((D, 3 * D), F32), jax.ShapeDtypeStruct((D, D), F32)],
        scratch_shapes=[pltpu.VMEM((T, D), BF16), pltpu.VMEM((T, 3*D), BF16), pltpu.VMEM((T, D), BF16), pltpu.VMEM((T, D), BF16), pltpu.VMEM((T, 3*D), BF16)],
        compiler_params=pltpu.CompilerParams(vmem_limit_bytes=56 * 2**20, dimension_semantics=("arbitrary",)),
        cost_estimate=pl.CostEstimate(flops=int(9e9), bytes_accessed=int(2e7), transcendentals=int(2e6)),
        name="attention_grads",
    )(tokens, cot, wq, wp)


def permute(block, axis, partner):
    n = lax.axis_size(axis)
    return lax.ppermute(block, axis, [(i, partner(i, n)) for i in range(n)])


def up(i, n):
    return (i + 1) % n


def down(i, n):
    return (i - 1) % n


def near(i, n):
    return i ^ 1


def far(i, n):
    return (i + 1) % n if i % 2 else (i - 1) % n


def opposite(i, n):
    return i ^ 2


def pair_body(wq, bq, wp, bp, after, out):
    rows = wq.shape[0]
    out[:rows] = (wq[...].astype(F32) + bq[...].astype(F32)).astype(BF16)
    width = wp.shape[1]
    for c in range(wp.shape[0] // rows):
        part = slice(c * rows, (c + 1) * rows)
        out[rows:, c * width : (c + 1) * width] = (
            wp[part].astype(F32) + bp[part].astype(F32)
        ).astype(BF16)


def pair_sums(wq, bq, wp, bp, after):
    rows, cols = bq.shape
    last = wq.shape[0] // rows - 1
    return pl.pallas_call(
        pair_body,
        grid=(1,),
        in_specs=[
            pl.BlockSpec((rows, cols), lambda i: (last, 0)),
            pl.BlockSpec(bq.shape, lambda i: (0, 0)),
            pl.BlockSpec(wp.shape, lambda i: (0, 0)),
            pl.BlockSpec(bp.shape, lambda i: (0, 0)),
            pl.BlockSpec(memory_space=pl.ANY),
        ],
        out_specs=pl.BlockSpec((2 * rows, cols), lambda i: (0, 0)),
        out_shape=jax.ShapeDtypeStruct((2 * rows, cols), BF16),
        compiler_params=pltpu.CompilerParams(vmem_limit_bytes=VMEM_LIMIT),
        cost_estimate=pl.CostEstimate(flops=2 * rows * cols, bytes_accessed=12 * rows * cols, transcendentals=0),
        name="pair_sums",
    )(wq, bq, wp, bp, after)


def partial_body(top, gq, wq, nq, fq, aq, gp, wp, np_, acc_q, acc_p):
    i = pl.program_id(0)
    total = wq[...].astype(F32) + nq[...].astype(F32) + fq[...].astype(F32)
    total = total + jnp.where(i < top, aq[...].astype(F32), 0.0)
    acc_q[...] = total / 5.0 - LR * gq[...]
    acc_p[...] = (wp[...].astype(F32) + np_[...].astype(F32)) / 5.0 - LR * gp[...]


def partial_totals(gq, wq, nq, fq, aq, gp, wp, np_):
    block = 128
    steps = wq.shape[0] // block
    top = aq.shape[0] // block
    q = pl.BlockSpec((block, wq.shape[1]), lambda i: (i, 0))
    p = pl.BlockSpec((block, wp.shape[1]), lambda i: (i, 0))
    a = pl.BlockSpec((block, wq.shape[1]), lambda i: (jnp.minimum(i, top - 1), 0))
    return pl.pallas_call(
        functools.partial(partial_body, top),
        grid=(steps,),
        in_specs=[q, q, q, q, a, p, p, p],
        out_specs=[q, p],
        out_shape=[jax.ShapeDtypeStruct(wq.shape, F32), jax.ShapeDtypeStruct(wp.shape, F32)],
        compiler_params=pltpu.CompilerParams(vmem_limit_bytes=VMEM_LIMIT),
        cost_estimate=pl.CostEstimate(flops=10 * wq.size, bytes_accessed=20 * wq.size, transcendentals=0),
        name="partial_totals",
    )(gq, wq, nq, fq, aq, gp, wp, np_)


def final_body(top, acc_q, a2, sq, acc_p, fp, sp, out_q, out_p):
    i = pl.program_id(0)
    late = jnp.where(i < top, a2[...], sq[...]).astype(F32)
    out_q[...] = (acc_q[...] + late / 5.0).astype(BF16)
    out_p[...] = (acc_p[...] + (fp[...].astype(F32) + sp[...].astype(F32)) / 5.0).astype(BF16)


def final_totals(acc_q, a2, acc_p, fp, sums):
    block = 128
    steps = acc_q.shape[0] // block
    top = a2.shape[0] // block
    side = (acc_q.shape[0] - a2.shape[0]) // block
    wide, width = acc_q.shape[1], acc_p.shape[1]
    q = pl.BlockSpec((block, wide), lambda i: (i, 0))
    p = pl.BlockSpec((block, width), lambda i: (i, 0))
    return pl.pallas_call(
        functools.partial(final_body, top),
        grid=(steps,),
        in_specs=[
            q,
            pl.BlockSpec((block, wide), lambda i: (jnp.minimum(i, top - 1), 0)),
            pl.BlockSpec((block, wide), lambda i: (jnp.maximum(i - top, 0), 0)),
            p,
            p,
            pl.BlockSpec((block, width), lambda i: (side + i % side, i // side)),
        ],
        out_specs=[q, p],
        out_shape=[jax.ShapeDtypeStruct(acc_q.shape, BF16), jax.ShapeDtypeStruct(acc_p.shape, BF16)],
        compiler_params=pltpu.CompilerParams(vmem_limit_bytes=VMEM_LIMIT),
        cost_estimate=pl.CostEstimate(flops=4 * acc_q.size, bytes_accessed=10 * acc_q.size, transcendentals=0),
        name="final_totals",
    )(acc_q, a2, sums, acc_p, fp, sums)


def plain_average(weights, grad):
    total = weights.astype(F32)
    for axis in ("rx", "ry"):
        for partner in (up, down):
            total = total + permute(weights, axis, partner).astype(F32)
    return (total / 5.0 - LR * grad).astype(BF16)


def local(block_input, out_cotangent, w_qkv, w_proj):
    wq, wp = w_qkv[0, 0], w_proj[0, 0]
    tokens, cot = block_input[0, 0], out_cotangent[0, 0]
    if lax.axis_size("rx") != 4 or lax.axis_size("ry") % 2:
        gq, gp = grads(tokens, cot, wq, wp, HEADS)
        return plain_average(wq, gq)[None, None], plain_average(wp, gp)[None, None]
    half = wq.shape[0] * 2 // 3
    b1p = permute(wp, "rx", opposite)
    fq = permute(wq, "ry", far)
    a1 = permute(wq[:half], "rx", near)
    b1q = permute(wq[half:], "rx", opposite)
    nq = permute(wq, "ry", near)
    gq, gp = grads(tokens, cot, wq, wp, HEADS)
    a2 = permute(a1, "rx", opposite)
    sums = permute(pair_sums(wq, b1q, wp, b1p, gp), "rx", near)
    fp = permute(wp, "ry", far)
    np_ = permute(wp, "ry", near)
    acc_q, acc_p = partial_totals(gq, wq, nq, fq, a1, gp, wp, np_)
    new_q, new_p = final_totals(acc_q, a2, acc_p, fp, sums)
    return new_q[None, None], new_p[None, None]


def solution(mesh):
    return jax.shard_map(
        local,
        mesh=mesh,
        in_specs=(
            P("rx", "ry", None, None, None),
            P("rx", "ry", None, None, None),
            P("rx", "ry", None, None),
            P("rx", "ry", None, None),
        ),
        out_specs=(P("rx", "ry", None, None), P("rx", "ry", None, None)),
        check_vma=False,
    )
```

time: 234 us -> 137 us (0.59)
  matrix products: 76.1 us -> 0 us
  Pallas kernels: 0 us -> 75.9 us
  waiting for transfers between devices: 114 us -> 39.3 us
  local copies, waits for them, and re-layouts: 23.8 us -> 9.68 us
  other arithmetic: 12.6 us -> 0 us
  starting transfers between devices: 6.94 us -> 10.8 us
    pallas_call x0 -> x4, Pallas kernels: none -> 75.9 us  [the longest x1 50.9 us: grads(): pl.pallas_call(functools.partial(grads_body, length, heads), grid=(images...]
    ppermute x4 -> x9, waiting for transfers between devices: 114 us -> 39.3 us  [permute(): return lax.ppermute(block, axis, [(i, partner(i, n)) for i in range(n)])]
    dot_general x9 -> x0, matrix products: 66.8 us -> none  [the longest x1 17.1 us: local_grads(): jnp.einsum('bhqk,bkhe->bqhe', d_scores, keys, preferred_element_type=f32)]
    add x1 -> x0, other arithmetic: 9.46 us -> none  [neighbour_total(): return total + stacked.astype(wide)]
    sub x1 -> x0, matrix products: 9.3 us -> none  [local_grads(): probs = jax.nn.softmax(scores, axis=-1)]
    reshape x3 -> x0, local copies, waits for them, and re-layouts: 7.51 us -> none  [the longest x1 2.51 us: local_grads(): d_values.reshape(images, length, width)]
    slice x4 -> x2, local copies, waits for them, and re-layouts: 9.33 us -> 4.52 us  [the longest x1 3.43 us: local(): a1 = permute(wq[:half], 'rx', near)]
    ppermute x4 -> x9, starting transfers between devices: 6.94 us -> 10.8 us  [permute(): return lax.ppermute(block, axis, [(i, partner(i, n)) for i in range(n)])]
  transfers between devices with their start and end apart: 4 -> 9, of which waited for: 4 -> 4; matrix products, arithmetic and copies ran while one was open for 38% -> 3% of each run, Pallas kernels for 0% -> 49%
where the time goes in v1:
time: 137 us; the launch traced here: 136 us
  Pallas kernels  75.9 us (55%)
  waiting for transfers between devices  39.3 us (29%)
  starting transfers between devices  10.8 us (8%)
  local copies, waits for them, and re-layouts  9.68 us (7%)
    pallas_call x1, Pallas kernels, grads(): pl.pallas_call(functools.partial(grads_body, length, heads), grid=(images...  50.9 us
    ppermute x9, waiting for transfers between devices, permute(): return lax.ppermute(block, axis, [(i, partner(i, n)) for i in range(n)])  39.3 us
    pallas_call x1, Pallas kernels, partial_totals(): pl.pallas_call(functools.partial(partial_body, top), grid=(steps,), in_sp...  12.3 us
    ppermute x9, starting transfers between devices, permute(): return lax.ppermute(block, axis, [(i, partner(i, n)) for i in range(n)])  10.8 us
    pallas_call x1, Pallas kernels, final_totals(): pl.pallas_call(functools.partial(final_body, top), grid=(steps,), in_spec...  8.39 us
    pallas_call x1, Pallas kernels, pair_sums(): pl.pallas_call(pair_body, grid=(1,), in_specs=[pl.BlockSpec((rows, cols),...  4.3 us
    slice x1, local copies, waits for them, and re-layouts, local(): a1 = permute(wq[:half], 'rx', near)  3.43 us
    unnamed x16, local copies, waits for them, and re-layouts  2.85 us
  transfers between devices with their start and end apart: 9, of which 4 were waited for; matrix products, arithmetic and copies ran while one was open for 3% of the time, Pallas kernels for 49%

profile of v1, /device:TPU:0, one launch (start us, length us, event | category | flops | bytes accessed | tf_op | source)
XLA Modules:
  0.0 136.4 jit_solution(2117803051879107297)
XLA Ops:
  0.6 0.0 copy-start
  0.6 3.4 %slice_bitcast_fusion = bf16[512,2304]{1,0:T(8,128)(2,1)} fusion(bf16[1,1,768,2304]{3,2,1,0:T(8,128)(2,1)} %param.6), kind=kLoop, calls=%fused_computation | loop fusion | bytes 4718592 | tf_op jit(solution)/shard_map/slice | solution.py:226
  4.1 2.9 %collective-permute-start.2 = (bf16[512,2304]{1,0:T(8,128)(2,1)}, bf16[512,2304]{1,0:T(8,128)(2,1)S(1)}, u32[]{:S(2)}, u32[]{:S(2)}) collective-permute-start(bf16[512,2304]{1,0:T(8,128)(2,1)} %slice_bitcast_fusion), channel_id=1, source_target_pairs={{0,8},{8,0},{16,24},{24,16},{1,9},{9,1},{17,25},{25,17},{2,10},{10... | collective-permute-start | bytes 7077896 | tf_op jit(solution)/shard_map/ppermute | solution.py:93
  7.0 0.0 collective-permute-start
  7.0 3.7 %collective-permute-start.1 = (bf16[768,2304]{1,0:T(8,128)(2,1)S(1)}, bf16[768,2304]{1,0:T(8,128)(2,1)}, u32[]{:S(2)}, u32[]{:S(2)}) collective-permute-start(bf16[768,2304]{1,0:T(8,128)(2,1)S(1)} %bitcast.18), channel_id=1, source_target_pairs={{0,7},{1,2},{2,1},{3,4},{4,3},{5,6},{6,5},{7,0},{8,15},{9,10},{10,... | collective-permute-start | bytes 10616840 | tf_op jit(solution)/shard_map/ppermute | solution.py:93
  10.7 1.5 %collective-permute-start.6 = (bf16[768,768]{1,0:T(8,128)(2,1)}, bf16[768,768]{1,0:T(8,128)(2,1)S(1)}, u32[]{:S(2)}, u32[]{:S(2)}) collective-permute-start(bf16[768,768]{1,0:T(8,128)(2,1)} %bitcast.3.wp), channel_id=1, source_target_pairs={{0,16},{8,24},{16,0},{24,8},{1,17},{9,25},{17,1},{25,9},{2,18},{10... | collective-permute-start | bytes 3538952 | tf_op jit(solution)/shard_map/ppermute | solution.py:93
  12.3 1.1 slice_bitcast_fusion.1
  13.3 0.5 collective-permute-start.5
  13.9 0.1 copy.11
  14.0 0.1 copy.10
  14.1 1.2 pad.7.tok
  15.3 1.1 pad.8.cot
  16.4 50.9 %attention_grads.1 = (f32[768,2304]{1,0:T(8,128)}, f32[768,768]{1,0:T(8,128)}) custom-call(bf16[4,208,768]{2,1,0:T(8,128)(2,1)} %pad.7.tok, bf16[4,208,768]{2,1,0:T(8,128)(2,1)} %pad.8.cot, bf16[768,2304]{1,0:T(8,128)(2,1)} %bitcast.14, bf16[768,768]{1,0:T(8,128)(2,1)} %bitcast.3.wp), custom_call_target="tpu_custom_call" | custom-call | flops 8999999488 | bytes 20000000 | tf_op jit(solution)/shard_map/attention_grads/pallas_call | solution.py:78
  67.3 0.0 collective-permute-done.6.bp
  67.3 0.1 collective-permute-start.3
  67.4 0.0 collective-permute-done.5.bq
  67.4 0.0 copy-start.6
  67.5 0.9 copy-done.5
  68.4 0.4 copy-done.6
  68.7 4.3 %pair_sums.1 = bf16[512,2304]{1,0:T(8,128)(2,1)} custom-call(bf16[768,2304]{1,0:T(8,128)(2,1)} %bitcast.15, bf16[256,2304]{1,0:T(8,128)(2,1)} %copy-done.6, bf16[768,768]{1,0:T(8,128)(2,1)} %bitcast.3.wp, bf16[768,768]{1,0:T(8,128)(2,1)} %copy-done.5, f32[768,768]{1,0:T(8,128)} %get-tuple-element.9.gp.after), custom_call_target="tpu_custom_call" | custom-call | flops 1179648 | bytes 7077888 | tf_op jit(solution)/shard_map/pair_sums/pallas_call | solution.py:130
  73.0 0.5 collective-permute-start.7
  73.6 1.5 %collective-permute-start.4 = (bf16[512,2304]{1,0:T(8,128)(2,1)S(1)}, bf16[512,2304]{1,0:T(8,128)(2,1)}, u32[]{:S(2)}, u32[]{:S(2)}) collective-permute-start(bf16[512,2304]{1,0:T(8,128)(2,1)S(1)} %collective-permute-done.2.aq), channel_id=1, source_target_pairs={{0,16},{8,24},{16,0},{24,8},{1,17},{9,25},{17,1},{25,9},{2,18},{10... | collective-permute-start | bytes 7077896 | tf_op jit(solution)/shard_map/ppermute | solution.py:93
  75.1 0.0 collective-permute-done.3.np_
  75.1 0.0 collective-permute-start.8
  75.1 0.0 collective-permute-done.nq
  75.1 12.6 %collective-permute-done.1.fq = bf16[768,2304]{1,0:T(8,128)(2,1)} collective-permute-done((bf16[768,2304]{1,0:T(8,128)(2,1)S(1)}, bf16[768,2304]{1,0:T(8,128)(2,1)}, u32[]{:S(2)}, u32[]{:S(2)}) %collective-permute-start.1) | collective-permute-done | bytes 3538976 | tf_op jit(solution)/shard_map/ppermute | solution.py:93
  87.7 12.3 %partial_totals.1 = (f32[768,2304]{1,0:T(8,128)}, f32[768,768]{1,0:T(8,128)}) custom-call(f32[768,2304]{1,0:T(8,128)} %get-tuple-element.8.gq, bf16[768,2304]{1,0:T(8,128)(2,1)} %bitcast.16, bf16[768,2304]{1,0:T(8,128)(2,1)} %collective-permute-done.nq, bf16[768,2304]{1,0:T(8,128)(2,1)} %collective-permute-done.1.fq, bf16[512,2304]{1,0:T(8,128)(2,1)} %copy-done.2, ...), custom_call_target="tpu_custom_call" | custom-call | flops 17694720 | bytes 35389440 | tf_op jit(solution)/shard_map/partial_totals/pallas_call | solution.py:163
  100.0 12.5 %collective-permute-done.8.fp = bf16[768,768]{1,0:T(8,128)(2,1)} collective-permute-done((bf16[768,768]{1,0:T(8,128)(2,1)}, bf16[768,768]{1,0:T(8,128)(2,1)}, u32[]{:S(2)}, u32[]{:S(2)}) %collective-permute-start.8) | collective-permute-done | bytes 1179680 | tf_op jit(solution)/shard_map/ppermute | solution.py:93
  112.5 14.1 %collective-permute-done.7.sq.sp = bf16[512,2304]{1,0:T(8,128)(2,1)S(1)} collective-permute-done((bf16[512,2304]{1,0:T(8,128)(2,1)}, bf16[512,2304]{1,0:T(8,128)(2,1)S(1)}, u32[]{:S(2)}, u32[]{:S(2)}) %collective-permute-start.7) | collective-permute-done | bytes 2359328 | tf_op jit(solution)/shard_map/ppermute | solution.py:93
  126.6 0.1 collective-permute-done.4.a2
  126.8 1.3 copy-done.1
  128.0 8.4 %final_totals.1 = (bf16[768,2304]{1,0:T(8,128)(2,1)}, bf16[768,768]{1,0:T(8,128)(2,1)}) custom-call(f32[768,2304]{1,0:T(8,128)} %get-tuple-element.10.acc_q, bf16[512,2304]{1,0:T(8,128)(2,1)} %collective-permute-done.4.a2, bf16[512,2304]{1,0:T(8,128)(2,1)} %copy-done.1, f32[768,768]{1,0:T(8,128)} %get-tuple-element.11.acc_p, ...), custom_call_target="tpu_custom_call" | custom-call | flops 7077888 | bytes 17694720 | tf_op jit(solution)/shard_map/final_totals/pallas_call | solution.py:190
  (10 shorter events, 0.0 us)
Async XLA Ops:
  0.6 6.4 %copy-start = (bf16[1,1,768,2304]{3,2,1,0:T(8,128)(2,1)S(1)}, bf16[1,1,768,2304]{3,2,1,0:T(8,128)(2,1)}, u32[]{:S(2)}) copy-start(bf16[1,1,768,2304]{3,2,1,0:T(8,128)(2,1)} %param.6) | copy-start | bytes 10616836
  4.1 9.8 %copy-start.3 = (bf16[1,1,4,197,768]{4,2,3,1,0:T(4,128)(2,1)S(1)}, bf16[1,1,4,197,768]{4,2,3,1,0:T(4,128)(2,1)}, u32[]{:S(2)}) copy-start(bf16[1,1,4,197,768]{4,2,3,1,0:T(4,128)(2,1)} %param.4) | copy-start | bytes 3631108
  4.1 69.5 %collective-permute-start.2 = (bf16[512,2304]{1,0:T(8,128)(2,1)}, bf16[512,2304]{1,0:T(8,128)(2,1)S(1)}, u32[]{:S(2)}, u32[]{:S(2)}) collective-permute-start(bf16[512,2304]{1,0:T(8,128)(2,1)} %slice_bitcast_fusion), channel_id=1, source_target_pairs={{0,8},{8,0},{16,24},{24,16},{1,9},{9,1},{17,25},{25,17},{2,10},{10... | collective-permute-start | bytes 7077896 | tf_op jit(solution)/shard_map/ppermute | solution.py:93
  7.0 68.1 %collective-permute-start = (bf16[768,2304]{1,0:T(8,128)(2,1)S(1)}, bf16[768,2304]{1,0:T(8,128)(2,1)}, u32[]{:S(2)}, u32[]{:S(2)}) collective-permute-start(bf16[768,2304]{1,0:T(8,128)(2,1)S(1)} %bitcast.17), channel_id=1, source_target_pairs={{0,1},{1,0},{2,3},{3,2},{4,5},{5,4},{6,7},{7,6},{8,9},{9,8},{10,11... | collective-permute-start | bytes 10616840 | tf_op jit(solution)/shard_map/ppermute | solution.py:93
  7.0 80.7 %collective-permute-start.1 = (bf16[768,2304]{1,0:T(8,128)(2,1)S(1)}, bf16[768,2304]{1,0:T(8,128)(2,1)}, u32[]{:S(2)}, u32[]{:S(2)}) collective-permute-start(bf16[768,2304]{1,0:T(8,128)(2,1)S(1)} %bitcast.18), channel_id=1, source_target_pairs={{0,7},{1,2},{2,1},{3,4},{4,3},{5,6},{6,5},{7,0},{8,15},{9,10},{10,... | collective-permute-start | bytes 10616840 | tf_op jit(solution)/shard_map/ppermute | solution.py:93
  10.7 3.3 %copy-start.4 = (bf16[1,1,4,197,768]{4,2,3,1,0:T(4,128)(2,1)S(1)}, bf16[1,1,4,197,768]{4,2,3,1,0:T(4,128)(2,1)}, u32[]{:S(2)}) copy-start(bf16[1,1,4,197,768]{4,2,3,1,0:T(4,128)(2,1)} %param.5) | copy-start | bytes 3631108
  10.7 56.6 %collective-permute-start.6 = (bf16[768,768]{1,0:T(8,128)(2,1)}, bf16[768,768]{1,0:T(8,128)(2,1)S(1)}, u32[]{:S(2)}, u32[]{:S(2)}) collective-permute-start(bf16[768,768]{1,0:T(8,128)(2,1)} %bitcast.3.wp), channel_id=1, source_target_pairs={{0,16},{8,24},{16,0},{24,8},{1,17},{9,25},{17,1},{25,9},{2,18},{10... | collective-permute-start | bytes 3538952 | tf_op jit(solution)/shard_map/ppermute | solution.py:93
  13.3 54.1 %collective-permute-start.5 = (bf16[256,2304]{1,0:T(8,128)(2,1)}, bf16[256,2304]{1,0:T(8,128)(2,1)S(1)}, u32[]{:S(2)}, u32[]{:S(2)}) collective-permute-start(bf16[256,2304]{1,0:T(8,128)(2,1)} %slice_bitcast_fusion.1), channel_id=1, source_target_pairs={{0,16},{8,24},{16,0},{24,8},{1,17},{9,25},{17,1},{25,9},{2,18},{10... | collective-permute-start | bytes 3538952 | tf_op jit(solution)/shard_map/ppermute | solution.py:93
  67.3 1.0 copy-start.5
  67.3 7.8 %collective-permute-start.3 = (bf16[768,768]{1,0:T(8,128)(2,1)}, bf16[768,768]{1,0:T(8,128)(2,1)}, u32[]{:S(2)}, u32[]{:S(2)}) collective-permute-start(bf16[768,768]{1,0:T(8,128)(2,1)} %bitcast.3.wp), channel_id=1, source_target_pairs={{0,1},{1,0},{2,3},{3,2},{4,5},{5,4},{6,7},{7,6},{8,9},{9,8},{10,11... | collective-permute-start | bytes 3538952 | tf_op jit(solution)/shard_map/ppermute | solution.py:93
  67.4 1.3 copy-start.6
  73.0 53.6 %collective-permute-start.7 = (bf16[512,2304]{1,0:T(8,128)(2,1)}, bf16[512,2304]{1,0:T(8,128)(2,1)S(1)}, u32[]{:S(2)}, u32[]{:S(2)}) collective-permute-start(bf16[512,2304]{1,0:T(8,128)(2,1)} %pair_sums.1), channel_id=1, source_target_pairs={{0,8},{8,0},{16,24},{24,16},{1,9},{9,1},{17,25},{25,17},{2,10},{10... | collective-permute-start | bytes 7077896 | tf_op jit(solution)/shard_map/ppermute | solution.py:93
  73.6 14.1 %copy-start.2 = (bf16[512,2304]{1,0:T(8,128)(2,1)}, bf16[512,2304]{1,0:T(8,128)(2,1)S(1)}, u32[]{:S(2)}) copy-start(bf16[512,2304]{1,0:T(8,128)(2,1)S(1)} %collective-permute-done.2.aq) | copy-start | bytes 7077892
  73.6 53.2 %collective-permute-start.4 = (bf16[512,2304]{1,0:T(8,128)(2,1)S(1)}, bf16[512,2304]{1,0:T(8,128)(2,1)}, u32[]{:S(2)}, u32[]{:S(2)}) collective-permute-start(bf16[512,2304]{1,0:T(8,128)(2,1)S(1)} %collective-permute-done.2.aq), channel_id=1, source_target_pairs={{0,16},{8,24},{16,0},{24,8},{1,17},{9,25},{17,1},{25,9},{2,18},{10... | collective-permute-start | bytes 7077896 | tf_op jit(solution)/shard_map/ppermute | solution.py:93
  75.1 37.4 %collective-permute-start.8 = (bf16[768,768]{1,0:T(8,128)(2,1)}, bf16[768,768]{1,0:T(8,128)(2,1)}, u32[]{:S(2)}, u32[]{:S(2)}) collective-permute-start(bf16[768,768]{1,0:T(8,128)(2,1)} %bitcast.3.wp), channel_id=1, source_target_pairs={{0,7},{1,2},{2,1},{3,4},{4,3},{5,6},{6,5},{7,0},{8,15},{9,10},{10,... | collective-permute-start | bytes 3538952 | tf_op jit(solution)/shard_map/ppermute | solution.py:93
  126.6 1.4 %copy-start.1 = (bf16[512,2304]{1,0:T(8,128)(2,1)}, bf16[512,2304]{1,0:T(8,128)(2,1)S(1)}, u32[]{:S(2)}) copy-start(bf16[512,2304]{1,0:T(8,128)(2,1)S(1)} %collective-permute-done.7.sq.sp) | copy-start | bytes 7077892

commit v2 on v0

v2 whole, which is shorter than its diff:
```python
import functools

import jax
import jax.numpy as jnp
from jax import lax
from jax.experimental import pallas as pl
from jax.experimental.pallas import tpu as pltpu
from jax.sharding import PartitionSpec as P

HEADS = 12
LR = 1
F32 = jnp.float32
BF16 = jnp.bfloat16
MIB = 2**20


def mm(a, b, ca, cb):
    return lax.dot_general(a, b, (((ca,), (cb,)), ((), ())), preferred_element_type=F32)


def call(body, outs, operands, name, flops, moved, vmem, grid=None, in_specs=None, out_specs=None, scratch=(), exps=0):
    whole = pl.BlockSpec(memory_space=pltpu.VMEM)
    kwargs = {} if grid is None else {"grid": grid}
    return pl.pallas_call(
        body,
        in_specs=in_specs or [whole] * len(operands),
        out_specs=out_specs or [whole] * len(outs),
        out_shape=[jax.ShapeDtypeStruct(shape, dtype) for shape, dtype in outs],
        scratch_shapes=list(scratch),
        compiler_params=pltpu.CompilerParams(vmem_limit_bytes=vmem * MIB),
        cost_estimate=pl.CostEstimate(flops=flops, bytes_accessed=moved, transcendentals=exps),
        name=name,
        **kwargs,
    )(*operands)


def project_body(rows, tok, cot, wq, wp, turned, qkv, datt, normed):
    c = pl.program_id(0)
    total, width = normed.shape
    scale = width**-0.5

    @pl.when(c == 0)
    def _():
        for r in range(0, total, rows):
            part = slice(r, r + rows)
            x = tok[part].astype(F32)
            xc = x - jnp.mean(x, axis=-1, keepdims=True)
            var = jnp.mean(xc * xc, axis=-1, keepdims=True)
            normed[part] = (xc * lax.rsqrt(var + 1e-06)).astype(BF16)
            datt[part] = (mm(cot[part], wp[...], 1, 1) * scale).astype(BF16)
        turned[...] = normed[...].T

    for r in range(0, total, rows):
        part = slice(r, r + rows)
        qkv[part] = (mm(normed[part], wq[...], 1, 0) * scale).astype(BF16)


def project(tokens, cot, wq, wp, rows):
    total, width = tokens.shape
    fixed = pl.BlockSpec((total, width), lambda c: (0, 0))
    return call(
        functools.partial(project_body, rows),
        [((width, total), BF16), ((total, 3 * width), BF16), ((total, width), BF16)],
        (tokens, cot, wq, wp),
        "project",
        flops=8 * total * width * width,
        moved=16 * total * width + 8 * width * width,
        vmem=32,
        grid=(3,),
        in_specs=[
            fixed,
            fixed,
            pl.BlockSpec((width, width), lambda c: (0, c)),
            pl.BlockSpec((width, width), lambda c: (0, 0)),
        ],
        out_specs=[
            pl.BlockSpec((width, total), lambda c: (0, 0)),
            pl.BlockSpec((total, width), lambda c: (0, c)),
            fixed,
        ],
        scratch=[pltpu.VMEM((total, width), BF16)],
    )


def attention_body(length, heads, unroll, qkv, datt, att, dqkv):
    rows, width = datt.shape
    hd = width // heads
    hscale = hd**-0.5
    pack = 128 // hd
    full = rows // 16 * 16 - 16
    keep = lax.broadcasted_iota(jnp.int32, (rows - full, rows), 0) < length - full
    lane = lax.broadcasted_iota(jnp.int32, (rows, 128), 1)

    def group(g, carry):
        at = [pl.ds(pl.multiple_of(c * width + g * 128, 128), 128) for c in range(3)]
        qg, kg, vg = (qkv[:, a] for a in at)
        dg = datt[:, at[0]]
        kt, vt = kg.T, vg.T
        dk, dv, at_t, dq_t = 0.0, 0.0, [], []
        for j in range(pack):
            own = (lane >= j * hd) & (lane < (j + 1) * hd)
            q = jnp.where(own, qg, jnp.zeros_like(qg)) * jnp.asarray(hscale, BF16)
            da = jnp.where(own, dg, jnp.zeros_like(dg))
            s = mm(kg, q, 1, 1)
            s = jnp.concatenate([s[:full], jnp.where(keep, s[full:], -1e30)], axis=0)
            e = jnp.exp(s - jnp.max(s, axis=0, keepdims=True))
            p = e * (1.0 / jnp.sum(e, axis=0, keepdims=True))
            pb = p.astype(BF16)
            dp = mm(vg, da, 1, 1)
            ds = (p * (dp - jnp.sum(dp * p, axis=0, keepdims=True))).astype(BF16)
            mine = slice(j * hd, (j + 1) * hd)
            at_t.append(mm(vt[mine], pb, 1, 0))
            dq_t.append(mm(kt[mine], ds, 1, 0) * hscale)
            dk = dk + mm(ds, q, 1, 0)
            dv = dv + mm(pb, da, 1, 0)
        att[pl.ds(pl.multiple_of(g * 128, 128), 128), :] = jnp.concatenate(at_t, axis=0).astype(BF16)
        dqkv[:, at[0]] = jnp.concatenate(dq_t, axis=0).astype(BF16).T
        dqkv[:, at[1]] = dk.astype(BF16)
        dqkv[:, at[2]] = dv.astype(BF16)
        return carry

    lax.fori_loop(0, heads // pack, group, 0, unroll=unroll)


def attention(qkv, datt, first, count, rows, length, heads, unroll=6):
    width = datt.shape[1]
    here = lambda b: (b + first, 0)
    there = lambda b: (b, 0)
    return call(
        functools.partial(attention_body, length, heads, unroll),
        [((count * width, rows), BF16), ((count * rows, 3 * width), BF16)],
        (qkv, datt),
        "attention",
        flops=12 * count * rows * 256 * 256 * heads,
        moved=16 * count * rows * width,
        vmem=16,
        grid=(count,),
        in_specs=[pl.BlockSpec((rows, 3 * width), here), pl.BlockSpec((rows, width), here)],
        out_specs=[pl.BlockSpec((width, rows), there), pl.BlockSpec((rows, 3 * width), there)],
        exps=count * heads * rows * rows,
    )


def weight_grad(left, rights):
    at, total = 0, 0.0
    for right in rights:
        total = total + mm(left[:, at : at + right.shape[0]], right[...], 1, 0)
        at += right.shape[0]
    return total


def partial_body(top, parts, normed, wq, nq, a1, *refs):
    dqkv, acc = refs[:parts], refs[parts]
    i = pl.program_id(0)
    scale = (wq.shape[1] // 3) ** -0.5
    total = wq[...].astype(F32) + nq[...].astype(F32)
    total = total + jnp.where(i < top, a1[...].astype(F32), 0.0)
    acc[...] = total / 5.0 - LR * (weight_grad(normed, dqkv) * scale)


def partial_qkv(normed, dqkv, wq, nq, a1, block):
    width, total = normed.shape
    wide = wq.shape[1]
    top = a1.shape[0] // block
    row = pl.BlockSpec((block, wide), lambda i: (i, 0))
    return call(
        functools.partial(partial_body, top, len(dqkv)),
        [(wq.shape, F32)],
        (normed, wq, nq, a1, *dqkv),
        "partial_qkv",
        flops=2 * total * width * wide,
        moved=12 * width * wide,
        vmem=32,
        grid=(width // block,),
        in_specs=[
            pl.BlockSpec((block, total), lambda i: (i, 0)),
            row,
            row,
            pl.BlockSpec((block, wide), lambda i: (jnp.minimum(i, top - 1), 0)),
            *[pl.BlockSpec(d.shape, lambda i: (0, 0)) for d in dqkv],
        ],
        out_specs=[row],
    )[0]


def proj_body(parts, cot, wp, np_, fp, sp, *refs):
    att, out = refs[:parts], refs[parts]
    scale = wp.shape[0] ** -0.5
    total = wp[...].astype(F32) + np_[...].astype(F32) + fp[...].astype(F32) + sp[...].astype(F32)
    rows, width = att[0].shape[1], wp.shape[1]
    at, grad = 0, 0.0
    for a in att:
        for r in range(0, a.shape[0], width):
            grad = grad + mm(a[r : r + width], cot[at : at + rows], 1, 0)
            at += rows
    out[...] = (total / 5.0 - LR * (grad * scale)).astype(BF16)


def new_proj(cot, att, wp, np_, fp, sp):
    total, width = cot.shape
    return call(
        functools.partial(proj_body, len(att)),
        [(wp.shape, BF16)],
        (cot, wp, np_, fp, sp, *att),
        "new_proj",
        flops=2 * total * width * width,
        moved=12 * width * width,
        vmem=16,
    )[0]


def final_body(top, side, acc, fq, a2, s2, other, out):
    i = pl.program_id(0)
    half = (pl.num_programs(0) - top) // 2
    mine = (i - top) // half == side[0]
    rest = jnp.where(mine, s2[...], other[...])
    late = fq[...].astype(F32) + jnp.where(i < top, a2[...], rest).astype(F32)
    out[...] = (acc[...] + late / 5.0).astype(BF16)


def final_qkv(side, acc, fq, a2, s2, other, block):
    rows, wide = acc.shape
    top, half = a2.shape[0] // block, s2.shape[0] // block
    row = lambda at: pl.BlockSpec((block, wide), lambda i: (at(i), 0))
    low = row(lambda i: jnp.maximum(i - top, 0) % half)
    return call(
        functools.partial(final_body, top),
        [(acc.shape, BF16)],
        (side, acc, fq, a2, s2, other),
        "final_qkv",
        flops=4 * rows * wide,
        moved=10 * rows * wide,
        vmem=16,
        grid=(rows // block,),
        in_specs=[
            pl.BlockSpec(memory_space=pltpu.SMEM),
            row(lambda i: i),
            row(lambda i: i),
            row(lambda i: jnp.minimum(i, top - 1)),
            low,
            low,
        ],
        out_specs=[row(lambda i: i)],
    )[0]


def pair_body(a, b, out):
    out[...] = (a[...].astype(F32) + b[...].astype(F32)).astype(BF16)


def pair_sum(a, b):
    return call(
        pair_body, [(a.shape, BF16)], (a, b), "pair_sum", flops=a.size, moved=6 * a.size, vmem=8
    )[0]


def rows_body(count, source, out, done):
    copy = pltpu.make_async_copy(source.at[:count], out, done)
    copy.start()
    copy.wait()


def first_rows(a, count):
    return call(
        functools.partial(rows_body, count),
        [((count, a.shape[1]), a.dtype)],
        (a,),
        "first_rows",
        flops=0,
        moved=4 * count * a.shape[1],
        vmem=8,
        in_specs=[pl.BlockSpec(memory_space=pl.ANY)],
        scratch=[pltpu.SemaphoreType.DMA],
    )[0]


def permute(block, axis, partner):
    n = lax.axis_size(axis)
    return lax.ppermute(block, axis, [(i, partner(i, n)) for i in range(n)])


def up(i, n):
    return (i + 1) % n


def down(i, n):
    return (i - 1) % n


def near(i, n):
    return i ^ 1


def far(i, n):
    return (i + 1) % n if i % 2 else (i - 1) % n


def opposite(i, n):
    return i ^ 2


def after(values, *others):
    return lax.optimization_barrier((values, others))[0]


def plain_average(weights, grad):
    total = weights.astype(F32)
    for axis in ("rx", "ry"):
        for partner in (up, down):
            total = total + permute(weights, axis, partner).astype(F32)
    return (total / 5.0 - LR * grad).astype(BF16)


def local(block_input, out_cotangent, w_qkv, w_proj):
    wq, wp = w_qkv[0, 0], w_proj[0, 0]
    images, length, width = block_input.shape[2:]
    rows = -(-length // 16) * 16
    pad = ((0, 0), (0, rows - length), (0, 0))
    tokens = jnp.pad(block_input[0, 0], pad).reshape(images * rows, width)
    cot = jnp.pad(out_cotangent[0, 0], pad).reshape(images * rows, width)
    half = images // 2

    if lax.axis_size("rx") != 4 or lax.axis_size("ry") % 2:
        normed, qkv, datt = project(tokens, cot, wq, wp, rows)
        att, dqkv = attention(qkv, datt, 0, images, rows, length, HEADS)
        scale = width**-0.5
        gq = mm(normed, dqkv, 1, 0) * scale
        gp = jnp.einsum("bdt,bte->de", att.reshape(images, width, rows), cot.reshape(images, rows, width), preferred_element_type=F32) * scale
        return plain_average(wq, gq)[None, None], plain_average(wp, gp)[None, None]

    block = width // 8
    cut, part = 4 * block, 2 * block
    side = lax.axis_index("rx") // 2
    top = first_rows(wq, cut)
    sent = lax.dynamic_slice_in_dim(wq, cut + (1 - side) * part, part)
    kept = lax.dynamic_slice_in_dim(wq, cut + side * part, part)
    b1 = permute(wp, "rx", opposite)
    fp = permute(wp, "ry", far)
    a1 = permute(top, "rx", near)
    nq = permute(wq, "ry", near)
    np_ = permute(wp, "ry", near)
    normed, qkv, datt = project(tokens, cot, wq, wp, rows)

    wq2, sent, qkv, datt = after((wq, sent, qkv, datt), nq, np_)
    b2 = permute(sent, "rx", opposite)
    fq = permute(wq2, "ry", far)
    att0, dqkv0 = attention(qkv, datt, 0, half, rows, length, HEADS)

    b1, fp = after((b1, fp), att0)
    qkv, datt = after((qkv, datt), b1, fp)
    att1, dqkv1 = attention(qkv, datt, half, images - half, rows, length, HEADS)

    a1, b2 = after((a1, b2), att1)
    a2 = permute(a1, "rx", opposite)
    pair2 = pair_sum(kept, b2)
    s2 = permute(pair2, "rx", near)
    dqkv0, dqkv1 = after((dqkv0, dqkv1), pair2)
    acc = partial_qkv(normed, (dqkv0, dqkv1), wq, nq, a1, block)
    s2 = after(s2, acc)
    other = permute(s2, "rx", opposite)
    pair1 = pair_sum(wp, after(b1, s2))
    s1 = permute(pair1, "rx", near)
    out_p = new_proj(cot, (att0, att1), wp, np_, fp, s1)
    out_q = final_qkv(side.reshape(1), acc, fq, a2, s2, other, block)
    return out_q[None, None], out_p[None, None]


def solution(mesh):
    return jax.shard_map(
        local,
        mesh=mesh,
        in_specs=(
            P("rx", "ry", None, None, None),
            P("rx", "ry", None, None, None),
            P("rx", "ry", None, None),
            P("rx", "ry", None, None),
        ),
        out_specs=(P("rx", "ry", None, None), P("rx", "ry", None, None)),
        check_vma=False,
    )
```

time: 234 us -> 115 us (0.49)
  matrix products: 76.1 us -> 0 us
  waiting for transfers between devices: 114 us -> 46.8 us
  Pallas kernels: 0 us -> 46.3 us
  local copies, waits for them, and re-layouts: 23.8 us -> 5.13 us
  other arithmetic: 12.6 us -> 0 us
  starting transfers between devices: 6.94 us -> 15.2 us
    dot_general x9 -> x0, matrix products: 66.8 us -> none  [the longest x1 17.1 us: local_grads(): jnp.einsum('bhqk,bkhe->bqhe', d_scores, keys, preferred_element_type=f32)]
    ppermute x4 -> x11, waiting for transfers between devices: 114 us -> 46.8 us  [permute(): return lax.ppermute(block, axis, [(i, partner(i, n)) for i in range(n)])]
    pallas_call x0 -> x9, Pallas kernels: none -> 46.3 us  [call(): pl.pallas_call(body, in_specs=in_specs or [whole] * len(operands), out_sp...]
    add x1 -> x0, other arithmetic: 9.46 us -> none  [neighbour_total(): return total + stacked.astype(wide)]
    slice x4 -> x0, local copies, waits for them, and re-layouts: 9.33 us -> none  [the longest x2 3.83 us: local_grads(): values = qkv[:, :, 2 * width:].reshape(images, length, HEADS, head_size)]
    sub x1 -> x0, matrix products: 9.3 us -> none  [local_grads(): probs = jax.nn.softmax(scores, axis=-1)]
    ppermute x4 -> x11, starting transfers between devices: 6.94 us -> 15.2 us  [permute(): return lax.ppermute(block, axis, [(i, partner(i, n)) for i in range(n)])]
    reshape x3 -> x0, local copies, waits for them, and re-layouts: 7.51 us -> none  [the longest x1 2.51 us: local_grads(): d_values.reshape(images, length, width)]
  transfers between devices with their start and end apart: 4 -> 11, of which waited for: 4 -> 7; matrix products, arithmetic and copies ran while one was open for 38% -> 0% of each run, Pallas kernels for 0% -> 37%
where the time goes in v2:
time: 115 us; the launch traced here: 114 us
  waiting for transfers between devices  46.8 us (41%)
  Pallas kernels  46.3 us (40%)
  starting transfers between devices  15.2 us (13%)
  local copies, waits for them, and re-layouts  5.13 us (4%)
    ppermute x11, waiting for transfers between devices, permute(): return lax.ppermute(block, axis, [(i, partner(i, n)) for i in range(n)])  46.8 us
    pallas_call x9, Pallas kernels, call(): pl.pallas_call(body, in_specs=in_specs or [whole] * len(operands), out_sp...  46.3 us
    ppermute x11, starting transfers between devices, permute(): return lax.ppermute(block, axis, [(i, partner(i, n)) for i in range(n)])  15.2 us
    unnamed x12, local copies, waits for them, and re-layouts  4.85 us
  transfers between devices with their start and end apart: 11, of which 7 were waited for; matrix products, arithmetic and copies ran while one was open for 0% of the time, Pallas kernels for 37%

profile of v2, /device:TPU:0, one launch (start us, length us, event | category | flops | bytes accessed | tf_op | source)
XLA Modules:
  0.0 114.2 jit_solution(1745668531388941166)
XLA Ops:
  0.6 0.5 collective-permute-start
  1.2 4.7 %collective-permute-start.5 = (bf16[768,768]{1,0:T(8,128)(2,1)}, bf16[768,768]{1,0:T(8,128)(2,1)}, u32[]{:S(2)}, u32[]{:S(2)}) collective-permute-start(bf16[768,768]{1,0:T(8,128)(2,1)} %bitcast.21), channel_id=1, source_target_pairs={{0,7},{1,2},{2,1},{3,4},{4,3},{5,6},{6,5},{7,0},{8,15},{9,10},{10,... | collective-permute-start | bytes 3538952 | tf_op jit(solution)/shard_map/ppermute | solution.py:279
  5.9 1.5 %collective-permute-start.4 = (bf16[768,768]{1,0:T(8,128)(2,1)}, bf16[768,768]{1,0:T(8,128)(2,1)}, u32[]{:S(2)}, u32[]{:S(2)}) collective-permute-start(bf16[768,768]{1,0:T(8,128)(2,1)} %bitcast.22), channel_id=1, source_target_pairs={{0,16},{8,24},{16,0},{24,8},{1,17},{9,25},{17,1},{25,9},{2,18},{10... | collective-permute-start | bytes 3538952 | tf_op jit(solution)/shard_map/ppermute | solution.py:279
  7.5 2.0 %copy-done = bf16[1,1,768,2304]{3,2,1,0:T(8,128)(2,1)S(1)} copy-done((bf16[1,1,768,2304]{3,2,1,0:T(8,128)(2,1)S(1)}, bf16[1,1,768,2304]{3,2,1,0:T(8,128)(2,1)}, u32[]{:S(2)}) %copy-start) | copy-done | bytes 3538968
  9.5 1.6 %first_rows.1 = bf16[384,2304]{1,0:T(8,128)(2,1)} custom-call(bf16[768,2304]{1,0:T(8,128)(2,1)S(1)} %bitcast.14), custom_call_target="tpu_custom_call" | custom-call | bytes 3538944 | tf_op jit(solution)/shard_map/first_rows/pallas_call | solution.py:24
  11.0 1.6 %collective-permute-start.1 = (bf16[384,2304]{1,0:T(8,128)(2,1)}, bf16[384,2304]{1,0:T(8,128)(2,1)}, u32[]{:S(2)}, u32[]{:S(2)}) collective-permute-start(bf16[384,2304]{1,0:T(8,128)(2,1)} %first_rows.1), channel_id=1, source_target_pairs={{0,8},{8,0},{16,24},{24,16},{1,9},{9,1},{17,25},{25,17},{2,10},{10... | collective-permute-start | bytes 5308424 | tf_op jit(solution)/shard_map/ppermute | solution.py:279
  12.6 0.1 dynamic-slice_bitcast_fusion
  12.7 1.1 %copy-done.3 = bf16[1,1,4,197,768]{4,2,3,1,0:T(4,128)(2,1)S(1)} copy-done((bf16[1,1,4,197,768]{4,2,3,1,0:T(4,128)(2,1)S(1)}, bf16[1,1,4,197,768]{4,2,3,1,0:T(4,128)(2,1)}, u32[]{:S(2)}) %copy-start.3) | copy-done | bytes 1210392
  13.9 0.1 copy.8
  14.0 0.3 copy-done.4
  14.3 0.1 copy.9
  14.6 1.2 %copy-done.2 = bf16[1,1,768,768]{3,2,1,0:T(8,128)(2,1)S(1)} copy-done((bf16[1,1,768,768]{3,2,1,0:T(8,128)(2,1)S(1)}, bf16[1,1,768,768]{3,2,1,0:T(8,128)(2,1)}, u32[]{:S(2)}) %copy-start.2) | copy-done | bytes 1179672
  15.8 6.0 %project.1 = (bf16[768,832]{1,0:T(8,128)(2,1)S(1)}, bf16[832,2304]{1,0:T(8,128)(2,1)S(1)}, bf16[832,768]{1,0:T(8,128)(2,1)S(1)}) custom-call(bf16[832,768]{1,0:T(8,128)(2,1)S(1)} %bitcast.26, bf16[832,768]{1,0:T(8,128)(2,1)S(1)} %bitcast.18, bf16[768,2304]{1,0:T(8,128)(2,1)S(1)} %bitcast.15, bf16[768,768]{1,0:T(8,128)(2,1)S(1)} %bitcast.23), custom_call_target="tpu_custom_call" | custom-call | flops 3925868544 | bytes 14942208 | tf_op jit(solution)/shard_map/project/pallas_call | solution.py:24
  21.9 0.6 collective-permute-start.3
  22.4 9.9 %attention.2 = (bf16[1536,208]{1,0:T(8,128)(2,1)S(1)}, bf16[416,2304]{1,0:T(8,128)(2,1)S(1)}) custom-call(bf16[832,2304]{1,0:T(8,128)(2,1)S(1)} %get-tuple-element.32.qkv, bf16[832,768]{1,0:T(8,128)(2,1)S(1)} %get-tuple-element.33.datt), custom_call_target="tpu_custom_call" | custom-call | flops 3925868544 | bytes 5111808 | tf_op jit(solution)/shard_map/attention/pallas_call | solution.py:24
  32.3 0.4 collective-permute-done.5.fp
  32.7 2.5 %collective-permute-done.4.b = bf16[768,768]{1,0:T(8,128)(2,1)} collective-permute-done((bf16[768,768]{1,0:T(8,128)(2,1)}, bf16[768,768]{1,0:T(8,128)(2,1)}, u32[]{:S(2)}, u32[]{:S(2)}) %collective-permute-start.4) | collective-permute-done | bytes 1179680 | tf_op jit(solution)/shard_map/ppermute | solution.py:279
  35.2 9.9 %attention.3 = (bf16[1536,208]{1,0:T(8,128)(2,1)S(1)}, bf16[416,2304]{1,0:T(8,128)(2,1)S(1)}) custom-call(bf16[832,2304]{1,0:T(8,128)(2,1)S(1)} %get-tuple-element.32.qkv, bf16[832,768]{1,0:T(8,128)(2,1)S(1)} %get-tuple-element.33.datt), custom_call_target="tpu_custom_call" | custom-call | flops 3925868544 | bytes 5111808 | tf_op jit(solution)/shard_map/attention/pallas_call | solution.py:24
  45.1 5.0 %collective-permute-done.1.a1 = bf16[384,2304]{1,0:T(8,128)(2,1)} collective-permute-done((bf16[384,2304]{1,0:T(8,128)(2,1)}, bf16[384,2304]{1,0:T(8,128)(2,1)}, u32[]{:S(2)}, u32[]{:S(2)}) %collective-permute-start.1) | collective-permute-done | bytes 1769504 | tf_op jit(solution)/shard_map/ppermute | solution.py:279
  50.1 1.3 %collective-permute-done.3.b = bf16[192,2304]{1,0:T(8,128)(2,1)S(1)} collective-permute-done((bf16[192,2304]{1,0:T(8,128)(2,1)S(1)}, bf16[192,2304]{1,0:T(8,128)(2,1)S(1)}, u32[]{:S(2)}, u32[]{:S(2)}) %collective-permute-start.3) | collective-permute-done | bytes 884768 | tf_op jit(solution)/shard_map/ppermute | solution.py:279
  51.4 0.2 pair_sum.2
  51.6 1.6 %collective-permute-start.8 = (bf16[192,2304]{1,0:T(8,128)(2,1)S(1)}, bf16[192,2304]{1,0:T(8,128)(2,1)S(1)}, u32[]{:S(2)}, u32[]{:S(2)}) collective-permute-start(bf16[192,2304]{1,0:T(8,128)(2,1)S(1)} %pair_sum.2), channel_id=1, source_target_pairs={{0,8},{8,0},{16,24},{24,16},{1,9},{9,1},{17,25},{25,17},{2,10},{10... | collective-permute-start | bytes 2654216 | tf_op jit(solution)/shard_map/ppermute | solution.py:279
  53.2 1.5 %collective-permute-start.7 = (bf16[384,2304]{1,0:T(8,128)(2,1)}, bf16[384,2304]{1,0:T(8,128)(2,1)S(1)}, u32[]{:S(2)}, u32[]{:S(2)}) collective-permute-start(bf16[384,2304]{1,0:T(8,128)(2,1)} %collective-permute-done.1.a1), channel_id=1, source_target_pairs={{0,16},{8,24},{16,0},{24,8},{1,17},{9,25},{17,1},{25,9},{2,18},{10... | collective-permute-start | bytes 5308424 | tf_op jit(solution)/shard_map/ppermute | solution.py:279
  54.7 8.8 %partial_qkv.1.acc = f32[768,2304]{1,0:T(8,128)S(1)} custom-call(bf16[768,832]{1,0:T(8,128)(2,1)S(1)} %get-tuple-element.23.normed, bf16[768,2304]{1,0:T(8,128)(2,1)S(1)} %bitcast.17, bf16[768,2304]{1,0:T(8,128)(2,1)} %collective-permute-done.nq, bf16[384,2304]{1,0:T(8,128)(2,1)} %collective-permute-done.1.a1, ...), custom_call_target="tpu_custom_call" | custom-call | flops 2944401408 | bytes 21233664 | tf_op jit(solution)/shard_map/partial_qkv/pallas_call | solution.py:24
  63.5 7.3 %collective-permute-done.8.s2 = bf16[192,2304]{1,0:T(8,128)(2,1)S(1)} collective-permute-done((bf16[192,2304]{1,0:T(8,128)(2,1)S(1)}, bf16[192,2304]{1,0:T(8,128)(2,1)S(1)}, u32[]{:S(2)}, u32[]{:S(2)}) %collective-permute-start.8) | collective-permute-done | bytes 884768 | tf_op jit(solution)/shard_map/ppermute | solution.py:279
  70.8 1.5 %pair_sum.3 = bf16[768,768]{1,0:T(8,128)(2,1)S(1)} custom-call(bf16[768,768]{1,0:T(8,128)(2,1)S(1)} %bitcast.24, bf16[768,768]{1,0:T(8,128)(2,1)} %collective-permute-done.4.b), custom_call_target="tpu_custom_call" | custom-call | flops 589824 | bytes 3538944 | tf_op jit(solution)/shard_map/pair_sum/pallas_call | solution.py:24
  72.3 1.6 %collective-permute-start.10 = (bf16[768,768]{1,0:T(8,128)(2,1)S(1)}, bf16[768,768]{1,0:T(8,128)(2,1)S(1)}, u32[]{:S(2)}, u32[]{:S(2)}) collective-permute-start(bf16[768,768]{1,0:T(8,128)(2,1)S(1)} %pair_sum.3), channel_id=1, source_target_pairs={{0,8},{8,0},{16,24},{24,16},{1,9},{9,1},{17,25},{25,17},{2,10},{10... | collective-permute-start | bytes 3538952 | tf_op jit(solution)/shard_map/ppermute | solution.py:279
  73.9 1.5 %collective-permute-start.9 = (bf16[192,2304]{1,0:T(8,128)(2,1)S(1)}, bf16[192,2304]{1,0:T(8,128)(2,1)S(1)}, u32[]{:S(2)}, u32[]{:S(2)}) collective-permute-start(bf16[192,2304]{1,0:T(8,128)(2,1)S(1)} %collective-permute-done.8.s2), channel_id=1, source_target_pairs={{0,16},{8,24},{16,0},{24,8},{1,17},{9,25},{17,1},{25,9},{2,18},{10... | collective-permute-start | bytes 2654216 | tf_op jit(solution)/shard_map/ppermute | solution.py:279
  75.4 21.5 %collective-permute-done.10.sp = bf16[768,768]{1,0:T(8,128)(2,1)S(1)} collective-permute-done((bf16[768,768]{1,0:T(8,128)(2,1)S(1)}, bf16[768,768]{1,0:T(8,128)(2,1)S(1)}, u32[]{:S(2)}, u32[]{:S(2)}) %collective-permute-start.10) | collective-permute-done | bytes 1179680 | tf_op jit(solution)/shard_map/ppermute | solution.py:279
  96.9 4.4 %new_proj.1 = bf16[768,768]{1,0:T(8,128)(2,1)} custom-call(bf16[832,768]{1,0:T(8,128)(2,1)S(1)} %bitcast.19, bf16[768,768]{1,0:T(8,128)(2,1)S(1)} %bitcast.25, bf16[768,768]{1,0:T(8,128)(2,1)} %collective-permute-done.2.np_, bf16[768,768]{1,0:T(8,128)(2,1)} %collective-permute-done.5.fp, bf16[768,768]{1,0:T(8,128)(2,1)S(1)} %collective-permute-done.10.sp, ...), custom_call_target="tpu_custom_call" | custom-call | flops 981467136 | bytes 7077888 | tf_op jit(solution)/shard_map/new_proj/pallas_call | solution.py:24
  101.4 8.8 %collective-permute-done.9.other = bf16[192,2304]{1,0:T(8,128)(2,1)S(1)} collective-permute-done((bf16[192,2304]{1,0:T(8,128)(2,1)S(1)}, bf16[192,2304]{1,0:T(8,128)(2,1)S(1)}, u32[]{:S(2)}, u32[]{:S(2)}) %collective-permute-start.9) | collective-permute-done | bytes 884768 | tf_op jit(solution)/shard_map/ppermute | solution.py:279
  110.1 4.0 %final_qkv.1 = bf16[768,2304]{1,0:T(8,128)(2,1)} custom-call(s32[1]{0:T(128)} %bitcast.side, f32[768,2304]{1,0:T(8,128)S(1)} %partial_qkv.1.acc, bf16[768,2304]{1,0:T(8,128)(2,1)S(1)} %collective-permute-done.6.fq, bf16[384,2304]{1,0:T(8,128)(2,1)S(1)} %collective-permute-done.7.a2, bf16[192,2304]{1,0:T(8,128)(2,1)S(1)} %collective-permute-done.8.s2, ...), custom_call_target="tpu_custom_call" | custom-call | flops 7077888 | bytes 17694720 | tf_op jit(solution)/shard_map/final_qkv/pallas_call | solution.py:24
  (14 shorter events, 0.3 us)
Async XLA Ops:
  0.6 21.1 %collective-permute-start = (bf16[768,2304]{1,0:T(8,128)(2,1)}, bf16[768,2304]{1,0:T(8,128)(2,1)}, u32[]{:S(2)}, u32[]{:S(2)}) collective-permute-start(bf16[768,2304]{1,0:T(8,128)(2,1)} %bitcast.13), channel_id=1, source_target_pairs={{0,1},{1,0},{2,3},{3,2},{4,5},{5,4},{6,7},{7,6},{8,9},{9,8},{10,11... | collective-permute-start | bytes 10616840 | tf_op jit(solution)/shard_map/ppermute | solution.py:279
  1.1 20.6 %collective-permute-start.2 = (bf16[768,768]{1,0:T(8,128)(2,1)}, bf16[768,768]{1,0:T(8,128)(2,1)}, u32[]{:S(2)}, u32[]{:S(2)}) collective-permute-start(bf16[768,768]{1,0:T(8,128)(2,1)} %bitcast.20), channel_id=1, source_target_pairs={{0,1},{1,0},{2,3},{3,2},{4,5},{5,4},{6,7},{7,6},{8,9},{9,8},{10,11... | collective-permute-start | bytes 3538952 | tf_op jit(solution)/shard_map/ppermute | solution.py:279
  1.2 31.5 %collective-permute-start.5 = (bf16[768,768]{1,0:T(8,128)(2,1)}, bf16[768,768]{1,0:T(8,128)(2,1)}, u32[]{:S(2)}, u32[]{:S(2)}) collective-permute-start(bf16[768,768]{1,0:T(8,128)(2,1)} %bitcast.21), channel_id=1, source_target_pairs={{0,7},{1,2},{2,1},{3,4},{4,3},{5,6},{6,5},{7,0},{8,15},{9,10},{10,... | collective-permute-start | bytes 3538952 | tf_op jit(solution)/shard_map/ppermute | solution.py:279
  5.9 29.2 %collective-permute-start.4 = (bf16[768,768]{1,0:T(8,128)(2,1)}, bf16[768,768]{1,0:T(8,128)(2,1)}, u32[]{:S(2)}, u32[]{:S(2)}) collective-permute-start(bf16[768,768]{1,0:T(8,128)(2,1)} %bitcast.22), channel_id=1, source_target_pairs={{0,16},{8,24},{16,0},{24,8},{1,17},{9,25},{17,1},{25,9},{2,18},{10... | collective-permute-start | bytes 3538952 | tf_op jit(solution)/shard_map/ppermute | solution.py:279
  7.5 2.0 %copy-start = (bf16[1,1,768,2304]{3,2,1,0:T(8,128)(2,1)S(1)}, bf16[1,1,768,2304]{3,2,1,0:T(8,128)(2,1)}, u32[]{:S(2)}) copy-start(bf16[1,1,768,2304]{3,2,1,0:T(8,128)(2,1)} %param.6) | copy-start | bytes 10616836
  9.5 3.1 %copy-start.1 = (bf16[1,1,768,2304]{3,2,1,0:T(8,128)(2,1)S(1)}, bf16[1,1,768,2304]{3,2,1,0:T(8,128)(2,1)}, u32[]{:S(2)}) copy-start(bf16[1,1,768,2304]{3,2,1,0:T(8,128)(2,1)} %param.6) | copy-start | bytes 10616836
  11.0 39.0 %collective-permute-start.1 = (bf16[384,2304]{1,0:T(8,128)(2,1)}, bf16[384,2304]{1,0:T(8,128)(2,1)}, u32[]{:S(2)}, u32[]{:S(2)}) collective-permute-start(bf16[384,2304]{1,0:T(8,128)(2,1)} %first_rows.1), channel_id=1, source_target_pairs={{0,8},{8,0},{16,24},{24,16},{1,9},{9,1},{17,25},{25,17},{2,10},{10... | collective-permute-start | bytes 5308424 | tf_op jit(solution)/shard_map/ppermute | solution.py:279
  12.6 1.3 %copy-start.3 = (bf16[1,1,4,197,768]{4,2,3,1,0:T(4,128)(2,1)S(1)}, bf16[1,1,4,197,768]{4,2,3,1,0:T(4,128)(2,1)}, u32[]{:S(2)}) copy-start(bf16[1,1,4,197,768]{4,2,3,1,0:T(4,128)(2,1)} %param.4) | copy-start | bytes 3631108
  12.7 1.6 %copy-start.4 = (bf16[1,1,4,197,768]{4,2,3,1,0:T(4,128)(2,1)S(1)}, bf16[1,1,4,197,768]{4,2,3,1,0:T(4,128)(2,1)}, u32[]{:S(2)}) copy-start(bf16[1,1,4,197,768]{4,2,3,1,0:T(4,128)(2,1)} %param.5) | copy-start | bytes 3631108
  14.5 1.3 %copy-start.2 = (bf16[1,1,768,768]{3,2,1,0:T(8,128)(2,1)S(1)}, bf16[1,1,768,768]{3,2,1,0:T(8,128)(2,1)}, u32[]{:S(2)}) copy-start(bf16[1,1,768,768]{3,2,1,0:T(8,128)(2,1)} %param.7) | copy-start | bytes 3538948
  21.8 88.4 %collective-permute-start.6 = (bf16[768,2304]{1,0:T(8,128)(2,1)S(1)}, bf16[768,2304]{1,0:T(8,128)(2,1)S(1)}, u32[]{:S(2)}, u32[]{:S(2)}) collective-permute-start(bf16[768,2304]{1,0:T(8,128)(2,1)S(1)} %bitcast.16), channel_id=1, source_target_pairs={{0,7},{1,2},{2,1},{3,4},{4,3},{5,6},{6,5},{7,0},{8,15},{9,10},{10,... | collective-permute-start | bytes 10616840 | tf_op jit(solution)/shard_map/ppermute | solution.py:279
  21.9 29.5 %collective-permute-start.3 = (bf16[192,2304]{1,0:T(8,128)(2,1)S(1)}, bf16[192,2304]{1,0:T(8,128)(2,1)S(1)}, u32[]{:S(2)}, u32[]{:S(2)}) collective-permute-start(bf16[192,2304]{1,0:T(8,128)(2,1)S(1)} %get-tuple-element.26), channel_id=1, source_target_pairs={{0,16},{8,24},{16,0},{24,8},{1,17},{9,25},{17,1},{25,9},{2,18},{10... | collective-permute-start | bytes 2654216 | tf_op jit(solution)/shard_map/ppermute | solution.py:279
  51.6 19.2 %collective-permute-start.8 = (bf16[192,2304]{1,0:T(8,128)(2,1)S(1)}, bf16[192,2304]{1,0:T(8,128)(2,1)S(1)}, u32[]{:S(2)}, u32[]{:S(2)}) collective-permute-start(bf16[192,2304]{1,0:T(8,128)(2,1)S(1)} %pair_sum.2), channel_id=1, source_target_pairs={{0,8},{8,0},{16,24},{24,16},{1,9},{9,1},{17,25},{25,17},{2,10},{10... | collective-permute-start | bytes 2654216 | tf_op jit(solution)/shard_map/ppermute | solution.py:279
  53.2 57.0 %collective-permute-start.7 = (bf16[384,2304]{1,0:T(8,128)(2,1)}, bf16[384,2304]{1,0:T(8,128)(2,1)S(1)}, u32[]{:S(2)}, u32[]{:S(2)}) collective-permute-start(bf16[384,2304]{1,0:T(8,128)(2,1)} %collective-permute-done.1.a1), channel_id=1, source_target_pairs={{0,16},{8,24},{16,0},{24,8},{1,17},{9,25},{17,1},{25,9},{2,18},{10... | collective-permute-start | bytes 5308424 | tf_op jit(solution)/shard_map/ppermute | solution.py:279
  72.3 24.6 %collective-permute-start.10 = (bf16[768,768]{1,0:T(8,128)(2,1)S(1)}, bf16[768,768]{1,0:T(8,128)(2,1)S(1)}, u32[]{:S(2)}, u32[]{:S(2)}) collective-permute-start(bf16[768,768]{1,0:T(8,128)(2,1)S(1)} %pair_sum.3), channel_id=1, source_target_pairs={{0,8},{8,0},{16,24},{24,16},{1,9},{9,1},{17,25},{25,17},{2,10},{10... | collective-permute-start | bytes 3538952 | tf_op jit(solution)/shard_map/ppermute | solution.py:279
  73.9 36.2 %collective-permute-start.9 = (bf16[192,2304]{1,0:T(8,128)(2,1)S(1)}, bf16[192,2304]{1,0:T(8,128)(2,1)S(1)}, u32[]{:S(2)}, u32[]{:S(2)}) collective-permute-start(bf16[192,2304]{1,0:T(8,128)(2,1)S(1)} %collective-permute-done.8.s2), channel_id=1, source_target_pairs={{0,16},{8,24},{16,0},{24,8},{1,17},{9,25},{17,1},{25,9},{2,18},{10... | collective-permute-start | bytes 2654216 | tf_op jit(solution)/shard_map/ppermute | solution.py:279

commit v3 on v2

--- a/solution.py
+++ b/solution.py
@@ -18,7 +18,7 @@
     return lax.dot_general(a, b, (((ca,), (cb,)), ((), ())), preferred_element_type=F32)
 
 
-def call(body, outs, operands, name, flops, moved, vmem, grid=None, in_specs=None, out_specs=None, scratch=(), exps=0):
+def call(body, outs, operands, name, flops, moved, vmem, grid=None, in_specs=None, out_specs=None, scratch=(), exps=0, aliases=None, hint=1):
     whole = pl.BlockSpec(memory_space=pltpu.VMEM)
     kwargs = {} if grid is None else {"grid": grid}
     return pl.pallas_call(
@@ -28,7 +28,8 @@
         out_shape=[jax.ShapeDtypeStruct(shape, dtype) for shape, dtype in outs],
         scratch_shapes=list(scratch),
         compiler_params=pltpu.CompilerParams(vmem_limit_bytes=vmem * MIB),
-        cost_estimate=pl.CostEstimate(flops=flops, bytes_accessed=moved, transcendentals=exps),
+        cost_estimate=pl.CostEstimate(flops=int(flops * hint), bytes_accessed=int(moved * hint), transcendentals=int(exps * hint)),
+        input_output_aliases=aliases or {},
         name=name,
         **kwargs,
     )(*operands)
@@ -122,7 +123,7 @@
     lax.fori_loop(0, heads // pack, group, 0, unroll=unroll)
 
 
-def attention(qkv, datt, first, count, rows, length, heads, unroll=6):
+def attention(qkv, datt, first, count, rows, length, heads, hint=1, unroll=6):
     width = datt.shape[1]
     here = lambda b: (b + first, 0)
     there = lambda b: (b, 0)
@@ -138,109 +139,125 @@
         in_specs=[pl.BlockSpec((rows, 3 * width), here), pl.BlockSpec((rows, width), here)],
         out_specs=[pl.BlockSpec((width, rows), there), pl.BlockSpec((rows, 3 * width), there)],
         exps=count * heads * rows * rows,
+        hint=hint,
     )
 
 
-def weight_grad(left, rights):
-    at, total = 0, 0.0
-    for right in rights:
-        total = total + mm(left[:, at : at + right.shape[0]], right[...], 1, 0)
-        at += right.shape[0]
-    return total
-
-
-def partial_body(top, parts, normed, wq, nq, a1, *refs):
+def partial_body(parts, normed, wq, nq, a1, *refs):
     dqkv, acc = refs[:parts], refs[parts]
-    i = pl.program_id(0)
-    scale = (wq.shape[1] // 3) ** -0.5
-    total = wq[...].astype(F32) + nq[...].astype(F32)
-    total = total + jnp.where(i < top, a1[...].astype(F32), 0.0)
-    acc[...] = total / 5.0 - LR * (weight_grad(normed, dqkv) * scale)
-
-
-def partial_qkv(normed, dqkv, wq, nq, a1, block):
+    rows, wide = wq.shape
+    width = wide // 3
+    scale = width**-0.5
+    for first, last in ((0, a1.shape[0]), (a1.shape[0], rows)):
+        part = slice(first, last)
+        for c in range(0, wide, width):
+            cols = slice(c, c + width)
+            at, grad = 0, 0.0
+            for d in dqkv:
+                grad = grad + mm(normed[part, at : at + d.shape[0]], d[:, cols], 1, 0)
+                at += d.shape[0]
+            total = wq[part, cols].astype(F32) + nq[part, cols].astype(F32)
+            if first == 0:
+                total = total + a1[:, cols].astype(F32)
+            acc[part, cols] = total * 0.2 - LR * (grad * scale)
+
+
+def partial_qkv(normed, dqkv, wq, nq, a1):
     width, total = normed.shape
     wide = wq.shape[1]
-    top = a1.shape[0] // block
-    row = pl.BlockSpec((block, wide), lambda i: (i, 0))
-    return call(
-        functools.partial(partial_body, top, len(dqkv)),
+    return call(
+        functools.partial(partial_body, len(dqkv)),
         [(wq.shape, F32)],
         (normed, wq, nq, a1, *dqkv),
         "partial_qkv",
         flops=2 * total * width * wide,
         moved=12 * width * wide,
-        vmem=32,
-        grid=(width // block,),
-        in_specs=[
-            pl.BlockSpec((block, total), lambda i: (i, 0)),
-            row,
-            row,
-            pl.BlockSpec((block, wide), lambda i: (jnp.minimum(i, top - 1), 0)),
-            *[pl.BlockSpec(d.shape, lambda i: (0, 0)) for d in dqkv],
-        ],
-        out_specs=[row],
-    )[0]
-
-
-def proj_body(parts, cot, wp, np_, fp, sp, *refs):
-    att, out = refs[:parts], refs[parts]
+        vmem=16,
+    )[0]
+
+
+def partial_proj_body(parts, cot, wp, np_, fp, *refs):
+    att, acc = refs[:parts], refs[parts]
     scale = wp.shape[0] ** -0.5
-    total = wp[...].astype(F32) + np_[...].astype(F32) + fp[...].astype(F32) + sp[...].astype(F32)
+    total = wp[...].astype(F32) + np_[...].astype(F32) + fp[...].astype(F32)
     rows, width = att[0].shape[1], wp.shape[1]
     at, grad = 0, 0.0
     for a in att:
         for r in range(0, a.shape[0], width):
             grad = grad + mm(a[r : r + width], cot[at : at + rows], 1, 0)
             at += rows
-    out[...] = (total / 5.0 - LR * (grad * scale)).astype(BF16)
-
-
-def new_proj(cot, att, wp, np_, fp, sp):
+    acc[...] = total * 0.2 - LR * (grad * scale)
+
+
+def partial_proj(cot, att, wp, np_, fp):
     total, width = cot.shape
     return call(
-        functools.partial(proj_body, len(att)),
-        [(wp.shape, BF16)],
-        (cot, wp, np_, fp, sp, *att),
-        "new_proj",
+        functools.partial(partial_proj_body, len(att)),
+        [(wp.shape, F32)],
+        (cot, wp, np_, fp, *att),
+        "partial_proj",
         flops=2 * total * width * width,
         moved=12 * width * width,
         vmem=16,
-    )[0]
-
-
-def final_body(top, side, acc, fq, a2, s2, other, out):
-    i = pl.program_id(0)
-    half = (pl.num_programs(0) - top) // 2
-    mine = (i - top) // half == side[0]
-    rest = jnp.where(mine, s2[...], other[...])
-    late = fq[...].astype(F32) + jnp.where(i < top, a2[...], rest).astype(F32)
-    out[...] = (acc[...] + late / 5.0).astype(BF16)
-
-
-def final_qkv(side, acc, fq, a2, s2, other, block):
+        hint=10,
+    )[0]
+
+
+def final_proj_body(acc, s1, out):
+    out[...] = (acc[...] + s1[...].astype(F32) * 0.2).astype(BF16)
+
+
+def final_proj(acc, s1):
+    return call(
+        final_proj_body,
+        [(acc.shape, BF16)],
+        (acc, s1),
+        "final_proj",
+        flops=2 * acc.size,
+        moved=8 * acc.size,
+        vmem=8,
+    )[0]
+
+
+def final_body(cuts, side, acc, fq, a2, s2, other, out, held, done):
+    top, half = a2.shape[0], s2.shape[0]
+    copies = []
+    for k, (first, last) in enumerate(zip(cuts, cuts[1:])):
+        part = slice(first, last)
+        if first < top:
+            late = a2[part]
+        else:
+            low = slice((first - top) % half, (first - top) % half + last - first)
+            late = jnp.where(side[0] == (first - top) // half, s2[low], other[low])
+        late = fq[part].astype(F32) + late.astype(F32)
+        held[part] = (acc[part] + late * 0.2).astype(BF16)
+        part = pl.ds(first, last - first)
+        copies.append(pltpu.make_async_copy(held.at[part], out.at[part], done.at[k]))
+        copies[-1].start()
+    for copy in copies:
+        copy.wait()
+
+
+def final_qkv(side, acc, fq, a2, s2, other):
     rows, wide = acc.shape
-    top, half = a2.shape[0] // block, s2.shape[0] // block
-    row = lambda at: pl.BlockSpec((block, wide), lambda i: (at(i), 0))
-    low = row(lambda i: jnp.maximum(i - top, 0) % half)
-    return call(
-        functools.partial(final_body, top),
+    top, half = a2.shape[0], s2.shape[0]
+    cuts = []
+    for first, last in ((0, top), (top, top + half), (top + half, rows)):
+        steps = max(1, (last - first) // 96)
+        cuts += [first + (last - first) * k // steps // 16 * 16 for k in range(steps)]
+    cuts = (*cuts, rows)
+    whole = pl.BlockSpec(memory_space=pltpu.VMEM)
+    return call(
+        functools.partial(final_body, cuts),
         [(acc.shape, BF16)],
         (side, acc, fq, a2, s2, other),
         "final_qkv",
         flops=4 * rows * wide,
         moved=10 * rows * wide,
         vmem=16,
-        grid=(rows // block,),
-        in_specs=[
-            pl.BlockSpec(memory_space=pltpu.SMEM),
-            row(lambda i: i),
-            row(lambda i: i),
-            row(lambda i: jnp.minimum(i, top - 1)),
-            low,
-            low,
-        ],
-        out_specs=[row(lambda i: i)],
+        in_specs=[pl.BlockSpec(memory_space=pltpu.SMEM)] + [whole] * 5,
+        out_specs=[pl.BlockSpec(memory_space=pl.ANY)],
+        scratch=[pltpu.VMEM((rows, wide), BF16), pltpu.SemaphoreType.DMA((len(cuts) - 1,))],
     )[0]
 
 
@@ -254,23 +271,30 @@
     )[0]
 
 
-def rows_body(count, source, out, done):
-    copy = pltpu.make_async_copy(source.at[:count], out, done)
-    copy.start()
-    copy.wait()
+def rows_body(source, out, done):
+    pieces = done.shape[0]
+    rows = out.shape[0] // pieces
+    copies = []
+    for k in range(pieces):
+        part = pl.ds(k * rows, rows)
+        copies.append(pltpu.make_async_copy(source.at[part], out.at[part], done.at[k]))
+    for copy in copies:
+        copy.start()
+    for copy in copies:
+        copy.wait()
 
 
 def first_rows(a, count):
     return call(
-        functools.partial(rows_body, count),
+        rows_body,
         [((count, a.shape[1]), a.dtype)],
         (a,),
         "first_rows",
         flops=0,
         moved=4 * count * a.shape[1],
         vmem=8,
-        in_specs=[pl.BlockSpec(memory_space=pl.ANY)],
-        scratch=[pltpu.SemaphoreType.DMA],
+        in_specs=[pl.BlockSpec(memory_space=pltpu.HBM)],
+        scratch=[pltpu.SemaphoreType.DMA((2,))],
     )[0]
 
 
@@ -328,8 +352,8 @@
         gp = jnp.einsum("bdt,bte->de", att.reshape(images, width, rows), cot.reshape(images, rows, width), preferred_element_type=F32) * scale
         return plain_average(wq, gq)[None, None], plain_average(wp, gp)[None, None]
 
-    block = width // 8
-    cut, part = 4 * block, 2 * block
+    cut = width * 11 // 24
+    part = (width - cut) // 2
     side = lax.axis_index("rx") // 2
     top = first_rows(wq, cut)
     sent = lax.dynamic_slice_in_dim(wq, cut + (1 - side) * part, part)
@@ -350,18 +374,20 @@
     qkv, datt = after((qkv, datt), b1, fp)
     att1, dqkv1 = attention(qkv, datt, half, images - half, rows, length, HEADS)
 
-    a1, b2 = after((a1, b2), att1)
+    a1, b2 = after(a1, att1), after(b2, att1)
     a2 = permute(a1, "rx", opposite)
     pair2 = pair_sum(kept, b2)
     s2 = permute(pair2, "rx", near)
     dqkv0, dqkv1 = after((dqkv0, dqkv1), pair2)
-    acc = partial_qkv(normed, (dqkv0, dqkv1), wq, nq, a1, block)
+    acc = partial_qkv(normed, (dqkv0, dqkv1), wq, nq, a1)
     s2 = after(s2, acc)
     other = permute(s2, "rx", opposite)
     pair1 = pair_sum(wp, after(b1, s2))
     s1 = permute(pair1, "rx", near)
-    out_p = new_proj(cot, (att0, att1), wp, np_, fp, s1)
-    out_q = final_qkv(side.reshape(1), acc, fq, a2, s2, other, block)
+    acc_p = partial_proj(cot, after((att0, att1), pair1, a2), wp, np_, fp)
+    out_p = final_proj(acc_p, s1)
+    fq, a2, other = after((fq, a2, other), out_p)
+    out_q = final_qkv(side.reshape(1), acc, fq, a2, s2, other)
     return out_q[None, None], out_p[None, None]
 
 

time: 115 us -> 111 us (0.965)
  local copies, waits for them, and re-layouts: 5.13 us -> 11.8 us
  waiting for transfers between devices: 46.8 us -> 41.1 us
  Pallas kernels: 46.3 us -> 42.5 us
    unnamed x12 -> x32, local copies, waits for them, and re-layouts: 4.85 us -> 11.5 us
    ppermute x11, waiting for transfers between devices: 46.8 us -> 41.1 us  [permute(): return lax.ppermute(block, axis, [(i, partner(i, n)) for i in range(n)])]
    pallas_call x9 -> x10, Pallas kernels: 46.3 us -> 42.5 us  [call(): pl.pallas_call(body, in_specs=in_specs or [whole] * len(operands), out_sp...]
  transfers between devices with their start and end apart: 11 -> 11, of which waited for: 7 -> 5; matrix products, arithmetic and copies ran while one was open for 0% -> 0% of each run, Pallas kernels for 37% -> 36%
where the time goes in v3:
time: 111 us
  Pallas kernels  42.5 us (38%)
  waiting for transfers between devices  41.1 us (37%)
  starting transfers between devices  14.2 us (13%)
  local copies, waits for them, and re-layouts  11.8 us (11%)
    pallas_call x10, Pallas kernels, call(): pl.pallas_call(body, in_specs=in_specs or [whole] * len(operands), out_sp...  42.5 us
    ppermute x11, waiting for transfers between devices, permute(): return lax.ppermute(block, axis, [(i, partner(i, n)) for i in range(n)])  41.1 us
    ppermute x11, starting transfers between devices, permute(): return lax.ppermute(block, axis, [(i, partner(i, n)) for i in range(n)])  14.2 us
    unnamed x32, local copies, waits for them, and re-layouts  11.5 us
  transfers between devices with their start and end apart: 11, of which 5 were waited for; matrix products, arithmetic and copies ran while one was open for 0% of the time, Pallas kernels for 36%

profile of v3, /device:TPU:0, one launch (start us, length us, event | category | flops | bytes accessed | tf_op | source)
XLA Modules:
  0.0 110.7 jit_solution(4117678730595241601)
XLA Ops:
  0.6 0.5 collective-permute-start
  1.2 4.7 %collective-permute-start.4 = (bf16[768,768]{1,0:T(8,128)(2,1)}, bf16[768,768]{1,0:T(8,128)(2,1)}, u32[]{:S(2)}, u32[]{:S(2)}) collective-permute-start(bf16[768,768]{1,0:T(8,128)(2,1)} %bitcast.22), channel_id=1, source_target_pairs={{0,7},{1,2},{2,1},{3,4},{4,3},{5,6},{6,5},{7,0},{8,15},{9,10},{10,... | collective-permute-start | bytes 3538952 | tf_op jit(solution)/shard_map/ppermute | solution.py:303
  5.9 1.5 %collective-permute-start.3 = (bf16[768,768]{1,0:T(8,128)(2,1)}, bf16[768,768]{1,0:T(8,128)(2,1)}, u32[]{:S(2)}, u32[]{:S(2)}) collective-permute-start(bf16[768,768]{1,0:T(8,128)(2,1)} %bitcast.23), channel_id=1, source_target_pairs={{0,16},{8,24},{16,0},{24,8},{1,17},{9,25},{17,1},{25,9},{2,18},{10... | collective-permute-start | bytes 3538952 | tf_op jit(solution)/shard_map/ppermute | solution.py:303
  7.5 2.0 %copy-done = bf16[1,1,768,2304]{3,2,1,0:T(8,128)(2,1)S(1)} copy-done((bf16[1,1,768,2304]{3,2,1,0:T(8,128)(2,1)S(1)}, bf16[1,1,768,2304]{3,2,1,0:T(8,128)(2,1)}, u32[]{:S(2)}) %copy-start) | copy-done | bytes 3538968
  9.5 1.3 %first_rows.1 = bf16[352,2304]{1,0:T(8,128)(2,1)} custom-call(bf16[768,2304]{1,0:T(8,128)(2,1)S(1)} %bitcast.14), custom_call_target="tpu_custom_call" | custom-call | bytes 3244032 | tf_op jit(solution)/shard_map/first_rows/pallas_call | solution.py:24
  10.8 1.6 %collective-permute-start.1 = (bf16[352,2304]{1,0:T(8,128)(2,1)}, bf16[352,2304]{1,0:T(8,128)(2,1)}, u32[]{:S(2)}, u32[]{:S(2)}) collective-permute-start(bf16[352,2304]{1,0:T(8,128)(2,1)} %first_rows.1), channel_id=1, source_target_pairs={{0,8},{8,0},{16,24},{24,16},{1,9},{9,1},{17,25},{25,17},{2,10},{10... | collective-permute-start | bytes 4866056 | tf_op jit(solution)/shard_map/ppermute | solution.py:303
  12.9 2.2 %copy-done.1 = bf16[1,1,768,2304]{3,2,1,0:T(8,128)(2,1)S(1)} copy-done((bf16[1,1,768,2304]{3,2,1,0:T(8,128)(2,1)S(1)}, bf16[1,1,768,2304]{3,2,1,0:T(8,128)(2,1)}, u32[]{:S(2)}) %copy-start.1) | copy-done | bytes 3538968
  15.1 0.4 copy-done.6
  15.5 6.0 %project.1 = (bf16[768,832]{1,0:T(8,128)(2,1)S(1)}, bf16[832,2304]{1,0:T(8,128)(2,1)S(1)}, bf16[832,768]{1,0:T(8,128)(2,1)S(1)}) custom-call(bf16[832,768]{1,0:T(8,128)(2,1)S(1)} %bitcast.20, bf16[832,768]{1,0:T(8,128)(2,1)S(1)} %bitcast.18, bf16[768,2304]{1,0:T(8,128)(2,1)S(1)} %bitcast.15, bf16[768,768]{1,0:T(8,128)(2,1)S(1)} %bitcast.24), custom_call_target="tpu_custom_call" | custom-call | flops 3925868544 | bytes 14942208 | tf_op jit(solution)/shard_map/project/pallas_call | solution.py:24
  21.5 1.1 copy-done.2
  22.6 1.8 %copy-done.8 = bf16[832,2304]{1,0:T(8,128)(2,1)} copy-done((bf16[832,2304]{1,0:T(8,128)(2,1)}, bf16[832,2304]{1,0:T(8,128)(2,1)S(1)}, u32[]{:S(2)}) %copy-start.8) | copy-done | bytes 3833880
  24.4 1.1 %copy-done.10 = bf16[832,768]{1,0:T(8,128)(2,1)} copy-done((bf16[832,768]{1,0:T(8,128)(2,1)}, bf16[832,768]{1,0:T(8,128)(2,1)S(1)}, u32[]{:S(2)}) %copy-start.10) | copy-done | bytes 1277976
  25.8 0.6 collective-permute-start.5
  26.3 1.3 %copy-done.9 = bf16[832,2304]{1,0:T(8,128)(2,1)S(1)} copy-done((bf16[832,2304]{1,0:T(8,128)(2,1)S(1)}, bf16[832,2304]{1,0:T(8,128)(2,1)}, u32[]{:S(2)}) %copy-start.9) | copy-done | bytes 3833880
  27.6 1.3 %copy-done.11 = bf16[832,768]{1,0:T(8,128)(2,1)S(1)} copy-done((bf16[832,768]{1,0:T(8,128)(2,1)S(1)}, bf16[832,768]{1,0:T(8,128)(2,1)}, u32[]{:S(2)}) %copy-start.11) | copy-done | bytes 1277976
  28.9 9.9 %attention.2 = (bf16[1536,208]{1,0:T(8,128)(2,1)S(1)}, bf16[416,2304]{1,0:T(8,128)(2,1)S(1)}) custom-call(bf16[832,2304]{1,0:T(8,128)(2,1)S(1)} %copy-done.9, bf16[832,768]{1,0:T(8,128)(2,1)S(1)} %copy-done.11), custom_call_target="tpu_custom_call" | custom-call | flops 3925868544 | bytes 5111808 | tf_op jit(solution)/shard_map/attention/pallas_call | solution.py:24
  38.8 10.1 %attention.3 = (bf16[1536,208]{1,0:T(8,128)(2,1)S(1)}, bf16[416,2304]{1,0:T(8,128)(2,1)S(1)}) custom-call(bf16[832,2304]{1,0:T(8,128)(2,1)S(1)} %copy-done.9, bf16[832,768]{1,0:T(8,128)(2,1)S(1)} %copy-done.12), custom_call_target="tpu_custom_call" | custom-call | flops 3925868544 | bytes 5111808 | tf_op jit(solution)/shard_map/attention/pallas_call | solution.py:24
  48.9 0.6 collective-permute-start.7
  49.5 6.1 %collective-permute-done.5.b = bf16[208,2304]{1,0:T(8,128)(2,1)S(1)} collective-permute-done((bf16[208,2304]{1,0:T(8,128)(2,1)S(1)}, bf16[208,2304]{1,0:T(8,128)(2,1)S(1)}, u32[]{:S(2)}, u32[]{:S(2)}) %collective-permute-start.5) | collective-permute-done | bytes 958496 | tf_op jit(solution)/shard_map/ppermute | solution.py:303
  55.6 0.2 pair_sum.2
  55.8 1.6 %collective-permute-start.8 = (bf16[208,2304]{1,0:T(8,128)(2,1)S(1)}, bf16[208,2304]{1,0:T(8,128)(2,1)S(1)}, u32[]{:S(2)}, u32[]{:S(2)}) collective-permute-start(bf16[208,2304]{1,0:T(8,128)(2,1)S(1)} %pair_sum.2), channel_id=1, source_target_pairs={{0,8},{8,0},{16,24},{24,16},{1,9},{9,1},{17,25},{25,17},{2,10},{10... | collective-permute-start | bytes 2875400 | tf_op jit(solution)/shard_map/ppermute | solution.py:303
  57.4 6.6 %partial_qkv.1.acc = f32[768,2304]{1,0:T(8,128)S(1)} custom-call(bf16[768,832]{1,0:T(8,128)(2,1)S(1)} %copy-done.3, bf16[768,2304]{1,0:T(8,128)(2,1)S(1)} %bitcast.17, bf16[768,2304]{1,0:T(8,128)(2,1)} %collective-permute-done.nq, bf16[352,2304]{1,0:T(8,128)(2,1)} %collective-permute-done.1.a1, bf16[416,2304]{1,0:T(8,128)(2,1)S(1)} %get-tuple-element.44.refs_0_, ...), custom_call_target="tpu_custom_call" | custom-call | flops 2944401408 | bytes 21233664 | tf_op jit(solution)/shard_map/partial_qkv/pallas_call | solution.py:24
  64.0 11.6 %collective-permute-done.8.s2 = bf16[208,2304]{1,0:T(8,128)(2,1)S(1)} collective-permute-done((bf16[208,2304]{1,0:T(8,128)(2,1)S(1)}, bf16[208,2304]{1,0:T(8,128)(2,1)S(1)}, u32[]{:S(2)}, u32[]{:S(2)}) %collective-permute-start.8) | collective-permute-done | bytes 958496 | tf_op jit(solution)/shard_map/ppermute | solution.py:303
  75.7 1.5 %pair_sum.3 = bf16[768,768]{1,0:T(8,128)(2,1)S(1)} custom-call(bf16[768,768]{1,0:T(8,128)(2,1)S(1)} %bitcast.25, bf16[768,768]{1,0:T(8,128)(2,1)} %collective-permute-done.3.b), custom_call_target="tpu_custom_call" | custom-call | flops 589824 | bytes 3538944 | tf_op jit(solution)/shard_map/pair_sum/pallas_call | solution.py:24
  77.2 1.6 %collective-permute-start.10 = (bf16[768,768]{1,0:T(8,128)(2,1)S(1)}, bf16[768,768]{1,0:T(8,128)(2,1)S(1)}, u32[]{:S(2)}, u32[]{:S(2)}) collective-permute-start(bf16[768,768]{1,0:T(8,128)(2,1)S(1)} %pair_sum.3), channel_id=1, source_target_pairs={{0,8},{8,0},{16,24},{24,16},{1,9},{9,1},{17,25},{25,17},{2,10},{10... | collective-permute-start | bytes 3538952 | tf_op jit(solution)/shard_map/ppermute | solution.py:303
  78.8 1.5 %collective-permute-start.9 = (bf16[208,2304]{1,0:T(8,128)(2,1)S(1)}, bf16[208,2304]{1,0:T(8,128)(2,1)S(1)}, u32[]{:S(2)}, u32[]{:S(2)}) collective-permute-start(bf16[208,2304]{1,0:T(8,128)(2,1)S(1)} %collective-permute-done.8.s2), channel_id=1, source_target_pairs={{0,16},{8,24},{16,0},{24,8},{1,17},{9,25},{17,1},{25,9},{2,18},{10... | collective-permute-start | bytes 2875400 | tf_op jit(solution)/shard_map/ppermute | solution.py:303
  80.3 10.1 %collective-permute-done.7.a2 = bf16[352,2304]{1,0:T(8,128)(2,1)S(1)} collective-permute-done((bf16[352,2304]{1,0:T(8,128)(2,1)}, bf16[352,2304]{1,0:T(8,128)(2,1)S(1)}, u32[]{:S(2)}, u32[]{:S(2)}) %collective-permute-start.7) | collective-permute-done | bytes 1622048 | tf_op jit(solution)/shard_map/ppermute | solution.py:303
  90.4 3.3 %partial_proj.1.acc = f32[768,768]{1,0:T(8,128)S(1)} custom-call(bf16[832,768]{1,0:T(8,128)(2,1)S(1)} %bitcast.19, bf16[768,768]{1,0:T(8,128)(2,1)S(1)} %bitcast.26, bf16[768,768]{1,0:T(8,128)(2,1)} %collective-permute-done.2.np_, bf16[768,768]{1,0:T(8,128)(2,1)} %collective-permute-done.4.fp, bf16[1536,208]{1,0:T(8,128)(2,1)S(1)} %get-tuple-element.49.refs_0_, ...), custom_call_target="tpu_custom_call" | custom-call | flops 9814671360 | bytes 70778880 | tf_op jit(solution)/shard_map/partial_proj/pallas_call | solution.py:24
  93.7 5.5 %collective-permute-done.10.s1 = bf16[768,768]{1,0:T(8,128)(2,1)S(1)} collective-permute-done((bf16[768,768]{1,0:T(8,128)(2,1)S(1)}, bf16[768,768]{1,0:T(8,128)(2,1)S(1)}, u32[]{:S(2)}, u32[]{:S(2)}) %collective-permute-start.10) | collective-permute-done | bytes 1179680 | tf_op jit(solution)/shard_map/ppermute | solution.py:303
  99.2 1.3 %final_proj.1 = bf16[768,768]{1,0:T(8,128)(2,1)} custom-call(f32[768,768]{1,0:T(8,128)S(1)} %partial_proj.1.acc, bf16[768,768]{1,0:T(8,128)(2,1)S(1)} %collective-permute-done.10.s1), custom_call_target="tpu_custom_call" | custom-call | flops 1179648 | bytes 4718592 | tf_op jit(solution)/shard_map/final_proj/pallas_call | solution.py:24
  100.5 7.8 %collective-permute-done.9.other = bf16[208,2304]{1,0:T(8,128)(2,1)S(1)} collective-permute-done((bf16[208,2304]{1,0:T(8,128)(2,1)S(1)}, bf16[208,2304]{1,0:T(8,128)(2,1)S(1)}, u32[]{:S(2)}, u32[]{:S(2)}) %collective-permute-start.9) | collective-permute-done | bytes 958496 | tf_op jit(solution)/shard_map/ppermute | solution.py:303
  108.3 2.2 %final_qkv.1 = bf16[768,2304]{1,0:T(8,128)(2,1)} custom-call(s32[1]{0:T(128)} %bitcast.side, f32[768,2304]{1,0:T(8,128)S(1)} %partial_qkv.1.acc, bf16[768,2304]{1,0:T(8,128)(2,1)S(1)} %collective-permute-done.6.fq, bf16[352,2304]{1,0:T(8,128)(2,1)S(1)} %collective-permute-done.7.a2, bf16[208,2304]{1,0:T(8,128)(2,1)S(1)} %collective-permute-done.8.s2, ...), custom_call_target="tpu_custom_call" | custom-call | flops 7077888 | bytes 17694720 | tf_op jit(solution)/shard_map/final_qkv/pallas_call | solution.py:24
  (35 shorter events, 0.8 us)
Async XLA Ops:
  0.6 25.0 %collective-permute-start = (bf16[768,2304]{1,0:T(8,128)(2,1)}, bf16[768,2304]{1,0:T(8,128)(2,1)}, u32[]{:S(2)}, u32[]{:S(2)}) collective-permute-start(bf16[768,2304]{1,0:T(8,128)(2,1)} %bitcast.13), channel_id=1, source_target_pairs={{0,1},{1,0},{2,3},{3,2},{4,5},{5,4},{6,7},{7,6},{8,9},{9,8},{10,11... | collective-permute-start | bytes 10616840 | tf_op jit(solution)/shard_map/ppermute | solution.py:303
  1.1 24.5 %collective-permute-start.2 = (bf16[768,768]{1,0:T(8,128)(2,1)}, bf16[768,768]{1,0:T(8,128)(2,1)}, u32[]{:S(2)}, u32[]{:S(2)}) collective-permute-start(bf16[768,768]{1,0:T(8,128)(2,1)} %bitcast.21), channel_id=1, source_target_pairs={{0,1},{1,0},{2,3},{3,2},{4,5},{5,4},{6,7},{7,6},{8,9},{9,8},{10,11... | collective-permute-start | bytes 3538952 | tf_op jit(solution)/shard_map/ppermute | solution.py:303
  1.2 37.6 %collective-permute-start.4 = (bf16[768,768]{1,0:T(8,128)(2,1)}, bf16[768,768]{1,0:T(8,128)(2,1)}, u32[]{:S(2)}, u32[]{:S(2)}) collective-permute-start(bf16[768,768]{1,0:T(8,128)(2,1)} %bitcast.22), channel_id=1, source_target_pairs={{0,7},{1,2},{2,1},{3,4},{4,3},{5,6},{6,5},{7,0},{8,15},{9,10},{10,... | collective-permute-start | bytes 3538952 | tf_op jit(solution)/shard_map/ppermute | solution.py:303
  5.9 32.9 %collective-permute-start.3 = (bf16[768,768]{1,0:T(8,128)(2,1)}, bf16[768,768]{1,0:T(8,128)(2,1)}, u32[]{:S(2)}, u32[]{:S(2)}) collective-permute-start(bf16[768,768]{1,0:T(8,128)(2,1)} %bitcast.23), channel_id=1, source_target_pairs={{0,16},{8,24},{16,0},{24,8},{1,17},{9,25},{17,1},{25,9},{2,18},{10... | collective-permute-start | bytes 3538952 | tf_op jit(solution)/shard_map/ppermute | solution.py:303
  7.5 2.0 %copy-start = (bf16[1,1,768,2304]{3,2,1,0:T(8,128)(2,1)S(1)}, bf16[1,1,768,2304]{3,2,1,0:T(8,128)(2,1)}, u32[]{:S(2)}) copy-start(bf16[1,1,768,2304]{3,2,1,0:T(8,128)(2,1)} %param.6) | copy-start | bytes 10616836
  9.5 2.9 %copy-start.13 = (bf16[1,1,4,197,768]{4,2,3,1,0:T(4,128)(2,1)S(1)}, bf16[1,1,4,197,768]{4,2,3,1,0:T(4,128)(2,1)}, u32[]{:S(2)}) copy-start(bf16[1,1,4,197,768]{4,2,3,1,0:T(4,128)(2,1)} %param.4) | copy-start | bytes 3631108
  10.8 1.7 %copy-start.14 = (bf16[1,1,4,197,768]{4,2,3,1,0:T(4,128)(2,1)S(1)}, bf16[1,1,4,197,768]{4,2,3,1,0:T(4,128)(2,1)}, u32[]{:S(2)}) copy-start(bf16[1,1,4,197,768]{4,2,3,1,0:T(4,128)(2,1)} %param.5) | copy-start | bytes 3631108
  10.8 38.1 %collective-permute-start.1 = (bf16[352,2304]{1,0:T(8,128)(2,1)}, bf16[352,2304]{1,0:T(8,128)(2,1)}, u32[]{:S(2)}, u32[]{:S(2)}) collective-permute-start(bf16[352,2304]{1,0:T(8,128)(2,1)} %first_rows.1), channel_id=1, source_target_pairs={{0,8},{8,0},{16,24},{24,16},{1,9},{9,1},{17,25},{25,17},{2,10},{10... | collective-permute-start | bytes 4866056 | tf_op jit(solution)/shard_map/ppermute | solution.py:303
  12.7 2.5 %copy-start.1 = (bf16[1,1,768,2304]{3,2,1,0:T(8,128)(2,1)S(1)}, bf16[1,1,768,2304]{3,2,1,0:T(8,128)(2,1)}, u32[]{:S(2)}) copy-start(bf16[1,1,768,2304]{3,2,1,0:T(8,128)(2,1)} %param.6) | copy-start | bytes 10616836
  12.8 2.7 %copy-start.6 = (bf16[1,1,768,768]{3,2,1,0:T(8,128)(2,1)S(1)}, bf16[1,1,768,768]{3,2,1,0:T(8,128)(2,1)}, u32[]{:S(2)}) copy-start(bf16[1,1,768,768]{3,2,1,0:T(8,128)(2,1)} %param.7) | copy-start | bytes 3538948
  12.9 8.6 %copy-start.4 = (bf16[4,208,768]{2,1,0:T(8,128)(2,1)}, bf16[4,208,768]{2,1,0:T(8,128)(2,1)S(1)}, u32[]{:S(2)}) copy-start(bf16[4,208,768]{2,1,0:T(8,128)(2,1)S(1)} %pad.8.clone) | copy-start | bytes 3833860
  21.5 1.1 copy-start.2
  22.6 1.8 %copy-start.8 = (bf16[832,2304]{1,0:T(8,128)(2,1)}, bf16[832,2304]{1,0:T(8,128)(2,1)S(1)}, u32[]{:S(2)}) copy-start(bf16[832,2304]{1,0:T(8,128)(2,1)S(1)} %get-tuple-element.36.qkv) | copy-start | bytes 11501572
  24.4 1.1 %copy-start.10 = (bf16[832,768]{1,0:T(8,128)(2,1)}, bf16[832,768]{1,0:T(8,128)(2,1)S(1)}, u32[]{:S(2)}) copy-start(bf16[832,768]{1,0:T(8,128)(2,1)S(1)} %get-tuple-element.37.datt) | copy-start | bytes 3833860
  25.5 2.1 %copy-start.9 = (bf16[832,2304]{1,0:T(8,128)(2,1)S(1)}, bf16[832,2304]{1,0:T(8,128)(2,1)}, u32[]{:S(2)}) copy-start(bf16[832,2304]{1,0:T(8,128)(2,1)} %copy-done.8) | copy-start | bytes 11501572
  25.7 82.6 %collective-permute-start.6 = (bf16[768,2304]{1,0:T(8,128)(2,1)S(1)}, bf16[768,2304]{1,0:T(8,128)(2,1)S(1)}, u32[]{:S(2)}, u32[]{:S(2)}) collective-permute-start(bf16[768,2304]{1,0:T(8,128)(2,1)S(1)} %bitcast.16), channel_id=1, source_target_pairs={{0,7},{1,2},{2,1},{3,4},{4,3},{5,6},{6,5},{7,0},{8,15},{9,10},{10,... | collective-permute-start | bytes 10616840 | tf_op jit(solution)/shard_map/ppermute | solution.py:303
  25.8 29.8 %collective-permute-start.5 = (bf16[208,2304]{1,0:T(8,128)(2,1)S(1)}, bf16[208,2304]{1,0:T(8,128)(2,1)S(1)}, u32[]{:S(2)}, u32[]{:S(2)}) collective-permute-start(bf16[208,2304]{1,0:T(8,128)(2,1)S(1)} %get-tuple-element.42), channel_id=1, source_target_pairs={{0,16},{8,24},{16,0},{24,8},{1,17},{9,25},{17,1},{25,9},{2,18},{10... | collective-permute-start | bytes 2875400 | tf_op jit(solution)/shard_map/ppermute | solution.py:303
  27.6 1.3 %copy-start.11 = (bf16[832,768]{1,0:T(8,128)(2,1)S(1)}, bf16[832,768]{1,0:T(8,128)(2,1)}, u32[]{:S(2)}) copy-start(bf16[832,768]{1,0:T(8,128)(2,1)} %copy-done.10) | copy-start | bytes 3833860
  28.9 9.9 %copy-start.12 = (bf16[832,768]{1,0:T(8,128)(2,1)S(1)}, bf16[832,768]{1,0:T(8,128)(2,1)}, u32[]{:S(2)}) copy-start(bf16[832,768]{1,0:T(8,128)(2,1)} %copy-done.10) | copy-start | bytes 3833860
  48.9 41.4 %collective-permute-start.7 = (bf16[352,2304]{1,0:T(8,128)(2,1)}, bf16[352,2304]{1,0:T(8,128)(2,1)S(1)}, u32[]{:S(2)}, u32[]{:S(2)}) collective-permute-start(bf16[352,2304]{1,0:T(8,128)(2,1)} %collective-permute-done.1.a1), channel_id=1, source_target_pairs={{0,16},{8,24},{16,0},{24,8},{1,17},{9,25},{17,1},{25,9},{2,18},{10... | collective-permute-start | bytes 4866056 | tf_op jit(solution)/shard_map/ppermute | solution.py:303
  55.6 1.8 %copy-start.3 = (bf16[768,832]{1,0:T(8,128)(2,1)S(1)}, bf16[768,832]{1,0:T(8,128)(2,1)}, u32[]{:S(2)}) copy-start(bf16[768,832]{1,0:T(8,128)(2,1)} %copy-done.2) | copy-start | bytes 3833860
  55.8 19.8 %collective-permute-start.8 = (bf16[208,2304]{1,0:T(8,128)(2,1)S(1)}, bf16[208,2304]{1,0:T(8,128)(2,1)S(1)}, u32[]{:S(2)}, u32[]{:S(2)}) collective-permute-start(bf16[208,2304]{1,0:T(8,128)(2,1)S(1)} %pair_sum.2), channel_id=1, source_target_pairs={{0,8},{8,0},{16,24},{24,16},{1,9},{9,1},{17,25},{25,17},{2,10},{10... | collective-permute-start | bytes 2875400 | tf_op jit(solution)/shard_map/ppermute | solution.py:303
  57.4 18.3 %copy-start.7 = (bf16[1,1,768,768]{3,2,1,0:T(8,128)(2,1)S(1)}, bf16[1,1,768,768]{3,2,1,0:T(8,128)(2,1)}, u32[]{:S(2)}) copy-start(bf16[1,1,768,768]{3,2,1,0:T(8,128)(2,1)} %param.7) | copy-start | bytes 3538948
  64.0 26.3 %copy-start.5 = (bf16[4,208,768]{2,1,0:T(8,128)(2,1)S(1)}, bf16[4,208,768]{2,1,0:T(8,128)(2,1)}, u32[]{:S(2)}) copy-start(bf16[4,208,768]{2,1,0:T(8,128)(2,1)} %copy-done.4) | copy-start | bytes 3833860
  77.2 21.9 %collective-permute-start.10 = (bf16[768,768]{1,0:T(8,128)(2,1)S(1)}, bf16[768,768]{1,0:T(8,128)(2,1)S(1)}, u32[]{:S(2)}, u32[]{:S(2)}) collective-permute-start(bf16[768,768]{1,0:T(8,128)(2,1)S(1)} %pair_sum.3), channel_id=1, source_target_pairs={{0,8},{8,0},{16,24},{24,16},{1,9},{9,1},{17,25},{25,17},{2,10},{10... | collective-permute-start | bytes 3538952 | tf_op jit(solution)/shard_map/ppermute | solution.py:303
  78.8 29.5 %collective-permute-start.9 = (bf16[208,2304]{1,0:T(8,128)(2,1)S(1)}, bf16[208,2304]{1,0:T(8,128)(2,1)S(1)}, u32[]{:S(2)}, u32[]{:S(2)}) collective-permute-start(bf16[208,2304]{1,0:T(8,128)(2,1)S(1)} %collective-permute-done.8.s2), channel_id=1, source_target_pairs={{0,16},{8,24},{16,0},{24,8},{1,17},{9,25},{17,1},{25,9},{2,18},{10... | collective-permute-start | bytes 2875400 | tf_op jit(solution)/shard_map/ppermute | solution.py:303

commit v4 on v3

--- a/solution.py
+++ b/solution.py
@@ -219,45 +219,83 @@
     )[0]
 
 
-def final_body(cuts, side, acc, fq, a2, s2, other, out, held, done):
+def chunks(first, last):
+    steps = max(1, (last - first) // 96)
+    cuts = [first + (last - first) * k // steps // 16 * 16 for k in range(steps)] + [last]
+    return list(zip(cuts, cuts[1:]))
+
+
+def early_body(side, acc, f0, a2, s2, out, token, held, done):
     top, half = a2.shape[0], s2.shape[0]
     copies = []
-    for k, (first, last) in enumerate(zip(cuts, cuts[1:])):
+    for first, last in chunks(0, top) + chunks(top, top + half):
         part = slice(first, last)
         if first < top:
+            there = pl.ds(first, last - first)
             late = a2[part]
         else:
-            low = slice((first - top) % half, (first - top) % half + last - first)
-            late = jnp.where(side[0] == (first - top) // half, s2[low], other[low])
-        late = fq[part].astype(F32) + late.astype(F32)
-        held[part] = (acc[part] + late * 0.2).astype(BF16)
-        part = pl.ds(first, last - first)
-        copies.append(pltpu.make_async_copy(held.at[part], out.at[part], done.at[k]))
+            there = pl.ds(pl.multiple_of(first + side[0] * half, 16), last - first)
+            late = s2[first - top : last - top]
+        late = f0[part].astype(F32) + late.astype(F32)
+        held[part] = (acc[there] + late * 0.2).astype(BF16)
+        copies.append(pltpu.make_async_copy(held.at[part], out.at[there], done.at[len(copies)]))
         copies[-1].start()
     for copy in copies:
         copy.wait()
-
-
-def final_qkv(side, acc, fq, a2, s2, other):
-    rows, wide = acc.shape
-    top, half = a2.shape[0], s2.shape[0]
-    cuts = []
-    for first, last in ((0, top), (top, top + half), (top + half, rows)):
-        steps = max(1, (last - first) // 96)
-        cuts += [first + (last - first) * k // steps // 16 * 16 for k in range(steps)]
-    cuts = (*cuts, rows)
+    token[...] = jnp.zeros_like(token)
+
+
+def early_rows(side, acc, f0, a2, s2):
+    top, half, wide = a2.shape[0], s2.shape[0], acc.shape[1]
+    steps = len(chunks(0, top) + chunks(top, top + half))
     whole = pl.BlockSpec(memory_space=pltpu.VMEM)
     return call(
-        functools.partial(final_body, cuts),
+        early_body,
+        [(acc.shape, BF16), ((8, 128), F32)],
+        (side, acc, f0, a2, s2),
+        "early_rows",
+        flops=4 * f0.size,
+        moved=10 * f0.size,
+        vmem=16,
+        in_specs=[pl.BlockSpec(memory_space=pltpu.SMEM)] + [whole] * 4,
+        out_specs=[pl.BlockSpec(memory_space=pl.ANY), whole],
+        scratch=[pltpu.VMEM((top + half, wide), BF16), pltpu.SemaphoreType.DMA((steps,))],
+    )
+
+
+def last_body(side, acc, f1, other, early, out, held, done):
+    half = other.shape[0]
+    top = acc.shape[0] - 2 * half
+    copies = []
+    for first, last in chunks(0, half):
+        part = slice(first, last)
+        there = pl.ds(pl.multiple_of(top + first + (1 - side[0]) * half, 16), last - first)
+        late = f1[part].astype(F32) + other[part].astype(F32)
+        held[part] = (acc[there] + late * 0.2).astype(BF16)
+        copies.append(pltpu.make_async_copy(held.at[part], out.at[there], done.at[len(copies)]))
+        copies[-1].start()
+    for copy in copies:
+        copy.wait()
+
+
+def last_rows(side, acc, f1, other, early):
+    whole = pl.BlockSpec(memory_space=pltpu.VMEM)
+    anywhere = pl.BlockSpec(memory_space=pl.ANY)
+    return call(
+        last_body,
         [(acc.shape, BF16)],
-        (side, acc, fq, a2, s2, other),
-        "final_qkv",
-        flops=4 * rows * wide,
-        moved=10 * rows * wide,
+        (side, acc, f1, other, early),
+        "last_rows",
+        flops=4 * f1.size,
+        moved=10 * f1.size,
         vmem=16,
-        in_specs=[pl.BlockSpec(memory_space=pltpu.SMEM)] + [whole] * 5,
-        out_specs=[pl.BlockSpec(memory_space=pl.ANY)],
-        scratch=[pltpu.VMEM((rows, wide), BF16), pltpu.SemaphoreType.DMA((len(cuts) - 1,))],
+        in_specs=[pl.BlockSpec(memory_space=pltpu.SMEM)] + [whole] * 3 + [anywhere],
+        out_specs=[anywhere],
+        scratch=[
+            pltpu.VMEM(other.shape, BF16),
+            pltpu.SemaphoreType.DMA((len(chunks(0, other.shape[0])),)),
+        ],
+        aliases={4: 0},
     )[0]
 
 
@@ -365,9 +403,10 @@
     np_ = permute(wp, "ry", near)
     normed, qkv, datt = project(tokens, cot, wq, wp, rows)
 
-    wq2, sent, qkv, datt = after((wq, sent, qkv, datt), nq, np_)
+    most = jnp.concatenate([top, kept], axis=0)
+    most, sent, qkv, datt = after((most, sent, qkv, datt), nq, np_)
     b2 = permute(sent, "rx", opposite)
-    fq = permute(wq2, "ry", far)
+    f0 = permute(most, "ry", far)
     att0, dqkv0 = attention(qkv, datt, 0, half, rows, length, HEADS)
 
     b1, fp = after((b1, fp), att0)
@@ -385,9 +424,12 @@
     pair1 = pair_sum(wp, after(b1, s2))
     s1 = permute(pair1, "rx", near)
     acc_p = partial_proj(cot, after((att0, att1), pair1, a2), wp, np_, fp)
-    out_p = final_proj(acc_p, s1)
-    fq, a2, other = after((fq, a2, other), out_p)
-    out_q = final_qkv(side.reshape(1), acc, fq, a2, s2, other)
+    f1 = permute(after(sent, s2), "ry", far)
+    side = side.reshape(1)
+    early, token = early_rows(side, acc, f0, a2, s2)
+    out_p = final_proj(acc_p, after(s1, token))
+    f1, other = after(f1, out_p), after(other, out_p)
+    out_q = last_rows(side, acc, f1, other, early)
     return out_q[None, None], out_p[None, None]
 
 

time: 111 us -> 110 us (level)
  local copies, waits for them, and re-layouts: 11.8 us -> 9.8 us
  waiting for transfers between devices: 41.1 us -> 39.2 us
  other arithmetic: 0 us -> 1.74 us
  Pallas kernels: 42.5 us -> 43.9 us
    unnamed x32 -> x30, local copies, waits for them, and re-layouts: 11.5 us -> 9.5 us
    ppermute x11 -> x12, waiting for transfers between devices: 41.1 us -> 39.2 us  [permute(): return lax.ppermute(block, axis, [(i, partner(i, n)) for i in range(n)])]
    concatenate x0 -> x1, other arithmetic: none -> 1.74 us  [local(): most = jnp.concatenate([top, kept], axis=0)]
    pallas_call x10 -> x11, Pallas kernels: 42.5 us -> 43.9 us  [call(): pl.pallas_call(body, in_specs=in_specs or [whole] * len(operands), out_sp...]
    ppermute x11 -> x12, starting transfers between devices: 14.2 us -> 14.1 us  [permute(): return lax.ppermute(block, axis, [(i, partner(i, n)) for i in range(n)])]
  transfers between devices with their start and end apart: 11 -> 12, of which waited for: 5 -> 7; matrix products, arithmetic and copies ran while one was open for 0% -> 2% of each run, Pallas kernels for 36% -> 39%
where the time goes in v4:
time: 110 us
  Pallas kernels  43.9 us (40%)
  waiting for transfers between devices  39.2 us (36%)
  starting transfers between devices  14.1 us (13%)
  local copies, waits for them, and re-layouts  9.8 us (9%)
  other arithmetic  1.74 us (2%)
    pallas_call x11, Pallas kernels, call(): pl.pallas_call(body, in_specs=in_specs or [whole] * len(operands), out_sp...  43.9 us
    ppermute x12, waiting for transfers between devices, permute(): return lax.ppermute(block, axis, [(i, partner(i, n)) for i in range(n)])  39.2 us
    ppermute x12, starting transfers between devices, permute(): return lax.ppermute(block, axis, [(i, partner(i, n)) for i in range(n)])  14.1 us
    unnamed x30, local copies, waits for them, and re-layouts  9.5 us
  transfers between devices with their start and end apart: 12, of which 7 were waited for; matrix products, arithmetic and copies ran while one was open for 2% of the time, Pallas kernels for 39%

profile of v4, /device:TPU:0, one launch (start us, length us, event | category | flops | bytes accessed | tf_op | source)
XLA Modules:
  0.0 109.7 jit_solution(13017299573670670434)
XLA Ops:
  0.6 0.5 collective-permute-start
  1.1 4.7 %collective-permute-start.4 = (bf16[768,768]{1,0:T(8,128)(2,1)}, bf16[768,768]{1,0:T(8,128)(2,1)}, u32[]{:S(2)}, u32[]{:S(2)}) collective-permute-start(bf16[768,768]{1,0:T(8,128)(2,1)} %bitcast.20), channel_id=1, source_target_pairs={{0,7},{1,2},{2,1},{3,4},{4,3},{5,6},{6,5},{7,0},{8,15},{9,10},{10,... | collective-permute-start | bytes 3538952 | tf_op jit(solution)/shard_map/ppermute | solution.py:341
  5.9 1.5 %collective-permute-start.3 = (bf16[768,768]{1,0:T(8,128)(2,1)}, bf16[768,768]{1,0:T(8,128)(2,1)}, u32[]{:S(2)}, u32[]{:S(2)}) collective-permute-start(bf16[768,768]{1,0:T(8,128)(2,1)} %bitcast.21), channel_id=1, source_target_pairs={{0,16},{8,24},{16,0},{24,8},{1,17},{9,25},{17,1},{25,9},{2,18},{10... | collective-permute-start | bytes 3538952 | tf_op jit(solution)/shard_map/ppermute | solution.py:341
  7.4 2.0 %copy-done = bf16[1,1,768,2304]{3,2,1,0:T(8,128)(2,1)S(1)} copy-done((bf16[1,1,768,2304]{3,2,1,0:T(8,128)(2,1)S(1)}, bf16[1,1,768,2304]{3,2,1,0:T(8,128)(2,1)}, u32[]{:S(2)}) %copy-start) | copy-done | bytes 3538968
  9.4 1.3 %first_rows.1 = bf16[352,2304]{1,0:T(8,128)(2,1)} custom-call(bf16[768,2304]{1,0:T(8,128)(2,1)S(1)} %bitcast.14), custom_call_target="tpu_custom_call" | custom-call | bytes 3244032 | tf_op jit(solution)/shard_map/first_rows/pallas_call | solution.py:24
  10.7 1.6 %collective-permute-start.1 = (bf16[352,2304]{1,0:T(8,128)(2,1)}, bf16[352,2304]{1,0:T(8,128)(2,1)}, u32[]{:S(2)}, u32[]{:S(2)}) collective-permute-start(bf16[352,2304]{1,0:T(8,128)(2,1)} %first_rows.1), channel_id=1, source_target_pairs={{0,8},{8,0},{16,24},{24,16},{1,9},{9,1},{17,25},{25,17},{2,10},{10... | collective-permute-start | bytes 4866056 | tf_op jit(solution)/shard_map/ppermute | solution.py:341
  12.8 2.2 %copy-done.1 = bf16[1,1,768,2304]{3,2,1,0:T(8,128)(2,1)S(1)} copy-done((bf16[1,1,768,2304]{3,2,1,0:T(8,128)(2,1)S(1)}, bf16[1,1,768,2304]{3,2,1,0:T(8,128)(2,1)}, u32[]{:S(2)}) %copy-start.1) | copy-done | bytes 3538968
  15.4 6.0 %project.1 = (bf16[768,832]{1,0:T(8,128)(2,1)S(1)}, bf16[832,2304]{1,0:T(8,128)(2,1)S(1)}, bf16[832,768]{1,0:T(8,128)(2,1)S(1)}) custom-call(bf16[832,768]{1,0:T(8,128)(2,1)S(1)} %bitcast.19, bf16[832,768]{1,0:T(8,128)(2,1)S(1)} %bitcast.17, bf16[768,2304]{1,0:T(8,128)(2,1)S(1)} %bitcast.15, bf16[768,768]{1,0:T(8,128)(2,1)S(1)} %bitcast.23), custom_call_target="tpu_custom_call" | custom-call | flops 3925868544 | bytes 14942208 | tf_op jit(solution)/shard_map/project/pallas_call | solution.py:24
  21.4 1.1 copy-done.2
  22.5 1.8 %copy-done.8 = bf16[832,2304]{1,0:T(8,128)(2,1)} copy-done((bf16[832,2304]{1,0:T(8,128)(2,1)}, bf16[832,2304]{1,0:T(8,128)(2,1)S(1)}, u32[]{:S(2)}) %copy-start.8) | copy-done | bytes 3833880
  24.3 1.1 %copy-done.10 = bf16[832,768]{1,0:T(8,128)(2,1)} copy-done((bf16[832,768]{1,0:T(8,128)(2,1)}, bf16[832,768]{1,0:T(8,128)(2,1)S(1)}, u32[]{:S(2)}) %copy-start.10) | copy-done | bytes 1277976
  25.6 1.7 %pad_maximum_fusion = bf16[560,2304]{1,0:T(8,128)(2,1)S(1)} fusion(bf16[208,2304]{1,0:T(8,128)(2,1)S(1)} %get-tuple-element.57.a, bf16[352,2304]{1,0:T(8,128)(2,1)} %first_rows.1), kind=kLoop, calls=%fused_computation | loop fusion | flops 5160960 | bytes 5160960 | tf_op jit(solution)/shard_map/concatenate | solution.py:406
  27.4 0.6 collective-permute-start.5
  28.5 9.9 %attention.2 = (bf16[1536,208]{1,0:T(8,128)(2,1)S(1)}, bf16[416,2304]{1,0:T(8,128)(2,1)S(1)}) custom-call(bf16[832,2304]{1,0:T(8,128)(2,1)S(1)} %copy-done.9, bf16[832,768]{1,0:T(8,128)(2,1)S(1)} %copy-done.11), custom_call_target="tpu_custom_call" | custom-call | flops 3925868544 | bytes 5111808 | tf_op jit(solution)/shard_map/attention/pallas_call | solution.py:24
  38.4 10.1 %attention.3 = (bf16[1536,208]{1,0:T(8,128)(2,1)S(1)}, bf16[416,2304]{1,0:T(8,128)(2,1)S(1)}) custom-call(bf16[832,2304]{1,0:T(8,128)(2,1)S(1)} %copy-done.9, bf16[832,768]{1,0:T(8,128)(2,1)S(1)} %copy-done.11), custom_call_target="tpu_custom_call" | custom-call | flops 3925868544 | bytes 5111808 | tf_op jit(solution)/shard_map/attention/pallas_call | solution.py:24
  48.5 0.5 collective-permute-done.1.a1
  49.0 0.6 collective-permute-start.8
  49.5 3.8 %collective-permute-done.5.b = bf16[208,2304]{1,0:T(8,128)(2,1)S(1)} collective-permute-done((bf16[208,2304]{1,0:T(8,128)(2,1)S(1)}, bf16[208,2304]{1,0:T(8,128)(2,1)S(1)}, u32[]{:S(2)}, u32[]{:S(2)}) %collective-permute-start.5) | collective-permute-done | bytes 958496 | tf_op jit(solution)/shard_map/ppermute | solution.py:341
  53.6 1.6 %collective-permute-start.6 = (bf16[208,2304]{1,0:T(8,128)(2,1)S(1)}, bf16[208,2304]{1,0:T(8,128)(2,1)S(1)}, u32[]{:S(2)}, u32[]{:S(2)}) collective-permute-start(bf16[208,2304]{1,0:T(8,128)(2,1)S(1)} %pair_sum.2), channel_id=1, source_target_pairs={{0,8},{8,0},{16,24},{24,16},{1,9},{9,1},{17,25},{25,17},{2,10},{10... | collective-permute-start | bytes 2875400 | tf_op jit(solution)/shard_map/ppermute | solution.py:341
  55.2 6.7 %partial_qkv.1.acc = f32[768,2304]{1,0:T(8,128)S(1)} custom-call(bf16[768,832]{1,0:T(8,128)(2,1)S(1)} %copy-done.3, bf16[768,2304]{1,0:T(8,128)(2,1)S(1)} %bitcast.16, bf16[768,2304]{1,0:T(8,128)(2,1)} %collective-permute-done.nq, bf16[352,2304]{1,0:T(8,128)(2,1)} %collective-permute-done.1.a1, bf16[416,2304]{1,0:T(8,128)(2,1)S(1)} %get-tuple-element.45.refs_0_, ...), custom_call_target="tpu_custom_call" | custom-call | flops 2944401408 | bytes 21233664 | tf_op jit(solution)/shard_map/partial_qkv/pallas_call | solution.py:24
  61.9 12.5 %collective-permute-done.6.s2 = bf16[208,2304]{1,0:T(8,128)(2,1)S(1)} collective-permute-done((bf16[208,2304]{1,0:T(8,128)(2,1)S(1)}, bf16[208,2304]{1,0:T(8,128)(2,1)S(1)}, u32[]{:S(2)}, u32[]{:S(2)}) %collective-permute-start.6) | collective-permute-done | bytes 958496 | tf_op jit(solution)/shard_map/ppermute | solution.py:341
  74.4 1.5 %pair_sum.3 = bf16[768,768]{1,0:T(8,128)(2,1)S(1)} custom-call(bf16[768,768]{1,0:T(8,128)(2,1)S(1)} %bitcast.24, bf16[768,768]{1,0:T(8,128)(2,1)} %collective-permute-done.3.b), custom_call_target="tpu_custom_call" | custom-call | flops 589824 | bytes 3538944 | tf_op jit(solution)/shard_map/pair_sum/pallas_call | solution.py:24
  75.9 1.5 %collective-permute-start.9 = (bf16[768,768]{1,0:T(8,128)(2,1)S(1)}, bf16[768,768]{1,0:T(8,128)(2,1)S(1)}, u32[]{:S(2)}, u32[]{:S(2)}) collective-permute-start(bf16[768,768]{1,0:T(8,128)(2,1)S(1)} %pair_sum.3), channel_id=1, source_target_pairs={{0,8},{8,0},{16,24},{24,16},{1,9},{9,1},{17,25},{25,17},{2,10},{10... | collective-permute-start | bytes 3538952 | tf_op jit(solution)/shard_map/ppermute | solution.py:341
  77.4 1.5 %collective-permute-start.10 = (bf16[208,2304]{1,0:T(8,128)(2,1)S(1)}, bf16[208,2304]{1,0:T(8,128)(2,1)S(1)}, u32[]{:S(2)}, u32[]{:S(2)}) collective-permute-start(bf16[208,2304]{1,0:T(8,128)(2,1)S(1)} %collective-permute-done.6.s2), channel_id=1, source_target_pairs={{0,16},{8,24},{16,0},{24,8},{1,17},{9,25},{17,1},{25,9},{2,18},{10... | collective-permute-start | bytes 2875400 | tf_op jit(solution)/shard_map/ppermute | solution.py:341
  79.0 9.2 %collective-permute-done.8.a2 = bf16[352,2304]{1,0:T(8,128)(2,1)S(1)} collective-permute-done((bf16[352,2304]{1,0:T(8,128)(2,1)}, bf16[352,2304]{1,0:T(8,128)(2,1)S(1)}, u32[]{:S(2)}, u32[]{:S(2)}) %collective-permute-start.8) | collective-permute-done | bytes 1622048 | tf_op jit(solution)/shard_map/ppermute | solution.py:341
  88.1 3.3 %partial_proj.1.acc = f32[768,768]{1,0:T(8,128)S(1)} custom-call(bf16[832,768]{1,0:T(8,128)(2,1)S(1)} %bitcast.18, bf16[768,768]{1,0:T(8,128)(2,1)S(1)} %bitcast.25, bf16[768,768]{1,0:T(8,128)(2,1)} %collective-permute-done.2.np_, bf16[768,768]{1,0:T(8,128)(2,1)} %collective-permute-done.4.fp, bf16[1536,208]{1,0:T(8,128)(2,1)S(1)} %get-tuple-element.50.refs_0_, ...), custom_call_target="tpu_custom_call" | custom-call | flops 9814671360 | bytes 70778880 | tf_op jit(solution)/shard_map/partial_proj/pallas_call | solution.py:24
  91.5 2.4 %early_rows.1 = (bf16[768,2304]{1,0:T(8,128)(2,1)}, f32[8,128]{1,0:T(8,128)}) custom-call(s32[1]{0:T(128)} %bitcast.side, f32[768,2304]{1,0:T(8,128)S(1)} %partial_qkv.1.acc, bf16[560,2304]{1,0:T(8,128)(2,1)S(1)} %collective-permute-done.11.f0, bf16[352,2304]{1,0:T(8,128)(2,1)S(1)} %collective-permute-done.8.a2, bf16[208,2304]{1,0:T(8,128)(2,1)S(1)} %collective-permute-done.6.s2), custom_call_target="tpu_custom_call" | custom-call | flops 5160960 | bytes 12902400 | tf_op jit(solution)/shard_map/early_rows/pallas_call | solution.py:24
  93.9 6.7 %collective-permute-done.9.s1 = bf16[768,768]{1,0:T(8,128)(2,1)S(1)} collective-permute-done((bf16[768,768]{1,0:T(8,128)(2,1)S(1)}, bf16[768,768]{1,0:T(8,128)(2,1)S(1)}, u32[]{:S(2)}, u32[]{:S(2)}) %collective-permute-start.9) | collective-permute-done | bytes 1179680 | tf_op jit(solution)/shard_map/ppermute | solution.py:341
  100.6 1.3 %final_proj.1 = bf16[768,768]{1,0:T(8,128)(2,1)} custom-call(f32[768,768]{1,0:T(8,128)S(1)} %partial_proj.1.acc, bf16[768,768]{1,0:T(8,128)(2,1)S(1)} %collective-permute-done.9.s1), custom_call_target="tpu_custom_call" | custom-call | flops 1179648 | bytes 4718592 | tf_op jit(solution)/shard_map/final_proj/pallas_call | solution.py:24
  101.9 6.0 %collective-permute-done.10.other = bf16[208,2304]{1,0:T(8,128)(2,1)S(1)} collective-permute-done((bf16[208,2304]{1,0:T(8,128)(2,1)S(1)}, bf16[208,2304]{1,0:T(8,128)(2,1)S(1)}, u32[]{:S(2)}, u32[]{:S(2)}) %collective-permute-start.10) | collective-permute-done | bytes 958496 | tf_op jit(solution)/shard_map/ppermute | solution.py:341
  107.8 0.6 collective-permute-done.7.f1
  108.4 1.1 %last_rows.1 = bf16[768,2304]{1,0:T(8,128)(2,1)} custom-call(s32[1]{0:T(128)} %bitcast.side, f32[768,2304]{1,0:T(8,128)S(1)} %partial_qkv.1.acc, bf16[208,2304]{1,0:T(8,128)(2,1)S(1)} %collective-permute-done.7.f1, bf16[208,2304]{1,0:T(8,128)(2,1)S(1)} %collective-permute-done.10.other, ...), custom_call_target="tpu_custom_call", output_to_operand_aliasing={{}: (4, {})} | custom-call | flops 1916928 | bytes 4792320 | tf_op jit(solution)/shard_map/last_rows/pallas_call | solution.py:24
  (37 shorter events, 1.8 us)
Async XLA Ops:
  0.6 26.7 %collective-permute-start = (bf16[768,2304]{1,0:T(8,128)(2,1)}, bf16[768,2304]{1,0:T(8,128)(2,1)}, u32[]{:S(2)}, u32[]{:S(2)}) collective-permute-start(bf16[768,2304]{1,0:T(8,128)(2,1)} %bitcast.13), channel_id=1, source_target_pairs={{0,1},{1,0},{2,3},{3,2},{4,5},{5,4},{6,7},{7,6},{8,9},{9,8},{10,11... | collective-permute-start | bytes 10616840 | tf_op jit(solution)/shard_map/ppermute | solution.py:341
  1.1 37.3 %collective-permute-start.4 = (bf16[768,768]{1,0:T(8,128)(2,1)}, bf16[768,768]{1,0:T(8,128)(2,1)}, u32[]{:S(2)}, u32[]{:S(2)}) collective-permute-start(bf16[768,768]{1,0:T(8,128)(2,1)} %bitcast.20), channel_id=1, source_target_pairs={{0,7},{1,2},{2,1},{3,4},{4,3},{5,6},{6,5},{7,0},{8,15},{9,10},{10,... | collective-permute-start | bytes 3538952 | tf_op jit(solution)/shard_map/ppermute | solution.py:341
  5.9 32.6 %collective-permute-start.3 = (bf16[768,768]{1,0:T(8,128)(2,1)}, bf16[768,768]{1,0:T(8,128)(2,1)}, u32[]{:S(2)}, u32[]{:S(2)}) collective-permute-start(bf16[768,768]{1,0:T(8,128)(2,1)} %bitcast.21), channel_id=1, source_target_pairs={{0,16},{8,24},{16,0},{24,8},{1,17},{9,25},{17,1},{25,9},{2,18},{10... | collective-permute-start | bytes 3538952 | tf_op jit(solution)/shard_map/ppermute | solution.py:341
  7.4 20.0 %collective-permute-start.2 = (bf16[768,768]{1,0:T(8,128)(2,1)}, bf16[768,768]{1,0:T(8,128)(2,1)}, u32[]{:S(2)}, u32[]{:S(2)}) collective-permute-start(bf16[768,768]{1,0:T(8,128)(2,1)} %bitcast.22), channel_id=1, source_target_pairs={{0,1},{1,0},{2,3},{3,2},{4,5},{5,4},{6,7},{7,6},{8,9},{9,8},{10,11... | collective-permute-start | bytes 3538952 | tf_op jit(solution)/shard_map/ppermute | solution.py:341
  7.4 2.0 %copy-start = (bf16[1,1,768,2304]{3,2,1,0:T(8,128)(2,1)S(1)}, bf16[1,1,768,2304]{3,2,1,0:T(8,128)(2,1)}, u32[]{:S(2)}) copy-start(bf16[1,1,768,2304]{3,2,1,0:T(8,128)(2,1)} %param.6) | copy-start | bytes 10616836
  9.4 2.9 %copy-start.12 = (bf16[1,1,4,197,768]{4,2,3,1,0:T(4,128)(2,1)S(1)}, bf16[1,1,4,197,768]{4,2,3,1,0:T(4,128)(2,1)}, u32[]{:S(2)}) copy-start(bf16[1,1,4,197,768]{4,2,3,1,0:T(4,128)(2,1)} %param.4) | copy-start | bytes 3631108
  10.7 1.7 %copy-start.13 = (bf16[1,1,4,197,768]{4,2,3,1,0:T(4,128)(2,1)S(1)}, bf16[1,1,4,197,768]{4,2,3,1,0:T(4,128)(2,1)}, u32[]{:S(2)}) copy-start(bf16[1,1,4,197,768]{4,2,3,1,0:T(4,128)(2,1)} %param.5) | copy-start | bytes 3631108
  10.7 38.2 %collective-permute-start.1 = (bf16[352,2304]{1,0:T(8,128)(2,1)}, bf16[352,2304]{1,0:T(8,128)(2,1)}, u32[]{:S(2)}, u32[]{:S(2)}) collective-permute-start(bf16[352,2304]{1,0:T(8,128)(2,1)} %first_rows.1), channel_id=1, source_target_pairs={{0,8},{8,0},{16,24},{24,16},{1,9},{9,1},{17,25},{25,17},{2,10},{10... | collective-permute-start | bytes 4866056 | tf_op jit(solution)/shard_map/ppermute | solution.py:341
  12.6 2.5 %copy-start.1 = (bf16[1,1,768,2304]{3,2,1,0:T(8,128)(2,1)S(1)}, bf16[1,1,768,2304]{3,2,1,0:T(8,128)(2,1)}, u32[]{:S(2)}) copy-start(bf16[1,1,768,2304]{3,2,1,0:T(8,128)(2,1)} %param.6) | copy-start | bytes 10616836
  12.7 2.7 %copy-start.6 = (bf16[1,1,768,768]{3,2,1,0:T(8,128)(2,1)S(1)}, bf16[1,1,768,768]{3,2,1,0:T(8,128)(2,1)}, u32[]{:S(2)}) copy-start(bf16[1,1,768,768]{3,2,1,0:T(8,128)(2,1)} %param.7) | copy-start | bytes 3538948
  12.8 8.6 %copy-start.4 = (bf16[4,208,768]{2,1,0:T(8,128)(2,1)}, bf16[4,208,768]{2,1,0:T(8,128)(2,1)S(1)}, u32[]{:S(2)}) copy-start(bf16[4,208,768]{2,1,0:T(8,128)(2,1)S(1)} %pad.8.clone) | copy-start | bytes 3833860
  21.4 1.1 %copy-start.2 = (bf16[768,832]{1,0:T(8,128)(2,1)}, bf16[768,832]{1,0:T(8,128)(2,1)S(1)}, u32[]{:S(2)}) copy-start(bf16[768,832]{1,0:T(8,128)(2,1)S(1)} %get-tuple-element.29.normed) | copy-start | bytes 3833860
  22.5 1.8 %copy-start.8 = (bf16[832,2304]{1,0:T(8,128)(2,1)}, bf16[832,2304]{1,0:T(8,128)(2,1)S(1)}, u32[]{:S(2)}) copy-start(bf16[832,2304]{1,0:T(8,128)(2,1)S(1)} %get-tuple-element.37.qkv) | copy-start | bytes 11501572
  24.3 1.1 %copy-start.10 = (bf16[832,768]{1,0:T(8,128)(2,1)}, bf16[832,768]{1,0:T(8,128)(2,1)S(1)}, u32[]{:S(2)}) copy-start(bf16[832,768]{1,0:T(8,128)(2,1)S(1)} %get-tuple-element.38.datt) | copy-start | bytes 3833860
  25.6 2.6 %copy-start.9 = (bf16[832,2304]{1,0:T(8,128)(2,1)S(1)}, bf16[832,2304]{1,0:T(8,128)(2,1)}, u32[]{:S(2)}) copy-start(bf16[832,2304]{1,0:T(8,128)(2,1)} %copy-done.8) | copy-start | bytes 11501572
  25.6 2.9 %copy-start.11 = (bf16[832,768]{1,0:T(8,128)(2,1)S(1)}, bf16[832,768]{1,0:T(8,128)(2,1)}, u32[]{:S(2)}) copy-start(bf16[832,768]{1,0:T(8,128)(2,1)} %copy-done.10) | copy-start | bytes 3833860
  27.4 26.0 %collective-permute-start.5 = (bf16[208,2304]{1,0:T(8,128)(2,1)S(1)}, bf16[208,2304]{1,0:T(8,128)(2,1)S(1)}, u32[]{:S(2)}, u32[]{:S(2)}) collective-permute-start(bf16[208,2304]{1,0:T(8,128)(2,1)S(1)} %get-tuple-element.48), channel_id=1, source_target_pairs={{0,16},{8,24},{16,0},{24,8},{1,17},{9,25},{17,1},{25,9},{2,18},{10... | collective-permute-start | bytes 2875400 | tf_op jit(solution)/shard_map/ppermute | solution.py:341
  27.9 63.5 %collective-permute-start.11 = (bf16[560,2304]{1,0:T(8,128)(2,1)S(1)}, bf16[560,2304]{1,0:T(8,128)(2,1)S(1)}, u32[]{:S(2)}, u32[]{:S(2)}) collective-permute-start(bf16[560,2304]{1,0:T(8,128)(2,1)S(1)} %pad_maximum_fusion), channel_id=1, source_target_pairs={{0,7},{1,2},{2,1},{3,4},{4,3},{5,6},{6,5},{7,0},{8,15},{9,10},{10,... | collective-permute-start | bytes 7741448 | tf_op jit(solution)/shard_map/ppermute | solution.py:341
  48.5 6.7 %copy-start.3 = (bf16[768,832]{1,0:T(8,128)(2,1)S(1)}, bf16[768,832]{1,0:T(8,128)(2,1)}, u32[]{:S(2)}) copy-start(bf16[768,832]{1,0:T(8,128)(2,1)} %copy-done.2) | copy-start | bytes 3833860
  49.0 39.1 %collective-permute-start.8 = (bf16[352,2304]{1,0:T(8,128)(2,1)}, bf16[352,2304]{1,0:T(8,128)(2,1)S(1)}, u32[]{:S(2)}, u32[]{:S(2)}) collective-permute-start(bf16[352,2304]{1,0:T(8,128)(2,1)} %collective-permute-done.1.a1), channel_id=1, source_target_pairs={{0,16},{8,24},{16,0},{24,8},{1,17},{9,25},{17,1},{25,9},{2,18},{10... | collective-permute-start | bytes 4866056 | tf_op jit(solution)/shard_map/ppermute | solution.py:341
  53.6 20.8 %collective-permute-start.6 = (bf16[208,2304]{1,0:T(8,128)(2,1)S(1)}, bf16[208,2304]{1,0:T(8,128)(2,1)S(1)}, u32[]{:S(2)}, u32[]{:S(2)}) collective-permute-start(bf16[208,2304]{1,0:T(8,128)(2,1)S(1)} %pair_sum.2), channel_id=1, source_target_pairs={{0,8},{8,0},{16,24},{24,16},{1,9},{9,1},{17,25},{25,17},{2,10},{10... | collective-permute-start | bytes 2875400 | tf_op jit(solution)/shard_map/ppermute | solution.py:341
  55.2 19.2 %copy-start.7 = (bf16[1,1,768,768]{3,2,1,0:T(8,128)(2,1)S(1)}, bf16[1,1,768,768]{3,2,1,0:T(8,128)(2,1)}, u32[]{:S(2)}) copy-start(bf16[1,1,768,768]{3,2,1,0:T(8,128)(2,1)} %param.7) | copy-start | bytes 3538948
  61.9 26.2 %copy-start.5 = (bf16[4,208,768]{2,1,0:T(8,128)(2,1)S(1)}, bf16[4,208,768]{2,1,0:T(8,128)(2,1)}, u32[]{:S(2)}) copy-start(bf16[4,208,768]{2,1,0:T(8,128)(2,1)} %copy-done.4) | copy-start | bytes 3833860
  75.9 24.6 %collective-permute-start.9 = (bf16[768,768]{1,0:T(8,128)(2,1)S(1)}, bf16[768,768]{1,0:T(8,128)(2,1)S(1)}, u32[]{:S(2)}, u32[]{:S(2)}) collective-permute-start(bf16[768,768]{1,0:T(8,128)(2,1)S(1)} %pair_sum.3), channel_id=1, source_target_pairs={{0,8},{8,0},{16,24},{24,16},{1,9},{9,1},{17,25},{25,17},{2,10},{10... | collective-permute-start | bytes 3538952 | tf_op jit(solution)/shard_map/ppermute | solution.py:341
  77.4 30.4 %collective-permute-start.10 = (bf16[208,2304]{1,0:T(8,128)(2,1)S(1)}, bf16[208,2304]{1,0:T(8,128)(2,1)S(1)}, u32[]{:S(2)}, u32[]{:S(2)}) collective-permute-start(bf16[208,2304]{1,0:T(8,128)(2,1)S(1)} %collective-permute-done.6.s2), channel_id=1, source_target_pairs={{0,16},{8,24},{16,0},{24,8},{1,17},{9,25},{17,1},{25,9},{2,18},{10... | collective-permute-start | bytes 2875400 | tf_op jit(solution)/shard_map/ppermute | solution.py:341
  79.0 29.5 %collective-permute-start.7 = (bf16[208,2304]{1,0:T(8,128)(2,1)S(1)}, bf16[208,2304]{1,0:T(8,128)(2,1)S(1)}, u32[]{:S(2)}, u32[]{:S(2)}) collective-permute-start(bf16[208,2304]{1,0:T(8,128)(2,1)S(1)} %get-tuple-element.48), channel_id=1, source_target_pairs={{0,7},{1,2},{2,1},{3,4},{4,3},{5,6},{6,5},{7,0},{8,15},{9,10},{10,... | collective-permute-start | bytes 2875400 | tf_op jit(solution)/shard_map/ppermute | solution.py:341

commit v5 on v4

--- a/solution.py
+++ b/solution.py
@@ -18,7 +18,7 @@
     return lax.dot_general(a, b, (((ca,), (cb,)), ((), ())), preferred_element_type=F32)
 
 
-def call(body, outs, operands, name, flops, moved, vmem, grid=None, in_specs=None, out_specs=None, scratch=(), exps=0, aliases=None, hint=1):
+def call(body, outs, operands, name, flops, moved, vmem, grid=None, in_specs=None, out_specs=None, scratch=(), exps=0, aliases=None):
     whole = pl.BlockSpec(memory_space=pltpu.VMEM)
     kwargs = {} if grid is None else {"grid": grid}
     return pl.pallas_call(
@@ -28,7 +28,7 @@
         out_shape=[jax.ShapeDtypeStruct(shape, dtype) for shape, dtype in outs],
         scratch_shapes=list(scratch),
         compiler_params=pltpu.CompilerParams(vmem_limit_bytes=vmem * MIB),
-        cost_estimate=pl.CostEstimate(flops=int(flops * hint), bytes_accessed=int(moved * hint), transcendentals=int(exps * hint)),
+        cost_estimate=pl.CostEstimate(flops=flops, bytes_accessed=moved, transcendentals=exps),
         input_output_aliases=aliases or {},
         name=name,
         **kwargs,
@@ -123,7 +123,7 @@
     lax.fori_loop(0, heads // pack, group, 0, unroll=unroll)
 
 
-def attention(qkv, datt, first, count, rows, length, heads, hint=1, unroll=6):
+def attention(qkv, datt, first, count, rows, length, heads, unroll=6):
     width = datt.shape[1]
     here = lambda b: (b + first, 0)
     there = lambda b: (b, 0)
@@ -139,16 +139,15 @@
         in_specs=[pl.BlockSpec((rows, 3 * width), here), pl.BlockSpec((rows, width), here)],
         out_specs=[pl.BlockSpec((width, rows), there), pl.BlockSpec((rows, 3 * width), there)],
         exps=count * heads * rows * rows,
-        hint=hint,
     )
 
 
-def partial_body(parts, normed, wq, nq, a1, *refs):
+def partial_body(parts, normed, wq, n0, n1, a1, *refs):
     dqkv, acc = refs[:parts], refs[parts]
     rows, wide = wq.shape
     width = wide // 3
     scale = width**-0.5
-    for first, last in ((0, a1.shape[0]), (a1.shape[0], rows)):
+    for near_rows, first, last in ((n0, 0, a1.shape[0]), (n1, a1.shape[0], rows)):
         part = slice(first, last)
         for c in range(0, wide, width):
             cols = slice(c, c + width)
@@ -156,19 +155,19 @@
             for d in dqkv:
                 grad = grad + mm(normed[part, at : at + d.shape[0]], d[:, cols], 1, 0)
                 at += d.shape[0]
-            total = wq[part, cols].astype(F32) + nq[part, cols].astype(F32)
+            total = wq[part, cols].astype(F32) + near_rows[:, cols].astype(F32)
             if first == 0:
                 total = total + a1[:, cols].astype(F32)
             acc[part, cols] = total * 0.2 - LR * (grad * scale)
 
 
-def partial_qkv(normed, dqkv, wq, nq, a1):
+def partial_qkv(normed, dqkv, wq, n0, n1, a1):
     width, total = normed.shape
     wide = wq.shape[1]
     return call(
         functools.partial(partial_body, len(dqkv)),
         [(wq.shape, F32)],
-        (normed, wq, nq, a1, *dqkv),
+        (normed, wq, n0, n1, a1, *dqkv),
         "partial_qkv",
         flops=2 * total * width * wide,
         moved=12 * width * wide,
@@ -176,10 +175,11 @@
     )[0]
 
 
-def partial_proj_body(parts, cot, wp, np_, fp, *refs):
+def partial_proj_body(parts, cot, wp, np0, np1, fp, *refs):
     att, acc = refs[:parts], refs[parts]
     scale = wp.shape[0] ** -0.5
-    total = wp[...].astype(F32) + np_[...].astype(F32) + fp[...].astype(F32)
+    near_rows = jnp.concatenate([np0[...], np1[...]], axis=0)
+    total = wp[...].astype(F32) + near_rows.astype(F32) + fp[...].astype(F32)
     rows, width = att[0].shape[1], wp.shape[1]
     at, grad = 0, 0.0
     for a in att:
@@ -189,17 +189,16 @@
     acc[...] = total * 0.2 - LR * (grad * scale)
 
 
-def partial_proj(cot, att, wp, np_, fp):
+def partial_proj(cot, att, wp, np0, np1, fp):
     total, width = cot.shape
     return call(
         functools.partial(partial_proj_body, len(att)),
         [(wp.shape, F32)],
-        (cot, wp, np_, fp, *att),
+        (cot, wp, np0, np1, fp, *att),
         "partial_proj",
         flops=2 * total * width * width,
         moved=12 * width * width,
         vmem=16,
-        hint=10,
     )[0]
 
 
@@ -399,31 +398,32 @@
     b1 = permute(wp, "rx", opposite)
     fp = permute(wp, "ry", far)
     a1 = permute(top, "rx", near)
-    nq = permute(wq, "ry", near)
-    np_ = permute(wp, "ry", near)
     normed, qkv, datt = project(tokens, cot, wq, wp, rows)
 
     most = jnp.concatenate([top, kept], axis=0)
-    most, sent, qkv, datt = after((most, sent, qkv, datt), nq, np_)
     b2 = permute(sent, "rx", opposite)
     f0 = permute(most, "ry", far)
     att0, dqkv0 = attention(qkv, datt, 0, half, rows, length, HEADS)
 
-    b1, fp = after((b1, fp), att0)
-    qkv, datt = after((qkv, datt), b1, fp)
+    fp, b1 = after((fp, b1), att0)
+    qkv, datt, top2, low = after((qkv, datt, top, wq[cut:]), fp, b1)
+    n0 = permute(top2, "ry", near)
+    n1 = permute(low, "ry", near)
     att1, dqkv1 = attention(qkv, datt, half, images - half, rows, length, HEADS)
 
     a1, b2 = after(a1, att1), after(b2, att1)
     a2 = permute(a1, "rx", opposite)
     pair2 = pair_sum(kept, b2)
     s2 = permute(pair2, "rx", near)
-    dqkv0, dqkv1 = after((dqkv0, dqkv1), pair2)
-    acc = partial_qkv(normed, (dqkv0, dqkv1), wq, nq, a1)
-    s2 = after(s2, acc)
+    wp_top, wp_low = after((wp[: width // 2], wp[width // 2 :]), a2, f0)
+    np_ = (permute(wp_top, "ry", near), permute(wp_low, "ry", near))
+    s2 = after(s2, n0, n1)
+    dqkv0, dqkv1 = after((dqkv0, dqkv1), s2)
+    acc = partial_qkv(normed, (dqkv0, dqkv1), wq, n0, n1, a1)
     other = permute(s2, "rx", opposite)
     pair1 = pair_sum(wp, after(b1, s2))
     s1 = permute(pair1, "rx", near)
-    acc_p = partial_proj(cot, after((att0, att1), pair1, a2), wp, np_, fp)
+    acc_p = partial_proj(cot, after((att0, att1), pair1), wp, *np_, fp)
     f1 = permute(after(sent, s2), "ry", far)
     side = side.reshape(1)
     early, token = early_rows(side, acc, f0, a2, s2)

time: 110 us -> 109 us (level)
  waiting for transfers between devices: 39.2 us -> 49 us
  Pallas kernels: 43.9 us -> 37.3 us
  local copies, waits for them, and re-layouts: 9.8 us -> 5.11 us
    ppermute x12 -> x14, waiting for transfers between devices: 39.2 us -> 49 us  [permute(): return lax.ppermute(block, axis, [(i, partner(i, n)) for i in range(n)])]
    pallas_call x11, Pallas kernels: 43.9 us -> 37.3 us  [call(): pl.pallas_call(body, in_specs=in_specs or [whole] * len(operands), out_sp...]
    unnamed x30 -> x10, local copies, waits for them, and re-layouts: 9.5 us -> 2.99 us
    dynamic_slice x1, local copies, waits for them, and re-layouts: 0.13 us -> 1.76 us  [local(): sent = lax.dynamic_slice_in_dim(wq, cut + (1 - side) * part, part)]
    ppermute x12 -> x14, starting transfers between devices: 14.1 us -> 15.1 us  [permute(): return lax.ppermute(block, axis, [(i, partner(i, n)) for i in range(n)])]
  transfers between devices with their start and end apart: 12 -> 14, of which waited for: 7 -> 9; matrix products, arithmetic and copies ran while one was open for 2% -> 4% of each run, Pallas kernels for 39% -> 33%
where the time goes in v5:
time: 109 us
  waiting for transfers between devices  49 us (45%)
  Pallas kernels  37.3 us (34%)
  starting transfers between devices  15.1 us (14%)
  local copies, waits for them, and re-layouts  5.11 us (5%)
  other arithmetic  1.64 us (2%)
    ppermute x14, waiting for transfers between devices, permute(): return lax.ppermute(block, axis, [(i, partner(i, n)) for i in range(n)])  49 us
    pallas_call x11, Pallas kernels, call(): pl.pallas_call(body, in_specs=in_specs or [whole] * len(operands), out_sp...  37.3 us
    ppermute x14, starting transfers between devices, permute(): return lax.ppermute(block, axis, [(i, partner(i, n)) for i in range(n)])  15.1 us
    unnamed x10, local copies, waits for them, and re-layouts  2.99 us
  transfers between devices with their start and end apart: 14, of which 9 were waited for; matrix products, arithmetic and copies ran while one was open for 4% of the time, Pallas kernels for 33%

profile of v5, /device:TPU:0, one launch (start us, length us, event | category | flops | bytes accessed | tf_op | source)
XLA Modules:
  0.0 109.1 jit_solution(16071005359095250799)
XLA Ops:
  0.6 4.6 %collective-permute-start = (bf16[768,768]{1,0:T(8,128)(2,1)}, bf16[768,768]{1,0:T(8,128)(2,1)S(1)}, u32[]{:S(2)}, u32[]{:S(2)}) collective-permute-start(bf16[768,768]{1,0:T(8,128)(2,1)} %bitcast.22), channel_id=1, source_target_pairs={{0,7},{1,2},{2,1},{3,4},{4,3},{5,6},{6,5},{7,0},{8,15},{9,10},{10,... | collective-permute-start | bytes 3538952 | tf_op jit(solution)/shard_map/ppermute | solution.py:340
  5.2 1.5 %collective-permute-start.1 = (bf16[768,768]{1,0:T(8,128)(2,1)}, bf16[768,768]{1,0:T(8,128)(2,1)S(1)}, u32[]{:S(2)}, u32[]{:S(2)}) collective-permute-start(bf16[768,768]{1,0:T(8,128)(2,1)} %bitcast.23), channel_id=1, source_target_pairs={{0,16},{8,24},{16,0},{24,8},{1,17},{9,25},{17,1},{25,9},{2,18},{10... | collective-permute-start | bytes 3538952 | tf_op jit(solution)/shard_map/ppermute | solution.py:340
  6.7 1.8 %dynamic-slice_bitcast_fusion = (bf16[208,2304]{1,0:T(8,128)(2,1)S(1)}, bf16[208,2304]{1,0:T(8,128)(2,1)S(1)}) fusion(bf16[1,1,768,2304]{3,2,1,0:T(8,128)(2,1)} %param.6, s32[]{:T(128)S(6)} %select_n.13, s32[]{:T(128)S(6)} %select_n.12), kind=kLoop, calls=%fused_computation.2 | loop fusion | bytes 3833864 | tf_op jit(solution)/shard_map/dynamic_slice | solution.py:396
  8.5 0.6 collective-permute-start.5
  9.5 1.6 %collective-permute-start.4 = (bf16[352,2304]{1,0:T(8,128)(2,1)S(1)}, bf16[352,2304]{1,0:T(8,128)(2,1)S(1)}, u32[]{:S(2)}, u32[]{:S(2)}) collective-permute-start(bf16[352,2304]{1,0:T(8,128)(2,1)S(1)} %first_rows.1), channel_id=1, source_target_pairs={{0,8},{8,0},{16,24},{24,16},{1,9},{9,1},{17,25},{25,17},{2,10},{10... | collective-permute-start | bytes 4866056 | tf_op jit(solution)/shard_map/ppermute | solution.py:340
  11.0 1.6 %pad_maximum_fusion = bf16[560,2304]{1,0:T(8,128)(2,1)} fusion(bf16[208,2304]{1,0:T(8,128)(2,1)S(1)} %get-tuple-element.57.a, bf16[352,2304]{1,0:T(8,128)(2,1)S(1)} %first_rows.1), kind=kLoop, calls=%fused_computation | loop fusion | flops 5160960 | bytes 5160960 | tf_op jit(solution)/shard_map/concatenate | solution.py:403
  12.8 1.1 %copy-done.2 = bf16[1,1,4,197,768]{4,2,3,1,0:T(4,128)(2,1)S(1)} copy-done((bf16[1,1,4,197,768]{4,2,3,1,0:T(4,128)(2,1)S(1)}, bf16[1,1,4,197,768]{4,2,3,1,0:T(4,128)(2,1)}, u32[]{:S(2)}) %copy-start.2) | copy-done | bytes 1210392
  14.1 0.3 copy-done.3
  14.7 1.1 copy-done.1
  15.8 6.0 %project.1 = (bf16[768,832]{1,0:T(8,128)(2,1)S(1)}, bf16[832,2304]{1,0:T(8,128)(2,1)S(1)}, bf16[832,768]{1,0:T(8,128)(2,1)S(1)}) custom-call(bf16[832,768]{1,0:T(8,128)(2,1)S(1)} %bitcast.29, bf16[832,768]{1,0:T(8,128)(2,1)S(1)} %bitcast.27, bf16[768,2304]{1,0:T(8,128)(2,1)S(1)} %bitcast.20, bf16[768,768]{1,0:T(8,128)(2,1)S(1)} %bitcast.24), custom_call_target="tpu_custom_call" | custom-call | flops 3925868544 | bytes 14942208 | tf_op jit(solution)/shard_map/project/pallas_call | solution.py:24
  21.7 9.9 %attention.2 = (bf16[1536,208]{1,0:T(8,128)(2,1)S(1)}, bf16[416,2304]{1,0:T(8,128)(2,1)S(1)}) custom-call(bf16[832,2304]{1,0:T(8,128)(2,1)S(1)} %get-tuple-element.37.qkv, bf16[832,768]{1,0:T(8,128)(2,1)S(1)} %get-tuple-element.38.datt), custom_call_target="tpu_custom_call" | custom-call | flops 3925868544 | bytes 5111808 | tf_op jit(solution)/shard_map/attention/pallas_call | solution.py:24
  31.9 2.4 %collective-permute-done.1.b = bf16[768,768]{1,0:T(8,128)(2,1)S(1)} collective-permute-done((bf16[768,768]{1,0:T(8,128)(2,1)}, bf16[768,768]{1,0:T(8,128)(2,1)S(1)}, u32[]{:S(2)}, u32[]{:S(2)}) %collective-permute-start.1) | collective-permute-done | bytes 1179680 | tf_op jit(solution)/shard_map/ppermute | solution.py:340
  34.3 0.5 collective-permute-start.2
  34.8 10.1 %attention.3 = (bf16[1536,208]{1,0:T(8,128)(2,1)S(1)}, bf16[416,2304]{1,0:T(8,128)(2,1)S(1)}) custom-call(bf16[832,2304]{1,0:T(8,128)(2,1)S(1)} %get-tuple-element.37.qkv, bf16[832,768]{1,0:T(8,128)(2,1)S(1)} %get-tuple-element.38.datt), custom_call_target="tpu_custom_call" | custom-call | flops 3925868544 | bytes 5111808 | tf_op jit(solution)/shard_map/attention/pallas_call | solution.py:24
  44.9 0.4 collective-permute-done.4.a1
  45.3 1.2 %collective-permute-start.8 = (bf16[352,2304]{1,0:T(8,128)(2,1)S(1)}, bf16[352,2304]{1,0:T(8,128)(2,1)S(1)}, u32[]{:S(2)}, u32[]{:S(2)}) collective-permute-start(bf16[352,2304]{1,0:T(8,128)(2,1)S(1)} %collective-permute-done.4.a1), channel_id=1, source_target_pairs={{0,16},{8,24},{16,0},{24,8},{1,17},{9,25},{17,1},{25,9},{2,18},{10... | collective-permute-start | bytes 4866056 | tf_op jit(solution)/shard_map/ppermute | solution.py:340
  46.5 8.4 %collective-permute-done.5.b = bf16[208,2304]{1,0:T(8,128)(2,1)S(1)} collective-permute-done((bf16[208,2304]{1,0:T(8,128)(2,1)S(1)}, bf16[208,2304]{1,0:T(8,128)(2,1)S(1)}, u32[]{:S(2)}, u32[]{:S(2)}) %collective-permute-start.5) | collective-permute-done | bytes 958496 | tf_op jit(solution)/shard_map/ppermute | solution.py:340
  55.1 1.6 %collective-permute-start.6 = (bf16[208,2304]{1,0:T(8,128)(2,1)S(1)}, bf16[208,2304]{1,0:T(8,128)(2,1)S(1)}, u32[]{:S(2)}, u32[]{:S(2)}) collective-permute-start(bf16[208,2304]{1,0:T(8,128)(2,1)S(1)} %pair_sum.2), channel_id=1, source_target_pairs={{0,8},{8,0},{16,24},{24,16},{1,9},{9,1},{17,25},{25,17},{2,10},{10... | collective-permute-start | bytes 2875400 | tf_op jit(solution)/shard_map/ppermute | solution.py:340
  56.6 19.6 %collective-permute-done.6.s2 = bf16[208,2304]{1,0:T(8,128)(2,1)S(1)} collective-permute-done((bf16[208,2304]{1,0:T(8,128)(2,1)S(1)}, bf16[208,2304]{1,0:T(8,128)(2,1)S(1)}, u32[]{:S(2)}, u32[]{:S(2)}) %collective-permute-start.6) | collective-permute-done | bytes 958496 | tf_op jit(solution)/shard_map/ppermute | solution.py:340
  76.2 0.3 pair_sum.3
  76.5 1.6 %collective-permute-start.12 = (bf16[768,768]{1,0:T(8,128)(2,1)S(1)}, bf16[768,768]{1,0:T(8,128)(2,1)S(1)}, u32[]{:S(2)}, u32[]{:S(2)}) collective-permute-start(bf16[768,768]{1,0:T(8,128)(2,1)S(1)} %pair_sum.3), channel_id=1, source_target_pairs={{0,8},{8,0},{16,24},{24,16},{1,9},{9,1},{17,25},{25,17},{2,10},{10... | collective-permute-start | bytes 3538952 | tf_op jit(solution)/shard_map/ppermute | solution.py:340
  78.0 1.5 %collective-permute-start.13 = (bf16[208,2304]{1,0:T(8,128)(2,1)S(1)}, bf16[208,2304]{1,0:T(8,128)(2,1)S(1)}, u32[]{:S(2)}, u32[]{:S(2)}) collective-permute-start(bf16[208,2304]{1,0:T(8,128)(2,1)S(1)} %collective-permute-done.6.s2), channel_id=1, source_target_pairs={{0,16},{8,24},{16,0},{24,8},{1,17},{9,25},{17,1},{25,9},{2,18},{10... | collective-permute-start | bytes 2875400 | tf_op jit(solution)/shard_map/ppermute | solution.py:340
  79.6 7.6 %collective-permute-done.9.f0 = bf16[560,2304]{1,0:T(8,128)(2,1)S(1)} collective-permute-done((bf16[560,2304]{1,0:T(8,128)(2,1)}, bf16[560,2304]{1,0:T(8,128)(2,1)S(1)}, u32[]{:S(2)}, u32[]{:S(2)}) %collective-permute-start.9) | collective-permute-done | bytes 2580512 | tf_op jit(solution)/shard_map/ppermute | solution.py:340
  87.2 2.4 %collective-permute-done.8.a2 = bf16[352,2304]{1,0:T(8,128)(2,1)S(1)} collective-permute-done((bf16[352,2304]{1,0:T(8,128)(2,1)S(1)}, bf16[352,2304]{1,0:T(8,128)(2,1)S(1)}, u32[]{:S(2)}, u32[]{:S(2)}) %collective-permute-start.8) | collective-permute-done | bytes 1622048 | tf_op jit(solution)/shard_map/ppermute | solution.py:340
  89.6 0.5 collective-permute-start.11
  90.1 4.2 %partial_qkv.1.acc = f32[768,2304]{1,0:T(8,128)S(1)} custom-call(bf16[768,832]{1,0:T(8,128)(2,1)S(1)} %get-tuple-element.29.normed, bf16[768,2304]{1,0:T(8,128)(2,1)S(1)} %bitcast.21, bf16[352,2304]{1,0:T(8,128)(2,1)S(1)} %collective-permute-done.2.n0, bf16[416,2304]{1,0:T(8,128)(2,1)S(1)} %collective-permute-done.3.n1, ...), custom_call_target="tpu_custom_call" | custom-call | flops 2944401408 | bytes 21233664 | tf_op jit(solution)/shard_map/partial_qkv/pallas_call | solution.py:24
  94.4 2.3 %early_rows.1 = (bf16[768,2304]{1,0:T(8,128)(2,1)}, f32[8,128]{1,0:T(8,128)}) custom-call(s32[1]{0:T(128)} %bitcast.side, f32[768,2304]{1,0:T(8,128)S(1)} %partial_qkv.1.acc, bf16[560,2304]{1,0:T(8,128)(2,1)S(1)} %collective-permute-done.9.f0, bf16[352,2304]{1,0:T(8,128)(2,1)S(1)} %collective-permute-done.8.a2, bf16[208,2304]{1,0:T(8,128)(2,1)S(1)} %collective-permute-done.6.s2), custom_call_target="tpu_custom_call" | custom-call | flops 5160960 | bytes 12902400 | tf_op jit(solution)/shard_map/early_rows/pallas_call | solution.py:24
  96.7 1.7 %partial_proj.1.acc = f32[768,768]{1,0:T(8,128)S(1)} custom-call(bf16[832,768]{1,0:T(8,128)(2,1)S(1)} %bitcast.28, bf16[768,768]{1,0:T(8,128)(2,1)S(1)} %bitcast.26, bf16[384,768]{1,0:T(8,128)(2,1)S(1)} %collective-permute-done.10.np0, bf16[384,768]{1,0:T(8,128)(2,1)S(1)} %collective-permute-done.11.np1, bf16[768,768]{1,0:T(8,128)(2,1)S(1)} %collective-permute-done.fp, ...), custom_call_target="tpu_custom_call" | custom-call | flops 981467136 | bytes 7077888 | tf_op jit(solution)/shard_map/partial_proj/pallas_call | solution.py:24
  98.4 0.4 collective-permute-done.12.s1
  98.9 1.3 %final_proj.1 = bf16[768,768]{1,0:T(8,128)(2,1)} custom-call(f32[768,768]{1,0:T(8,128)S(1)} %partial_proj.1.acc, bf16[768,768]{1,0:T(8,128)(2,1)S(1)} %collective-permute-done.12.s1), custom_call_target="tpu_custom_call" | custom-call | flops 1179648 | bytes 4718592 | tf_op jit(solution)/shard_map/final_proj/pallas_call | solution.py:24
  100.2 7.6 %collective-permute-done.13.other = bf16[208,2304]{1,0:T(8,128)(2,1)S(1)} collective-permute-done((bf16[208,2304]{1,0:T(8,128)(2,1)S(1)}, bf16[208,2304]{1,0:T(8,128)(2,1)S(1)}, u32[]{:S(2)}, u32[]{:S(2)}) %collective-permute-start.13) | collective-permute-done | bytes 958496 | tf_op jit(solution)/shard_map/ppermute | solution.py:340
  107.8 1.1 %last_rows.1 = bf16[768,2304]{1,0:T(8,128)(2,1)} custom-call(s32[1]{0:T(128)} %bitcast.side, f32[768,2304]{1,0:T(8,128)S(1)} %partial_qkv.1.acc, bf16[208,2304]{1,0:T(8,128)(2,1)S(1)} %collective-permute-done.7.f1, bf16[208,2304]{1,0:T(8,128)(2,1)S(1)} %collective-permute-done.13.other, ...), custom_call_target="tpu_custom_call", output_to_operand_aliasing={{}: (4, {})} | custom-call | flops 1916928 | bytes 4792320 | tf_op jit(solution)/shard_map/last_rows/pallas_call | solution.py:24
  (23 shorter events, 1.6 us)
Async XLA Ops:
  0.6 31.3 %collective-permute-start = (bf16[768,768]{1,0:T(8,128)(2,1)}, bf16[768,768]{1,0:T(8,128)(2,1)S(1)}, u32[]{:S(2)}, u32[]{:S(2)}) collective-permute-start(bf16[768,768]{1,0:T(8,128)(2,1)} %bitcast.22), channel_id=1, source_target_pairs={{0,7},{1,2},{2,1},{3,4},{4,3},{5,6},{6,5},{7,0},{8,15},{9,10},{10,... | collective-permute-start | bytes 3538952 | tf_op jit(solution)/shard_map/ppermute | solution.py:340
  5.2 29.1 %collective-permute-start.1 = (bf16[768,768]{1,0:T(8,128)(2,1)}, bf16[768,768]{1,0:T(8,128)(2,1)S(1)}, u32[]{:S(2)}, u32[]{:S(2)}) collective-permute-start(bf16[768,768]{1,0:T(8,128)(2,1)} %bitcast.23), channel_id=1, source_target_pairs={{0,16},{8,24},{16,0},{24,8},{1,17},{9,25},{17,1},{25,9},{2,18},{10... | collective-permute-start | bytes 3538952 | tf_op jit(solution)/shard_map/ppermute | solution.py:340
  6.7 2.6 %copy-start = (bf16[1,1,768,2304]{3,2,1,0:T(8,128)(2,1)S(1)}, bf16[1,1,768,2304]{3,2,1,0:T(8,128)(2,1)}, u32[]{:S(2)}) copy-start(bf16[1,1,768,2304]{3,2,1,0:T(8,128)(2,1)} %param.6) | copy-start | bytes 10616836
  8.5 46.4 %collective-permute-start.5 = (bf16[208,2304]{1,0:T(8,128)(2,1)S(1)}, bf16[208,2304]{1,0:T(8,128)(2,1)S(1)}, u32[]{:S(2)}, u32[]{:S(2)}) collective-permute-start(bf16[208,2304]{1,0:T(8,128)(2,1)S(1)} %get-tuple-element.47), channel_id=1, source_target_pairs={{0,16},{8,24},{16,0},{24,8},{1,17},{9,25},{17,1},{25,9},{2,18},{10... | collective-permute-start | bytes 2875400 | tf_op jit(solution)/shard_map/ppermute | solution.py:340
  9.5 35.8 %collective-permute-start.4 = (bf16[352,2304]{1,0:T(8,128)(2,1)S(1)}, bf16[352,2304]{1,0:T(8,128)(2,1)S(1)}, u32[]{:S(2)}, u32[]{:S(2)}) collective-permute-start(bf16[352,2304]{1,0:T(8,128)(2,1)S(1)} %first_rows.1), channel_id=1, source_target_pairs={{0,8},{8,0},{16,24},{24,16},{1,9},{9,1},{17,25},{25,17},{2,10},{10... | collective-permute-start | bytes 4866056 | tf_op jit(solution)/shard_map/ppermute | solution.py:340
  12.7 1.3 %copy-start.2 = (bf16[1,1,4,197,768]{4,2,3,1,0:T(4,128)(2,1)S(1)}, bf16[1,1,4,197,768]{4,2,3,1,0:T(4,128)(2,1)}, u32[]{:S(2)}) copy-start(bf16[1,1,4,197,768]{4,2,3,1,0:T(4,128)(2,1)} %param.5) | copy-start | bytes 3631108
  12.7 74.5 %collective-permute-start.9 = (bf16[560,2304]{1,0:T(8,128)(2,1)}, bf16[560,2304]{1,0:T(8,128)(2,1)S(1)}, u32[]{:S(2)}, u32[]{:S(2)}) collective-permute-start(bf16[560,2304]{1,0:T(8,128)(2,1)} %pad_maximum_fusion), channel_id=1, source_target_pairs={{0,7},{1,2},{2,1},{3,4},{4,3},{5,6},{6,5},{7,0},{8,15},{9,10},{10,... | collective-permute-start | bytes 7741448 | tf_op jit(solution)/shard_map/ppermute | solution.py:340
  12.8 1.5 %copy-start.3 = (bf16[1,1,4,197,768]{4,2,3,1,0:T(4,128)(2,1)S(1)}, bf16[1,1,4,197,768]{4,2,3,1,0:T(4,128)(2,1)}, u32[]{:S(2)}) copy-start(bf16[1,1,4,197,768]{4,2,3,1,0:T(4,128)(2,1)} %param.4) | copy-start | bytes 3631108
  14.5 1.3 %copy-start.1 = (bf16[1,1,768,768]{3,2,1,0:T(8,128)(2,1)S(1)}, bf16[1,1,768,768]{3,2,1,0:T(8,128)(2,1)}, u32[]{:S(2)}) copy-start(bf16[1,1,768,768]{3,2,1,0:T(8,128)(2,1)} %param.7) | copy-start | bytes 3538948
  34.3 41.9 %collective-permute-start.3 = (bf16[416,2304]{1,0:T(8,128)(2,1)S(1)}, bf16[416,2304]{1,0:T(8,128)(2,1)S(1)}, u32[]{:S(2)}, u32[]{:S(2)}) collective-permute-start(bf16[416,2304]{1,0:T(8,128)(2,1)S(1)} %slice_bitcast_fusion), channel_id=1, source_target_pairs={{0,1},{1,0},{2,3},{3,2},{4,5},{5,4},{6,7},{7,6},{8,9},{9,8},{10,11... | collective-permute-start | bytes 5750792 | tf_op jit(solution)/shard_map/ppermute | solution.py:340
  34.3 41.9 %collective-permute-start.2 = (bf16[352,2304]{1,0:T(8,128)(2,1)S(1)}, bf16[352,2304]{1,0:T(8,128)(2,1)S(1)}, u32[]{:S(2)}, u32[]{:S(2)}) collective-permute-start(bf16[352,2304]{1,0:T(8,128)(2,1)S(1)} %first_rows.1), channel_id=1, source_target_pairs={{0,1},{1,0},{2,3},{3,2},{4,5},{5,4},{6,7},{7,6},{8,9},{9,8},{10,11... | collective-permute-start | bytes 4866056 | tf_op jit(solution)/shard_map/ppermute | solution.py:340
  45.3 44.3 %collective-permute-start.8 = (bf16[352,2304]{1,0:T(8,128)(2,1)S(1)}, bf16[352,2304]{1,0:T(8,128)(2,1)S(1)}, u32[]{:S(2)}, u32[]{:S(2)}) collective-permute-start(bf16[352,2304]{1,0:T(8,128)(2,1)S(1)} %collective-permute-done.4.a1), channel_id=1, source_target_pairs={{0,16},{8,24},{16,0},{24,8},{1,17},{9,25},{17,1},{25,9},{2,18},{10... | collective-permute-start | bytes 4866056 | tf_op jit(solution)/shard_map/ppermute | solution.py:340
  55.1 21.1 %collective-permute-start.6 = (bf16[208,2304]{1,0:T(8,128)(2,1)S(1)}, bf16[208,2304]{1,0:T(8,128)(2,1)S(1)}, u32[]{:S(2)}, u32[]{:S(2)}) collective-permute-start(bf16[208,2304]{1,0:T(8,128)(2,1)S(1)} %pair_sum.2), channel_id=1, source_target_pairs={{0,8},{8,0},{16,24},{24,16},{1,9},{9,1},{17,25},{25,17},{2,10},{10... | collective-permute-start | bytes 2875400 | tf_op jit(solution)/shard_map/ppermute | solution.py:340
  76.5 22.4 %collective-permute-start.12 = (bf16[768,768]{1,0:T(8,128)(2,1)S(1)}, bf16[768,768]{1,0:T(8,128)(2,1)S(1)}, u32[]{:S(2)}, u32[]{:S(2)}) collective-permute-start(bf16[768,768]{1,0:T(8,128)(2,1)S(1)} %pair_sum.3), channel_id=1, source_target_pairs={{0,8},{8,0},{16,24},{24,16},{1,9},{9,1},{17,25},{25,17},{2,10},{10... | collective-permute-start | bytes 3538952 | tf_op jit(solution)/shard_map/ppermute | solution.py:340
  78.0 29.7 %collective-permute-start.13 = (bf16[208,2304]{1,0:T(8,128)(2,1)S(1)}, bf16[208,2304]{1,0:T(8,128)(2,1)S(1)}, u32[]{:S(2)}, u32[]{:S(2)}) collective-permute-start(bf16[208,2304]{1,0:T(8,128)(2,1)S(1)} %collective-permute-done.6.s2), channel_id=1, source_target_pairs={{0,16},{8,24},{16,0},{24,8},{1,17},{9,25},{17,1},{25,9},{2,18},{10... | collective-permute-start | bytes 2875400 | tf_op jit(solution)/shard_map/ppermute | solution.py:340
  79.5 28.2 %collective-permute-start.7 = (bf16[208,2304]{1,0:T(8,128)(2,1)S(1)}, bf16[208,2304]{1,0:T(8,128)(2,1)S(1)}, u32[]{:S(2)}, u32[]{:S(2)}) collective-permute-start(bf16[208,2304]{1,0:T(8,128)(2,1)S(1)} %get-tuple-element.47), channel_id=1, source_target_pairs={{0,7},{1,2},{2,1},{3,4},{4,3},{5,6},{6,5},{7,0},{8,15},{9,10},{10,... | collective-permute-start | bytes 2875400 | tf_op jit(solution)/shard_map/ppermute | solution.py:340
  89.6 7.1 %collective-permute-start.10 = (bf16[384,768]{1,0:T(8,128)(2,1)S(1)}, bf16[384,768]{1,0:T(8,128)(2,1)S(1)}, u32[]{:S(2)}, u32[]{:S(2)}) collective-permute-start(bf16[384,768]{1,0:T(8,128)(2,1)S(1)} %get-tuple-element.48), channel_id=1, source_target_pairs={{0,1},{1,0},{2,3},{3,2},{4,5},{5,4},{6,7},{7,6},{8,9},{9,8},{10,11... | collective-permute-start | bytes 1769480 | tf_op jit(solution)/shard_map/ppermute | solution.py:340
  89.6 7.1 %collective-permute-start.11 = (bf16[384,768]{1,0:T(8,128)(2,1)S(1)}, bf16[384,768]{1,0:T(8,128)(2,1)S(1)}, u32[]{:S(2)}, u32[]{:S(2)}) collective-permute-start(bf16[384,768]{1,0:T(8,128)(2,1)S(1)} %get-tuple-element.49), channel_id=1, source_target_pairs={{0,1},{1,0},{2,3},{3,2},{4,5},{5,4},{6,7},{7,6},{8,9},{9,8},{10,11... | collective-permute-start | bytes 1769480 | tf_op jit(solution)/shard_map/ppermute | solution.py:340

commit v6 on v5

--- a/solution.py
+++ b/solution.py
@@ -219,7 +219,7 @@
 
 
 def chunks(first, last):
-    steps = max(1, (last - first) // 96)
+    steps = max(1, (last - first) // 48)
     cuts = [first + (last - first) * k // steps // 16 * 16 for k in range(steps)] + [last]
     return list(zip(cuts, cuts[1:]))
 
@@ -389,7 +389,7 @@
         gp = jnp.einsum("bdt,bte->de", att.reshape(images, width, rows), cot.reshape(images, rows, width), preferred_element_type=F32) * scale
         return plain_average(wq, gq)[None, None], plain_average(wp, gp)[None, None]
 
-    cut = width * 11 // 24
+    cut = width // 2
     part = (width - cut) // 2
     side = lax.axis_index("rx") // 2
     top = first_rows(wq, cut)

time: 109 us -> 109 us (level)
  transfers between devices with their start and end apart: 14 -> 14, of which waited for: 9 -> 8; matrix products, arithmetic and copies ran while one was open for 4% -> 4% of each run, Pallas kernels for 33% -> 33%
where the time goes in v6:
time: 109 us
  waiting for transfers between devices  49.4 us (45%)
  Pallas kernels  37.1 us (34%)
  starting transfers between devices  15 us (14%)
  local copies, waits for them, and re-layouts  4.87 us (4%)
  other arithmetic  1.67 us (2%)
    ppermute x14, waiting for transfers between devices, permute(): return lax.ppermute(block, axis, [(i, partner(i, n)) for i in range(n)])  49.4 us
    pallas_call x11, Pallas kernels, call(): pl.pallas_call(body, in_specs=in_specs or [whole] * len(operands), out_sp...  37.1 us
    ppermute x14, starting transfers between devices, permute(): return lax.ppermute(block, axis, [(i, partner(i, n)) for i in range(n)])  15 us
    unnamed x10, local copies, waits for them, and re-layouts  2.81 us
  transfers between devices with their start and end apart: 14, of which 8 were waited for; matrix products, arithmetic and copies ran while one was open for 4% of the time, Pallas kernels for 33%

profile of v6, /device:TPU:0, one launch (start us, length us, event | category | flops | bytes accessed | tf_op | source)
XLA Modules:
  0.0 109.0 jit_solution(3862614572793032744)
XLA Ops:
  0.6 4.6 %collective-permute-start = (bf16[768,768]{1,0:T(8,128)(2,1)}, bf16[768,768]{1,0:T(8,128)(2,1)S(1)}, u32[]{:S(2)}, u32[]{:S(2)}) collective-permute-start(bf16[768,768]{1,0:T(8,128)(2,1)} %bitcast.22), channel_id=1, source_target_pairs={{0,7},{1,2},{2,1},{3,4},{4,3},{5,6},{6,5},{7,0},{8,15},{9,10},{10,... | collective-permute-start | bytes 3538952 | tf_op jit(solution)/shard_map/ppermute | solution.py:340
  5.2 1.5 %collective-permute-start.1 = (bf16[768,768]{1,0:T(8,128)(2,1)}, bf16[768,768]{1,0:T(8,128)(2,1)S(1)}, u32[]{:S(2)}, u32[]{:S(2)}) collective-permute-start(bf16[768,768]{1,0:T(8,128)(2,1)} %bitcast.23), channel_id=1, source_target_pairs={{0,16},{8,24},{16,0},{24,8},{1,17},{9,25},{17,1},{25,9},{2,18},{10... | collective-permute-start | bytes 3538952 | tf_op jit(solution)/shard_map/ppermute | solution.py:340
  6.7 1.7 %dynamic-slice_bitcast_fusion = (bf16[192,2304]{1,0:T(8,128)(2,1)S(1)}, bf16[192,2304]{1,0:T(8,128)(2,1)S(1)}) fusion(bf16[1,1,768,2304]{3,2,1,0:T(8,128)(2,1)} %param.6, s32[]{:T(128)S(6)} %select_n.13, s32[]{:T(128)S(6)} %select_n.12), kind=kLoop, calls=%fused_computation.2 | loop fusion | bytes 3538952 | tf_op jit(solution)/shard_map/dynamic_slice | solution.py:396
  8.4 0.6 collective-permute-start.5
  9.2 0.4 first_rows.1
  9.6 1.6 %collective-permute-start.4 = (bf16[384,2304]{1,0:T(8,128)(2,1)S(1)}, bf16[384,2304]{1,0:T(8,128)(2,1)S(1)}, u32[]{:S(2)}, u32[]{:S(2)}) collective-permute-start(bf16[384,2304]{1,0:T(8,128)(2,1)S(1)} %first_rows.1), channel_id=1, source_target_pairs={{0,8},{8,0},{16,24},{24,16},{1,9},{9,1},{17,25},{25,17},{2,10},{10... | collective-permute-start | bytes 5308424 | tf_op jit(solution)/shard_map/ppermute | solution.py:340
  11.2 1.7 %pad_maximum_fusion = bf16[576,2304]{1,0:T(8,128)(2,1)} fusion(bf16[192,2304]{1,0:T(8,128)(2,1)S(1)} %get-tuple-element.57.a, bf16[384,2304]{1,0:T(8,128)(2,1)S(1)} %first_rows.1), kind=kLoop, calls=%fused_computation | loop fusion | flops 5308416 | bytes 5308416 | tf_op jit(solution)/shard_map/concatenate | solution.py:403
  13.0 1.1 %copy-done.3 = bf16[1,1,4,197,768]{4,2,3,1,0:T(4,128)(2,1)S(1)} copy-done((bf16[1,1,4,197,768]{4,2,3,1,0:T(4,128)(2,1)S(1)}, bf16[1,1,4,197,768]{4,2,3,1,0:T(4,128)(2,1)}, u32[]{:S(2)}) %copy-start.3) | copy-done | bytes 1210392
  14.6 1.1 %copy-done.1 = bf16[1,1,768,768]{3,2,1,0:T(8,128)(2,1)S(1)} copy-done((bf16[1,1,768,768]{3,2,1,0:T(8,128)(2,1)S(1)}, bf16[1,1,768,768]{3,2,1,0:T(8,128)(2,1)}, u32[]{:S(2)}) %copy-start.1) | copy-done | bytes 1179672
  15.7 6.0 %project.1 = (bf16[768,832]{1,0:T(8,128)(2,1)S(1)}, bf16[832,2304]{1,0:T(8,128)(2,1)S(1)}, bf16[832,768]{1,0:T(8,128)(2,1)S(1)}) custom-call(bf16[832,768]{1,0:T(8,128)(2,1)S(1)} %bitcast.29, bf16[832,768]{1,0:T(8,128)(2,1)S(1)} %bitcast.27, bf16[768,2304]{1,0:T(8,128)(2,1)S(1)} %bitcast.20, bf16[768,768]{1,0:T(8,128)(2,1)S(1)} %bitcast.24), custom_call_target="tpu_custom_call" | custom-call | flops 3925868544 | bytes 14942208 | tf_op jit(solution)/shard_map/project/pallas_call | solution.py:24
  21.7 9.9 %attention.2 = (bf16[1536,208]{1,0:T(8,128)(2,1)S(1)}, bf16[416,2304]{1,0:T(8,128)(2,1)S(1)}) custom-call(bf16[832,2304]{1,0:T(8,128)(2,1)S(1)} %get-tuple-element.37.qkv, bf16[832,768]{1,0:T(8,128)(2,1)S(1)} %get-tuple-element.38.datt), custom_call_target="tpu_custom_call" | custom-call | flops 3925868544 | bytes 5111808 | tf_op jit(solution)/shard_map/attention/pallas_call | solution.py:24
  31.6 0.3 collective-permute-done.fp
  31.9 2.4 %collective-permute-done.1.b = bf16[768,768]{1,0:T(8,128)(2,1)S(1)} collective-permute-done((bf16[768,768]{1,0:T(8,128)(2,1)}, bf16[768,768]{1,0:T(8,128)(2,1)S(1)}, u32[]{:S(2)}, u32[]{:S(2)}) %collective-permute-start.1) | collective-permute-done | bytes 1179680 | tf_op jit(solution)/shard_map/ppermute | solution.py:340
  34.3 0.5 collective-permute-start.3
  34.8 10.1 %attention.3 = (bf16[1536,208]{1,0:T(8,128)(2,1)S(1)}, bf16[416,2304]{1,0:T(8,128)(2,1)S(1)}) custom-call(bf16[832,2304]{1,0:T(8,128)(2,1)S(1)} %get-tuple-element.37.qkv, bf16[832,768]{1,0:T(8,128)(2,1)S(1)} %get-tuple-element.38.datt), custom_call_target="tpu_custom_call" | custom-call | flops 3925868544 | bytes 5111808 | tf_op jit(solution)/shard_map/attention/pallas_call | solution.py:24
  44.9 3.7 %collective-permute-done.4.a1 = bf16[384,2304]{1,0:T(8,128)(2,1)S(1)} collective-permute-done((bf16[384,2304]{1,0:T(8,128)(2,1)S(1)}, bf16[384,2304]{1,0:T(8,128)(2,1)S(1)}, u32[]{:S(2)}, u32[]{:S(2)}) %collective-permute-start.4) | collective-permute-done | bytes 1769504 | tf_op jit(solution)/shard_map/ppermute | solution.py:340
  48.6 1.0 collective-permute-start.8
  49.6 3.5 %collective-permute-done.5.b = bf16[192,2304]{1,0:T(8,128)(2,1)S(1)} collective-permute-done((bf16[192,2304]{1,0:T(8,128)(2,1)S(1)}, bf16[192,2304]{1,0:T(8,128)(2,1)S(1)}, u32[]{:S(2)}, u32[]{:S(2)}) %collective-permute-start.5) | collective-permute-done | bytes 884768 | tf_op jit(solution)/shard_map/ppermute | solution.py:340
  53.3 1.6 %collective-permute-start.6 = (bf16[192,2304]{1,0:T(8,128)(2,1)S(1)}, bf16[192,2304]{1,0:T(8,128)(2,1)S(1)}, u32[]{:S(2)}, u32[]{:S(2)}) collective-permute-start(bf16[192,2304]{1,0:T(8,128)(2,1)S(1)} %pair_sum.2), channel_id=1, source_target_pairs={{0,8},{8,0},{16,24},{24,16},{1,9},{9,1},{17,25},{25,17},{2,10},{10... | collective-permute-start | bytes 2654216 | tf_op jit(solution)/shard_map/ppermute | solution.py:340
  54.8 18.0 %collective-permute-done.6.s2 = bf16[192,2304]{1,0:T(8,128)(2,1)S(1)} collective-permute-done((bf16[192,2304]{1,0:T(8,128)(2,1)S(1)}, bf16[192,2304]{1,0:T(8,128)(2,1)S(1)}, u32[]{:S(2)}, u32[]{:S(2)}) %collective-permute-start.6) | collective-permute-done | bytes 884768 | tf_op jit(solution)/shard_map/ppermute | solution.py:340
  72.8 0.3 pair_sum.3
  73.1 1.6 %collective-permute-start.12 = (bf16[768,768]{1,0:T(8,128)(2,1)S(1)}, bf16[768,768]{1,0:T(8,128)(2,1)S(1)}, u32[]{:S(2)}, u32[]{:S(2)}) collective-permute-start(bf16[768,768]{1,0:T(8,128)(2,1)S(1)} %pair_sum.3), channel_id=1, source_target_pairs={{0,8},{8,0},{16,24},{24,16},{1,9},{9,1},{17,25},{25,17},{2,10},{10... | collective-permute-start | bytes 3538952 | tf_op jit(solution)/shard_map/ppermute | solution.py:340
  74.6 1.7 %collective-permute-start.13 = (bf16[192,2304]{1,0:T(8,128)(2,1)S(1)}, bf16[192,2304]{1,0:T(8,128)(2,1)S(1)}, u32[]{:S(2)}, u32[]{:S(2)}) collective-permute-start(bf16[192,2304]{1,0:T(8,128)(2,1)S(1)} %collective-permute-done.6.s2), channel_id=1, source_target_pairs={{0,16},{8,24},{16,0},{24,8},{1,17},{9,25},{17,1},{25,9},{2,18},{10... | collective-permute-start | bytes 2654216 | tf_op jit(solution)/shard_map/ppermute | solution.py:340
  76.4 12.4 %collective-permute-done.9.f0 = bf16[576,2304]{1,0:T(8,128)(2,1)S(1)} collective-permute-done((bf16[576,2304]{1,0:T(8,128)(2,1)}, bf16[576,2304]{1,0:T(8,128)(2,1)S(1)}, u32[]{:S(2)}, u32[]{:S(2)}) %collective-permute-start.9) | collective-permute-done | bytes 2654240 | tf_op jit(solution)/shard_map/ppermute | solution.py:340
  88.8 2.2 %collective-permute-done.8.a2 = bf16[384,2304]{1,0:T(8,128)(2,1)S(1)} collective-permute-done((bf16[384,2304]{1,0:T(8,128)(2,1)S(1)}, bf16[384,2304]{1,0:T(8,128)(2,1)S(1)}, u32[]{:S(2)}, u32[]{:S(2)}) %collective-permute-start.8) | collective-permute-done | bytes 1769504 | tf_op jit(solution)/shard_map/ppermute | solution.py:340
  91.0 0.5 collective-permute-start.11
  91.5 4.0 %partial_qkv.1.acc = f32[768,2304]{1,0:T(8,128)S(1)} custom-call(bf16[768,832]{1,0:T(8,128)(2,1)S(1)} %get-tuple-element.29.normed, bf16[768,2304]{1,0:T(8,128)(2,1)S(1)} %bitcast.21, bf16[384,2304]{1,0:T(8,128)(2,1)S(1)} %collective-permute-done.2.n0, bf16[384,2304]{1,0:T(8,128)(2,1)S(1)} %collective-permute-done.3.n1, ...), custom_call_target="tpu_custom_call" | custom-call | flops 2944401408 | bytes 21233664 | tf_op jit(solution)/shard_map/partial_qkv/pallas_call | solution.py:24
  95.5 2.3 %early_rows.1 = (bf16[768,2304]{1,0:T(8,128)(2,1)}, f32[8,128]{1,0:T(8,128)}) custom-call(s32[1]{0:T(128)} %bitcast.side, f32[768,2304]{1,0:T(8,128)S(1)} %partial_qkv.1.acc, bf16[576,2304]{1,0:T(8,128)(2,1)S(1)} %collective-permute-done.9.f0, bf16[384,2304]{1,0:T(8,128)(2,1)S(1)} %collective-permute-done.8.a2, bf16[192,2304]{1,0:T(8,128)(2,1)S(1)} %collective-permute-done.6.s2), custom_call_target="tpu_custom_call" | custom-call | flops 5308416 | bytes 13271040 | tf_op jit(solution)/shard_map/early_rows/pallas_call | solution.py:24
  97.9 1.6 %partial_proj.1.acc = f32[768,768]{1,0:T(8,128)S(1)} custom-call(bf16[832,768]{1,0:T(8,128)(2,1)S(1)} %bitcast.28, bf16[768,768]{1,0:T(8,128)(2,1)S(1)} %bitcast.26, bf16[384,768]{1,0:T(8,128)(2,1)S(1)} %collective-permute-done.10.np0, bf16[384,768]{1,0:T(8,128)(2,1)S(1)} %collective-permute-done.11.np1, bf16[768,768]{1,0:T(8,128)(2,1)S(1)} %collective-permute-done.fp, ...), custom_call_target="tpu_custom_call" | custom-call | flops 981467136 | bytes 7077888 | tf_op jit(solution)/shard_map/partial_proj/pallas_call | solution.py:24
  99.5 1.3 %final_proj.1 = bf16[768,768]{1,0:T(8,128)(2,1)} custom-call(f32[768,768]{1,0:T(8,128)S(1)} %partial_proj.1.acc, bf16[768,768]{1,0:T(8,128)(2,1)S(1)} %collective-permute-done.12.s1), custom_call_target="tpu_custom_call" | custom-call | flops 1179648 | bytes 4718592 | tf_op jit(solution)/shard_map/final_proj/pallas_call | solution.py:24
  100.8 7.0 %collective-permute-done.13.other = bf16[192,2304]{1,0:T(8,128)(2,1)S(1)} collective-permute-done((bf16[192,2304]{1,0:T(8,128)(2,1)S(1)}, bf16[192,2304]{1,0:T(8,128)(2,1)S(1)}, u32[]{:S(2)}, u32[]{:S(2)}) %collective-permute-start.13) | collective-permute-done | bytes 884768 | tf_op jit(solution)/shard_map/ppermute | solution.py:340
  107.8 1.0 last_rows.1
  (23 shorter events, 1.1 us)
Async XLA Ops:
  0.6 31.3 %collective-permute-start = (bf16[768,768]{1,0:T(8,128)(2,1)}, bf16[768,768]{1,0:T(8,128)(2,1)S(1)}, u32[]{:S(2)}, u32[]{:S(2)}) collective-permute-start(bf16[768,768]{1,0:T(8,128)(2,1)} %bitcast.22), channel_id=1, source_target_pairs={{0,7},{1,2},{2,1},{3,4},{4,3},{5,6},{6,5},{7,0},{8,15},{9,10},{10,... | collective-permute-start | bytes 3538952 | tf_op jit(solution)/shard_map/ppermute | solution.py:340
  5.2 29.1 %collective-permute-start.1 = (bf16[768,768]{1,0:T(8,128)(2,1)}, bf16[768,768]{1,0:T(8,128)(2,1)S(1)}, u32[]{:S(2)}, u32[]{:S(2)}) collective-permute-start(bf16[768,768]{1,0:T(8,128)(2,1)} %bitcast.23), channel_id=1, source_target_pairs={{0,16},{8,24},{16,0},{24,8},{1,17},{9,25},{17,1},{25,9},{2,18},{10... | collective-permute-start | bytes 3538952 | tf_op jit(solution)/shard_map/ppermute | solution.py:340
  6.7 2.5 %copy-start = (bf16[1,1,768,2304]{3,2,1,0:T(8,128)(2,1)S(1)}, bf16[1,1,768,2304]{3,2,1,0:T(8,128)(2,1)}, u32[]{:S(2)}) copy-start(bf16[1,1,768,2304]{3,2,1,0:T(8,128)(2,1)} %param.6) | copy-start | bytes 10616836
  8.4 44.7 %collective-permute-start.5 = (bf16[192,2304]{1,0:T(8,128)(2,1)S(1)}, bf16[192,2304]{1,0:T(8,128)(2,1)S(1)}, u32[]{:S(2)}, u32[]{:S(2)}) collective-permute-start(bf16[192,2304]{1,0:T(8,128)(2,1)S(1)} %get-tuple-element.47), channel_id=1, source_target_pairs={{0,16},{8,24},{16,0},{24,8},{1,17},{9,25},{17,1},{25,9},{2,18},{10... | collective-permute-start | bytes 2654216 | tf_op jit(solution)/shard_map/ppermute | solution.py:340
  9.6 38.9 %collective-permute-start.4 = (bf16[384,2304]{1,0:T(8,128)(2,1)S(1)}, bf16[384,2304]{1,0:T(8,128)(2,1)S(1)}, u32[]{:S(2)}, u32[]{:S(2)}) collective-permute-start(bf16[384,2304]{1,0:T(8,128)(2,1)S(1)} %first_rows.1), channel_id=1, source_target_pairs={{0,8},{8,0},{16,24},{24,16},{1,9},{9,1},{17,25},{25,17},{2,10},{10... | collective-permute-start | bytes 5308424 | tf_op jit(solution)/shard_map/ppermute | solution.py:340
  11.2 1.7 %copy-start.2 = (bf16[1,1,4,197,768]{4,2,3,1,0:T(4,128)(2,1)S(1)}, bf16[1,1,4,197,768]{4,2,3,1,0:T(4,128)(2,1)}, u32[]{:S(2)}) copy-start(bf16[1,1,4,197,768]{4,2,3,1,0:T(4,128)(2,1)} %param.5) | copy-start | bytes 3631108
  12.9 1.3 %copy-start.3 = (bf16[1,1,4,197,768]{4,2,3,1,0:T(4,128)(2,1)S(1)}, bf16[1,1,4,197,768]{4,2,3,1,0:T(4,128)(2,1)}, u32[]{:S(2)}) copy-start(bf16[1,1,4,197,768]{4,2,3,1,0:T(4,128)(2,1)} %param.4) | copy-start | bytes 3631108
  12.9 75.9 %collective-permute-start.9 = (bf16[576,2304]{1,0:T(8,128)(2,1)}, bf16[576,2304]{1,0:T(8,128)(2,1)S(1)}, u32[]{:S(2)}, u32[]{:S(2)}) collective-permute-start(bf16[576,2304]{1,0:T(8,128)(2,1)} %pad_maximum_fusion), channel_id=1, source_target_pairs={{0,7},{1,2},{2,1},{3,4},{4,3},{5,6},{6,5},{7,0},{8,15},{9,10},{10,... | collective-permute-start | bytes 7962632 | tf_op jit(solution)/shard_map/ppermute | solution.py:340
  14.5 1.3 %copy-start.1 = (bf16[1,1,768,768]{3,2,1,0:T(8,128)(2,1)S(1)}, bf16[1,1,768,768]{3,2,1,0:T(8,128)(2,1)}, u32[]{:S(2)}) copy-start(bf16[1,1,768,768]{3,2,1,0:T(8,128)(2,1)} %param.7) | copy-start | bytes 3538948
  34.3 38.5 %collective-permute-start.2 = (bf16[384,2304]{1,0:T(8,128)(2,1)S(1)}, bf16[384,2304]{1,0:T(8,128)(2,1)S(1)}, u32[]{:S(2)}, u32[]{:S(2)}) collective-permute-start(bf16[384,2304]{1,0:T(8,128)(2,1)S(1)} %first_rows.1), channel_id=1, source_target_pairs={{0,1},{1,0},{2,3},{3,2},{4,5},{5,4},{6,7},{7,6},{8,9},{9,8},{10,11... | collective-permute-start | bytes 5308424 | tf_op jit(solution)/shard_map/ppermute | solution.py:340
  34.3 38.5 %collective-permute-start.3 = (bf16[384,2304]{1,0:T(8,128)(2,1)S(1)}, bf16[384,2304]{1,0:T(8,128)(2,1)S(1)}, u32[]{:S(2)}, u32[]{:S(2)}) collective-permute-start(bf16[384,2304]{1,0:T(8,128)(2,1)S(1)} %slice_bitcast_fusion), channel_id=1, source_target_pairs={{0,1},{1,0},{2,3},{3,2},{4,5},{5,4},{6,7},{7,6},{8,9},{9,8},{10,11... | collective-permute-start | bytes 5308424 | tf_op jit(solution)/shard_map/ppermute | solution.py:340
  48.6 42.4 %collective-permute-start.8 = (bf16[384,2304]{1,0:T(8,128)(2,1)S(1)}, bf16[384,2304]{1,0:T(8,128)(2,1)S(1)}, u32[]{:S(2)}, u32[]{:S(2)}) collective-permute-start(bf16[384,2304]{1,0:T(8,128)(2,1)S(1)} %collective-permute-done.4.a1), channel_id=1, source_target_pairs={{0,16},{8,24},{16,0},{24,8},{1,17},{9,25},{17,1},{25,9},{2,18},{10... | collective-permute-start | bytes 5308424 | tf_op jit(solution)/shard_map/ppermute | solution.py:340
  53.3 19.5 %collective-permute-start.6 = (bf16[192,2304]{1,0:T(8,128)(2,1)S(1)}, bf16[192,2304]{1,0:T(8,128)(2,1)S(1)}, u32[]{:S(2)}, u32[]{:S(2)}) collective-permute-start(bf16[192,2304]{1,0:T(8,128)(2,1)S(1)} %pair_sum.2), channel_id=1, source_target_pairs={{0,8},{8,0},{16,24},{24,16},{1,9},{9,1},{17,25},{25,17},{2,10},{10... | collective-permute-start | bytes 2654216 | tf_op jit(solution)/shard_map/ppermute | solution.py:340
  73.1 26.4 %collective-permute-start.12 = (bf16[768,768]{1,0:T(8,128)(2,1)S(1)}, bf16[768,768]{1,0:T(8,128)(2,1)S(1)}, u32[]{:S(2)}, u32[]{:S(2)}) collective-permute-start(bf16[768,768]{1,0:T(8,128)(2,1)S(1)} %pair_sum.3), channel_id=1, source_target_pairs={{0,8},{8,0},{16,24},{24,16},{1,9},{9,1},{17,25},{25,17},{2,10},{10... | collective-permute-start | bytes 3538952 | tf_op jit(solution)/shard_map/ppermute | solution.py:340
  74.6 33.1 %collective-permute-start.13 = (bf16[192,2304]{1,0:T(8,128)(2,1)S(1)}, bf16[192,2304]{1,0:T(8,128)(2,1)S(1)}, u32[]{:S(2)}, u32[]{:S(2)}) collective-permute-start(bf16[192,2304]{1,0:T(8,128)(2,1)S(1)} %collective-permute-done.6.s2), channel_id=1, source_target_pairs={{0,16},{8,24},{16,0},{24,8},{1,17},{9,25},{17,1},{25,9},{2,18},{10... | collective-permute-start | bytes 2654216 | tf_op jit(solution)/shard_map/ppermute | solution.py:340
  76.4 31.4 %collective-permute-start.7 = (bf16[192,2304]{1,0:T(8,128)(2,1)S(1)}, bf16[192,2304]{1,0:T(8,128)(2,1)S(1)}, u32[]{:S(2)}, u32[]{:S(2)}) collective-permute-start(bf16[192,2304]{1,0:T(8,128)(2,1)S(1)} %get-tuple-element.47), channel_id=1, source_target_pairs={{0,7},{1,2},{2,1},{3,4},{4,3},{5,6},{6,5},{7,0},{8,15},{9,10},{10,... | collective-permute-start | bytes 2654216 | tf_op jit(solution)/shard_map/ppermute | solution.py:340
  91.0 6.8 %collective-permute-start.10 = (bf16[384,768]{1,0:T(8,128)(2,1)S(1)}, bf16[384,768]{1,0:T(8,128)(2,1)S(1)}, u32[]{:S(2)}, u32[]{:S(2)}) collective-permute-start(bf16[384,768]{1,0:T(8,128)(2,1)S(1)} %get-tuple-element.48), channel_id=1, source_target_pairs={{0,1},{1,0},{2,3},{3,2},{4,5},{5,4},{6,7},{7,6},{8,9},{9,8},{10,11... | collective-permute-start | bytes 1769480 | tf_op jit(solution)/shard_map/ppermute | solution.py:340
  91.0 6.9 %collective-permute-start.11 = (bf16[384,768]{1,0:T(8,128)(2,1)S(1)}, bf16[384,768]{1,0:T(8,128)(2,1)S(1)}, u32[]{:S(2)}, u32[]{:S(2)}) collective-permute-start(bf16[384,768]{1,0:T(8,128)(2,1)S(1)} %get-tuple-element.49), channel_id=1, source_target_pairs={{0,1},{1,0},{2,3},{3,2},{4,5},{5,4},{6,7},{7,6},{8,9},{9,8},{10,11... | collective-permute-start | bytes 1769480 | tf_op jit(solution)/shard_map/ppermute | solution.py:340

commit v7 on v6

--- a/solution.py
+++ b/solution.py
@@ -219,7 +219,7 @@
 
 
 def chunks(first, last):
-    steps = max(1, (last - first) // 48)
+    steps = max(1, (last - first) // 32)
     cuts = [first + (last - first) * k // steps // 16 * 16 for k in range(steps)] + [last]
     return list(zip(cuts, cuts[1:]))
 

time: 109 us -> 109 us (level)
  no operation moved by 1% of the time
where the time goes in v7:
time: 109 us
  waiting for transfers between devices  49.4 us (45%)
  Pallas kernels  37.1 us (34%)
  starting transfers between devices  15 us (14%)
  local copies, waits for them, and re-layouts  4.87 us (4%)
  other arithmetic  1.67 us (2%)
    ppermute x14, waiting for transfers between devices, permute(): return lax.ppermute(block, axis, [(i, partner(i, n)) for i in range(n)])  49.4 us
    pallas_call x11, Pallas kernels, call(): pl.pallas_call(body, in_specs=in_specs or [whole] * len(operands), out_sp...  37.1 us
    ppermute x14, starting transfers between devices, permute(): return lax.ppermute(block, axis, [(i, partner(i, n)) for i in range(n)])  15 us
    unnamed x10, local copies, waits for them, and re-layouts  2.81 us
  transfers between devices with their start and end apart: 14, of which 8 were waited for; matrix products, arithmetic and copies ran while one was open for 4% of the time, Pallas kernels for 33%

profile of v7, /device:TPU:0, one launch (start us, length us, event | category | flops | bytes accessed | tf_op | source)
XLA Modules:
  0.0 109.0 jit_solution(2910231983290916661)
XLA Ops:
  0.6 4.6 %collective-permute-start = (bf16[768,768]{1,0:T(8,128)(2,1)}, bf16[768,768]{1,0:T(8,128)(2,1)S(1)}, u32[]{:S(2)}, u32[]{:S(2)}) collective-permute-start(bf16[768,768]{1,0:T(8,128)(2,1)} %bitcast.22), channel_id=1, source_target_pairs={{0,7},{1,2},{2,1},{3,4},{4,3},{5,6},{6,5},{7,0},{8,15},{9,10},{10,... | collective-permute-start | bytes 3538952 | tf_op jit(solution)/shard_map/ppermute | solution.py:340
  5.2 1.5 %collective-permute-start.1 = (bf16[768,768]{1,0:T(8,128)(2,1)}, bf16[768,768]{1,0:T(8,128)(2,1)S(1)}, u32[]{:S(2)}, u32[]{:S(2)}) collective-permute-start(bf16[768,768]{1,0:T(8,128)(2,1)} %bitcast.23), channel_id=1, source_target_pairs={{0,16},{8,24},{16,0},{24,8},{1,17},{9,25},{17,1},{25,9},{2,18},{10... | collective-permute-start | bytes 3538952 | tf_op jit(solution)/shard_map/ppermute | solution.py:340
  6.7 1.7 %dynamic-slice_bitcast_fusion = (bf16[192,2304]{1,0:T(8,128)(2,1)S(1)}, bf16[192,2304]{1,0:T(8,128)(2,1)S(1)}) fusion(bf16[1,1,768,2304]{3,2,1,0:T(8,128)(2,1)} %param.6, s32[]{:T(128)S(6)} %select_n.13, s32[]{:T(128)S(6)} %select_n.12), kind=kLoop, calls=%fused_computation.2 | loop fusion | bytes 3538952 | tf_op jit(solution)/shard_map/dynamic_slice | solution.py:396
  8.4 0.6 collective-permute-start.5
  9.2 0.4 first_rows.1
  9.6 1.6 %collective-permute-start.4 = (bf16[384,2304]{1,0:T(8,128)(2,1)S(1)}, bf16[384,2304]{1,0:T(8,128)(2,1)S(1)}, u32[]{:S(2)}, u32[]{:S(2)}) collective-permute-start(bf16[384,2304]{1,0:T(8,128)(2,1)S(1)} %first_rows.1), channel_id=1, source_target_pairs={{0,8},{8,0},{16,24},{24,16},{1,9},{9,1},{17,25},{25,17},{2,10},{10... | collective-permute-start | bytes 5308424 | tf_op jit(solution)/shard_map/ppermute | solution.py:340
  11.2 1.7 %pad_maximum_fusion = bf16[576,2304]{1,0:T(8,128)(2,1)} fusion(bf16[192,2304]{1,0:T(8,128)(2,1)S(1)} %get-tuple-element.57.a, bf16[384,2304]{1,0:T(8,128)(2,1)S(1)} %first_rows.1), kind=kLoop, calls=%fused_computation | loop fusion | flops 5308416 | bytes 5308416 | tf_op jit(solution)/shard_map/concatenate | solution.py:403
  13.0 1.1 %copy-done.3 = bf16[1,1,4,197,768]{4,2,3,1,0:T(4,128)(2,1)S(1)} copy-done((bf16[1,1,4,197,768]{4,2,3,1,0:T(4,128)(2,1)S(1)}, bf16[1,1,4,197,768]{4,2,3,1,0:T(4,128)(2,1)}, u32[]{:S(2)}) %copy-start.3) | copy-done | bytes 1210392
  14.6 1.1 %copy-done.1 = bf16[1,1,768,768]{3,2,1,0:T(8,128)(2,1)S(1)} copy-done((bf16[1,1,768,768]{3,2,1,0:T(8,128)(2,1)S(1)}, bf16[1,1,768,768]{3,2,1,0:T(8,128)(2,1)}, u32[]{:S(2)}) %copy-start.1) | copy-done | bytes 1179672
  15.7 6.0 %project.1 = (bf16[768,832]{1,0:T(8,128)(2,1)S(1)}, bf16[832,2304]{1,0:T(8,128)(2,1)S(1)}, bf16[832,768]{1,0:T(8,128)(2,1)S(1)}) custom-call(bf16[832,768]{1,0:T(8,128)(2,1)S(1)} %bitcast.29, bf16[832,768]{1,0:T(8,128)(2,1)S(1)} %bitcast.27, bf16[768,2304]{1,0:T(8,128)(2,1)S(1)} %bitcast.20, bf16[768,768]{1,0:T(8,128)(2,1)S(1)} %bitcast.24), custom_call_target="tpu_custom_call" | custom-call | flops 3925868544 | bytes 14942208 | tf_op jit(solution)/shard_map/project/pallas_call | solution.py:24
  21.7 9.9 %attention.2 = (bf16[1536,208]{1,0:T(8,128)(2,1)S(1)}, bf16[416,2304]{1,0:T(8,128)(2,1)S(1)}) custom-call(bf16[832,2304]{1,0:T(8,128)(2,1)S(1)} %get-tuple-element.37.qkv, bf16[832,768]{1,0:T(8,128)(2,1)S(1)} %get-tuple-element.38.datt), custom_call_target="tpu_custom_call" | custom-call | flops 3925868544 | bytes 5111808 | tf_op jit(solution)/shard_map/attention/pallas_call | solution.py:24
  31.6 0.3 collective-permute-done.fp
  31.9 2.4 %collective-permute-done.1.b = bf16[768,768]{1,0:T(8,128)(2,1)S(1)} collective-permute-done((bf16[768,768]{1,0:T(8,128)(2,1)}, bf16[768,768]{1,0:T(8,128)(2,1)S(1)}, u32[]{:S(2)}, u32[]{:S(2)}) %collective-permute-start.1) | collective-permute-done | bytes 1179680 | tf_op jit(solution)/shard_map/ppermute | solution.py:340
  34.3 0.5 collective-permute-start.3
  34.8 10.1 %attention.3 = (bf16[1536,208]{1,0:T(8,128)(2,1)S(1)}, bf16[416,2304]{1,0:T(8,128)(2,1)S(1)}) custom-call(bf16[832,2304]{1,0:T(8,128)(2,1)S(1)} %get-tuple-element.37.qkv, bf16[832,768]{1,0:T(8,128)(2,1)S(1)} %get-tuple-element.38.datt), custom_call_target="tpu_custom_call" | custom-call | flops 3925868544 | bytes 5111808 | tf_op jit(solution)/shard_map/attention/pallas_call | solution.py:24
  44.9 3.7 %collective-permute-done.4.a1 = bf16[384,2304]{1,0:T(8,128)(2,1)S(1)} collective-permute-done((bf16[384,2304]{1,0:T(8,128)(2,1)S(1)}, bf16[384,2304]{1,0:T(8,128)(2,1)S(1)}, u32[]{:S(2)}, u32[]{:S(2)}) %collective-permute-start.4) | collective-permute-done | bytes 1769504 | tf_op jit(solution)/shard_map/ppermute | solution.py:340
  48.6 1.0 collective-permute-start.8
  49.6 3.5 %collective-permute-done.5.b = bf16[192,2304]{1,0:T(8,128)(2,1)S(1)} collective-permute-done((bf16[192,2304]{1,0:T(8,128)(2,1)S(1)}, bf16[192,2304]{1,0:T(8,128)(2,1)S(1)}, u32[]{:S(2)}, u32[]{:S(2)}) %collective-permute-start.5) | collective-permute-done | bytes 884768 | tf_op jit(solution)/shard_map/ppermute | solution.py:340
  53.3 1.6 %collective-permute-start.6 = (bf16[192,2304]{1,0:T(8,128)(2,1)S(1)}, bf16[192,2304]{1,0:T(8,128)(2,1)S(1)}, u32[]{:S(2)}, u32[]{:S(2)}) collective-permute-start(bf16[192,2304]{1,0:T(8,128)(2,1)S(1)} %pair_sum.2), channel_id=1, source_target_pairs={{0,8},{8,0},{16,24},{24,16},{1,9},{9,1},{17,25},{25,17},{2,10},{10... | collective-permute-start | bytes 2654216 | tf_op jit(solution)/shard_map/ppermute | solution.py:340
  54.8 18.0 %collective-permute-done.6.s2 = bf16[192,2304]{1,0:T(8,128)(2,1)S(1)} collective-permute-done((bf16[192,2304]{1,0:T(8,128)(2,1)S(1)}, bf16[192,2304]{1,0:T(8,128)(2,1)S(1)}, u32[]{:S(2)}, u32[]{:S(2)}) %collective-permute-start.6) | collective-permute-done | bytes 884768 | tf_op jit(solution)/shard_map/ppermute | solution.py:340
  72.8 0.3 pair_sum.3
  73.1 1.6 %collective-permute-start.12 = (bf16[768,768]{1,0:T(8,128)(2,1)S(1)}, bf16[768,768]{1,0:T(8,128)(2,1)S(1)}, u32[]{:S(2)}, u32[]{:S(2)}) collective-permute-start(bf16[768,768]{1,0:T(8,128)(2,1)S(1)} %pair_sum.3), channel_id=1, source_target_pairs={{0,8},{8,0},{16,24},{24,16},{1,9},{9,1},{17,25},{25,17},{2,10},{10... | collective-permute-start | bytes 3538952 | tf_op jit(solution)/shard_map/ppermute | solution.py:340
  74.6 1.7 %collective-permute-start.13 = (bf16[192,2304]{1,0:T(8,128)(2,1)S(1)}, bf16[192,2304]{1,0:T(8,128)(2,1)S(1)}, u32[]{:S(2)}, u32[]{:S(2)}) collective-permute-start(bf16[192,2304]{1,0:T(8,128)(2,1)S(1)} %collective-permute-done.6.s2), channel_id=1, source_target_pairs={{0,16},{8,24},{16,0},{24,8},{1,17},{9,25},{17,1},{25,9},{2,18},{10... | collective-permute-start | bytes 2654216 | tf_op jit(solution)/shard_map/ppermute | solution.py:340
  76.4 12.4 %collective-permute-done.9.f0 = bf16[576,2304]{1,0:T(8,128)(2,1)S(1)} collective-permute-done((bf16[576,2304]{1,0:T(8,128)(2,1)}, bf16[576,2304]{1,0:T(8,128)(2,1)S(1)}, u32[]{:S(2)}, u32[]{:S(2)}) %collective-permute-start.9) | collective-permute-done | bytes 2654240 | tf_op jit(solution)/shard_map/ppermute | solution.py:340
  88.8 2.2 %collective-permute-done.8.a2 = bf16[384,2304]{1,0:T(8,128)(2,1)S(1)} collective-permute-done((bf16[384,2304]{1,0:T(8,128)(2,1)S(1)}, bf16[384,2304]{1,0:T(8,128)(2,1)S(1)}, u32[]{:S(2)}, u32[]{:S(2)}) %collective-permute-start.8) | collective-permute-done | bytes 1769504 | tf_op jit(solution)/shard_map/ppermute | solution.py:340
  91.0 0.5 collective-permute-start.11
  91.5 4.0 %partial_qkv.1.acc = f32[768,2304]{1,0:T(8,128)S(1)} custom-call(bf16[768,832]{1,0:T(8,128)(2,1)S(1)} %get-tuple-element.29.normed, bf16[768,2304]{1,0:T(8,128)(2,1)S(1)} %bitcast.21, bf16[384,2304]{1,0:T(8,128)(2,1)S(1)} %collective-permute-done.2.n0, bf16[384,2304]{1,0:T(8,128)(2,1)S(1)} %collective-permute-done.3.n1, ...), custom_call_target="tpu_custom_call" | custom-call | flops 2944401408 | bytes 21233664 | tf_op jit(solution)/shard_map/partial_qkv/pallas_call | solution.py:24
  95.5 2.4 %early_rows.1 = (bf16[768,2304]{1,0:T(8,128)(2,1)}, f32[8,128]{1,0:T(8,128)}) custom-call(s32[1]{0:T(128)} %bitcast.side, f32[768,2304]{1,0:T(8,128)S(1)} %partial_qkv.1.acc, bf16[576,2304]{1,0:T(8,128)(2,1)S(1)} %collective-permute-done.9.f0, bf16[384,2304]{1,0:T(8,128)(2,1)S(1)} %collective-permute-done.8.a2, bf16[192,2304]{1,0:T(8,128)(2,1)S(1)} %collective-permute-done.6.s2), custom_call_target="tpu_custom_call" | custom-call | flops 5308416 | bytes 13271040 | tf_op jit(solution)/shard_map/early_rows/pallas_call | solution.py:24
  97.9 1.6 %partial_proj.1.acc = f32[768,768]{1,0:T(8,128)S(1)} custom-call(bf16[832,768]{1,0:T(8,128)(2,1)S(1)} %bitcast.28, bf16[768,768]{1,0:T(8,128)(2,1)S(1)} %bitcast.26, bf16[384,768]{1,0:T(8,128)(2,1)S(1)} %collective-permute-done.10.np0, bf16[384,768]{1,0:T(8,128)(2,1)S(1)} %collective-permute-done.11.np1, bf16[768,768]{1,0:T(8,128)(2,1)S(1)} %collective-permute-done.fp, ...), custom_call_target="tpu_custom_call" | custom-call | flops 981467136 | bytes 7077888 | tf_op jit(solution)/shard_map/partial_proj/pallas_call | solution.py:24
  99.5 1.3 %final_proj.1 = bf16[768,768]{1,0:T(8,128)(2,1)} custom-call(f32[768,768]{1,0:T(8,128)S(1)} %partial_proj.1.acc, bf16[768,768]{1,0:T(8,128)(2,1)S(1)} %collective-permute-done.12.s1), custom_call_target="tpu_custom_call" | custom-call | flops 1179648 | bytes 4718592 | tf_op jit(solution)/shard_map/final_proj/pallas_call | solution.py:24
  100.8 6.9 %collective-permute-done.13.other = bf16[192,2304]{1,0:T(8,128)(2,1)S(1)} collective-permute-done((bf16[192,2304]{1,0:T(8,128)(2,1)S(1)}, bf16[192,2304]{1,0:T(8,128)(2,1)S(1)}, u32[]{:S(2)}, u32[]{:S(2)}) %collective-permute-start.13) | collective-permute-done | bytes 884768 | tf_op jit(solution)/shard_map/ppermute | solution.py:340
  107.8 1.0 last_rows.1
  (23 shorter events, 1.1 us)
Async XLA Ops:
  0.6 31.3 %collective-permute-start = (bf16[768,768]{1,0:T(8,128)(2,1)}, bf16[768,768]{1,0:T(8,128)(2,1)S(1)}, u32[]{:S(2)}, u32[]{:S(2)}) collective-permute-start(bf16[768,768]{1,0:T(8,128)(2,1)} %bitcast.22), channel_id=1, source_target_pairs={{0,7},{1,2},{2,1},{3,4},{4,3},{5,6},{6,5},{7,0},{8,15},{9,10},{10,... | collective-permute-start | bytes 3538952 | tf_op jit(solution)/shard_map/ppermute | solution.py:340
  5.2 29.1 %collective-permute-start.1 = (bf16[768,768]{1,0:T(8,128)(2,1)}, bf16[768,768]{1,0:T(8,128)(2,1)S(1)}, u32[]{:S(2)}, u32[]{:S(2)}) collective-permute-start(bf16[768,768]{1,0:T(8,128)(2,1)} %bitcast.23), channel_id=1, source_target_pairs={{0,16},{8,24},{16,0},{24,8},{1,17},{9,25},{17,1},{25,9},{2,18},{10... | collective-permute-start | bytes 3538952 | tf_op jit(solution)/shard_map/ppermute | solution.py:340
  6.7 2.5 %copy-start = (bf16[1,1,768,2304]{3,2,1,0:T(8,128)(2,1)S(1)}, bf16[1,1,768,2304]{3,2,1,0:T(8,128)(2,1)}, u32[]{:S(2)}) copy-start(bf16[1,1,768,2304]{3,2,1,0:T(8,128)(2,1)} %param.6) | copy-start | bytes 10616836
  8.4 44.7 %collective-permute-start.5 = (bf16[192,2304]{1,0:T(8,128)(2,1)S(1)}, bf16[192,2304]{1,0:T(8,128)(2,1)S(1)}, u32[]{:S(2)}, u32[]{:S(2)}) collective-permute-start(bf16[192,2304]{1,0:T(8,128)(2,1)S(1)} %get-tuple-element.47), channel_id=1, source_target_pairs={{0,16},{8,24},{16,0},{24,8},{1,17},{9,25},{17,1},{25,9},{2,18},{10... | collective-permute-start | bytes 2654216 | tf_op jit(solution)/shard_map/ppermute | solution.py:340
  9.6 38.9 %collective-permute-start.4 = (bf16[384,2304]{1,0:T(8,128)(2,1)S(1)}, bf16[384,2304]{1,0:T(8,128)(2,1)S(1)}, u32[]{:S(2)}, u32[]{:S(2)}) collective-permute-start(bf16[384,2304]{1,0:T(8,128)(2,1)S(1)} %first_rows.1), channel_id=1, source_target_pairs={{0,8},{8,0},{16,24},{24,16},{1,9},{9,1},{17,25},{25,17},{2,10},{10... | collective-permute-start | bytes 5308424 | tf_op jit(solution)/shard_map/ppermute | solution.py:340
  11.2 1.7 %copy-start.2 = (bf16[1,1,4,197,768]{4,2,3,1,0:T(4,128)(2,1)S(1)}, bf16[1,1,4,197,768]{4,2,3,1,0:T(4,128)(2,1)}, u32[]{:S(2)}) copy-start(bf16[1,1,4,197,768]{4,2,3,1,0:T(4,128)(2,1)} %param.5) | copy-start | bytes 3631108
  12.9 1.3 %copy-start.3 = (bf16[1,1,4,197,768]{4,2,3,1,0:T(4,128)(2,1)S(1)}, bf16[1,1,4,197,768]{4,2,3,1,0:T(4,128)(2,1)}, u32[]{:S(2)}) copy-start(bf16[1,1,4,197,768]{4,2,3,1,0:T(4,128)(2,1)} %param.4) | copy-start | bytes 3631108
  12.9 75.9 %collective-permute-start.9 = (bf16[576,2304]{1,0:T(8,128)(2,1)}, bf16[576,2304]{1,0:T(8,128)(2,1)S(1)}, u32[]{:S(2)}, u32[]{:S(2)}) collective-permute-start(bf16[576,2304]{1,0:T(8,128)(2,1)} %pad_maximum_fusion), channel_id=1, source_target_pairs={{0,7},{1,2},{2,1},{3,4},{4,3},{5,6},{6,5},{7,0},{8,15},{9,10},{10,... | collective-permute-start | bytes 7962632 | tf_op jit(solution)/shard_map/ppermute | solution.py:340
  14.5 1.3 %copy-start.1 = (bf16[1,1,768,768]{3,2,1,0:T(8,128)(2,1)S(1)}, bf16[1,1,768,768]{3,2,1,0:T(8,128)(2,1)}, u32[]{:S(2)}) copy-start(bf16[1,1,768,768]{3,2,1,0:T(8,128)(2,1)} %param.7) | copy-start | bytes 3538948
  34.3 38.5 %collective-permute-start.2 = (bf16[384,2304]{1,0:T(8,128)(2,1)S(1)}, bf16[384,2304]{1,0:T(8,128)(2,1)S(1)}, u32[]{:S(2)}, u32[]{:S(2)}) collective-permute-start(bf16[384,2304]{1,0:T(8,128)(2,1)S(1)} %first_rows.1), channel_id=1, source_target_pairs={{0,1},{1,0},{2,3},{3,2},{4,5},{5,4},{6,7},{7,6},{8,9},{9,8},{10,11... | collective-permute-start | bytes 5308424 | tf_op jit(solution)/shard_map/ppermute | solution.py:340
  34.3 38.5 %collective-permute-start.3 = (bf16[384,2304]{1,0:T(8,128)(2,1)S(1)}, bf16[384,2304]{1,0:T(8,128)(2,1)S(1)}, u32[]{:S(2)}, u32[]{:S(2)}) collective-permute-start(bf16[384,2304]{1,0:T(8,128)(2,1)S(1)} %slice_bitcast_fusion), channel_id=1, source_target_pairs={{0,1},{1,0},{2,3},{3,2},{4,5},{5,4},{6,7},{7,6},{8,9},{9,8},{10,11... | collective-permute-start | bytes 5308424 | tf_op jit(solution)/shard_map/ppermute | solution.py:340
  48.6 42.4 %collective-permute-start.8 = (bf16[384,2304]{1,0:T(8,128)(2,1)S(1)}, bf16[384,2304]{1,0:T(8,128)(2,1)S(1)}, u32[]{:S(2)}, u32[]{:S(2)}) collective-permute-start(bf16[384,2304]{1,0:T(8,128)(2,1)S(1)} %collective-permute-done.4.a1), channel_id=1, source_target_pairs={{0,16},{8,24},{16,0},{24,8},{1,17},{9,25},{17,1},{25,9},{2,18},{10... | collective-permute-start | bytes 5308424 | tf_op jit(solution)/shard_map/ppermute | solution.py:340
  53.3 19.5 %collective-permute-start.6 = (bf16[192,2304]{1,0:T(8,128)(2,1)S(1)}, bf16[192,2304]{1,0:T(8,128)(2,1)S(1)}, u32[]{:S(2)}, u32[]{:S(2)}) collective-permute-start(bf16[192,2304]{1,0:T(8,128)(2,1)S(1)} %pair_sum.2), channel_id=1, source_target_pairs={{0,8},{8,0},{16,24},{24,16},{1,9},{9,1},{17,25},{25,17},{2,10},{10... | collective-permute-start | bytes 2654216 | tf_op jit(solution)/shard_map/ppermute | solution.py:340
  73.1 26.4 %collective-permute-start.12 = (bf16[768,768]{1,0:T(8,128)(2,1)S(1)}, bf16[768,768]{1,0:T(8,128)(2,1)S(1)}, u32[]{:S(2)}, u32[]{:S(2)}) collective-permute-start(bf16[768,768]{1,0:T(8,128)(2,1)S(1)} %pair_sum.3), channel_id=1, source_target_pairs={{0,8},{8,0},{16,24},{24,16},{1,9},{9,1},{17,25},{25,17},{2,10},{10... | collective-permute-start | bytes 3538952 | tf_op jit(solution)/shard_map/ppermute | solution.py:340
  74.6 33.1 %collective-permute-start.13 = (bf16[192,2304]{1,0:T(8,128)(2,1)S(1)}, bf16[192,2304]{1,0:T(8,128)(2,1)S(1)}, u32[]{:S(2)}, u32[]{:S(2)}) collective-permute-start(bf16[192,2304]{1,0:T(8,128)(2,1)S(1)} %collective-permute-done.6.s2), channel_id=1, source_target_pairs={{0,16},{8,24},{16,0},{24,8},{1,17},{9,25},{17,1},{25,9},{2,18},{10... | collective-permute-start | bytes 2654216 | tf_op jit(solution)/shard_map/ppermute | solution.py:340
  76.4 31.4 %collective-permute-start.7 = (bf16[192,2304]{1,0:T(8,128)(2,1)S(1)}, bf16[192,2304]{1,0:T(8,128)(2,1)S(1)}, u32[]{:S(2)}, u32[]{:S(2)}) collective-permute-start(bf16[192,2304]{1,0:T(8,128)(2,1)S(1)} %get-tuple-element.47), channel_id=1, source_target_pairs={{0,7},{1,2},{2,1},{3,4},{4,3},{5,6},{6,5},{7,0},{8,15},{9,10},{10,... | collective-permute-start | bytes 2654216 | tf_op jit(solution)/shard_map/ppermute | solution.py:340
  91.0 6.9 %collective-permute-start.10 = (bf16[384,768]{1,0:T(8,128)(2,1)S(1)}, bf16[384,768]{1,0:T(8,128)(2,1)S(1)}, u32[]{:S(2)}, u32[]{:S(2)}) collective-permute-start(bf16[384,768]{1,0:T(8,128)(2,1)S(1)} %get-tuple-element.48), channel_id=1, source_target_pairs={{0,1},{1,0},{2,3},{3,2},{4,5},{5,4},{6,7},{7,6},{8,9},{9,8},{10,11... | collective-permute-start | bytes 1769480 | tf_op jit(solution)/shard_map/ppermute | solution.py:340
  91.0 6.9 %collective-permute-start.11 = (bf16[384,768]{1,0:T(8,128)(2,1)S(1)}, bf16[384,768]{1,0:T(8,128)(2,1)S(1)}, u32[]{:S(2)}, u32[]{:S(2)}) collective-permute-start(bf16[384,768]{1,0:T(8,128)(2,1)S(1)} %get-tuple-element.49), channel_id=1, source_target_pairs={{0,1},{1,0},{2,3},{3,2},{4,5},{5,4},{6,7},{7,6},{8,9},{9,8},{10,11... | collective-permute-start | bytes 1769480 | tf_op jit(solution)/shard_map/ppermute | solution.py:340
